TPU v7x, 128 devices: a whole 4x4x4 slice. The times are simulated.
128 devices in a mesh: grp: 2 (over y_lo), dev: 64 (over y_hi, z, x, core).
Axes of the slice: x: 4, y: 4 (y_hi: 2, y_lo: 2; y = y_hi * 2 + y_lo), z: 4, core: 2. Of those that a mesh axis runs over, the one named last changes fastest.
Arguments:
- queries: bfloat16 [256, 128, 576], P(('grp', 'dev')), may hold values from -240 to 240
- cache: bfloat16 [256, 2048, 576], P(('grp', 'dev')), may hold values from -6 to 6
- lengths: int32 [256], P(('grp', 'dev')), may hold values from 1 to 2048, 131072 in all
- w_uv: bfloat16 [128, 512, 128], P(('grp', 'dev')), may hold values from -3 to 3
- w_out: bfloat16 [16384, 7168], P(('grp', 'dev')), may hold values from -0.046875 to 0.046875
- residual: bfloat16 [256, 7168], P(('grp', 'dev')), may hold values from -3 to 3
- gain: float32 [7168], replicated, may hold values from 0.5 to 1.5
- ids: int32 [256, 8], P(('grp', 'dev')), may hold values from 0 to 31, all different within a row; in each aligned block of 2 rows (0 to 1, 2 to 3, ...) at most 2 rows name the same one
- gates: float32 [256, 8], P(('grp', 'dev')), may hold values from 0.05 to 0.5
- w_gate: bfloat16 [128, 7168, 256], P(('grp', 'dev')), may hold values from -0.0625 to 0.0625
- w_up: bfloat16 [128, 7168, 256], P(('grp', 'dev')), may hold values from -0.0625 to 0.0625
- w_down: bfloat16 [128, 256, 7168], P(('grp', 'dev')), may hold values from -0.1875 to 0.1875
Outputs:
- layer_out: bfloat16 [256, 7168], P(('grp', 'dev'))
Inputs may be any that keep to these rules, and one draw needn't show every extreme that they name: `ids`: among the rows of one device no expert is named by more than 2 rows, a bound that some block reaches. `lengths`: some request has all 2048 slots live.
All inputs are finite; a program needn't handle non-finite values. No bound on the sum of `lengths` on one device may be relied on, other than what follows from the above.
Results may differ from a plain program's by a relative error of at most 0.006.
Values may be sent and summed in bfloat16 or wider, within the bound.
No kernel may reach another device: no remote copies, remote signals or barrier semaphores. Data moves between devices by JAX's collectives and lax.ppermute only.
A program may use at most 128 MiB of HBM per device.

v0:
```python
import jax
import jax.numpy as jnp
from jax import lax
from jax.sharding import PartitionSpec as P

LATENT = 512
MOE_FF = 1024


softmax_scale = 192.0 ** (-0.5)


def attend_rows(query, cache, lengths):
    score = (
        jnp.einsum("rhc,rlc->rhl", query, cache, preferred_element_type=jnp.float32) * softmax_scale
    )
    places = jnp.arange(cache.shape[1], dtype=jnp.int32)
    live = places[None, None, :] < lengths[:, None, None]
    score = jnp.where(live, score, -jnp.inf)
    peak = jnp.max(score, axis=2, keepdims=True)
    weight = jnp.where(live, jnp.exp(score - peak), 0.0)
    total = jnp.sum(weight, axis=2, keepdims=True)
    summed = jnp.einsum(
        "rhl,rlc->rhc",
        weight.astype(jnp.bfloat16),
        cache[:, :, :LATENT],
        preferred_element_type=jnp.float32,
    )
    return (summed / total).astype(jnp.bfloat16)


def shards(queries, cache, lengths, w_uv, w_out, residual, gain, ids, gates, w_gate, w_up, w_down):
    devices = lax.axis_size(("grp", "dev"))
    rows_dev = residual.shape[0]
    top = ids.shape[1]
    slices = MOE_FF // w_gate.shape[2]
    experts = devices // slices
    cap = max(2, min(rows_dev, 3 * rows_dev * top // (2 * experts)))
    width = residual.shape[1]
    latents = attend_rows(queries, cache, lengths)
    gathered = lax.all_to_all(latents, ("grp", "dev"), split_axis=1, concat_axis=0, tiled=True)
    values = jnp.einsum("rhc,hcv->rhv", gathered, w_uv, preferred_element_type=jnp.float32).astype(
        jnp.bfloat16
    )
    values = values.reshape(values.shape[0], values.shape[1] * values.shape[2])
    attn = lax.psum_scatter(
        jnp.dot(values, w_out, preferred_element_type=jnp.float32),
        ("grp", "dev"),
        scatter_dimension=0,
        tiled=True,
    )
    mixed = residual.astype(jnp.float32) + attn
    normed = (
        mixed * lax.rsqrt(jnp.mean(mixed * mixed, axis=-1, keepdims=True) + 1e-06) * gain
    ).astype(jnp.bfloat16)
    pair_ids = ids.reshape(-1)
    hits = (pair_ids[:, None] == jnp.arange(experts, dtype=jnp.int32)[None, :]).astype(jnp.int32)
    slot = jnp.sum((jnp.cumsum(hits, axis=0) - 1) * hits, axis=1)
    target = pair_ids * cap + slot
    place = target[:, None] == jnp.arange(experts * cap, dtype=jnp.int32)[None, :]
    every_rows = lax.all_gather(normed, ("grp", "dev"), axis=0, tiled=True)
    every_ids = lax.all_gather(ids, ("grp", "dev"), axis=0, tiled=True)
    mine = lax.axis_index(("grp", "dev")) // slices
    mine_hit = (every_ids.reshape(devices, rows_dev * top) == mine).astype(jnp.int32)
    mine_slot = jnp.cumsum(mine_hit, axis=1) - 1
    chosen = (mine_hit[:, None, :] == 1) & (
        mine_slot[:, None, :] == jnp.arange(cap, dtype=jnp.int32)[None, :, None]
    )
    chosen = chosen.reshape(devices, cap, rows_dev, top).any(axis=3).astype(jnp.bfloat16)
    arrived = jnp.einsum(
        "ncr,nrd->ncd",
        chosen,
        every_rows.reshape(devices, rows_dev, width),
        preferred_element_type=jnp.float32,
    ).astype(jnp.bfloat16)
    flat_rows = arrived.reshape(-1, width)
    gate_val = jnp.dot(flat_rows, w_gate[0], preferred_element_type=jnp.float32)
    up_val = jnp.dot(flat_rows, w_up[0], preferred_element_type=jnp.float32)
    hidden = (jax.nn.silu(gate_val) * up_val).astype(jnp.bfloat16)
    result = jnp.dot(hidden, w_down[0], preferred_element_type=jnp.float32)
    produced = result.reshape(arrived.shape[0], arrived.shape[1], width)
    returned = lax.all_to_all(
        produced.astype(jnp.bfloat16), ("grp", "dev"), split_axis=0, concat_axis=0, tiled=True
    ).astype(produced.dtype)
    summed = jnp.sum(returned.reshape(experts, slices, cap, width), axis=1).reshape(
        experts * cap, width
    )
    combine = jnp.sum(
        place.astype(jnp.float32).reshape(rows_dev, top, experts * cap) * gates[:, :, None], axis=1
    )
    moe = jnp.dot(
        combine, summed, precision=lax.Precision.HIGHEST, preferred_element_type=jnp.float32
    )
    return (mixed + moe).astype(jnp.bfloat16)


def solution(mesh):
    in_specs = (
        P(("grp", "dev"), None, None),
        P(("grp", "dev"), None, None),
        P(("grp", "dev")),
        P(("grp", "dev"), None, None),
        P(("grp", "dev"), None),
        P(("grp", "dev"), None),
        P(),
        P(("grp", "dev"), None),
        P(("grp", "dev"), None),
        P(("grp", "dev"), None, None),
        P(("grp", "dev"), None, None),
        P(("grp", "dev"), None, None),
    )
    out_specs = P(("grp", "dev"), None)
    return jax.shard_map(shards, mesh=mesh, in_specs=in_specs, out_specs=out_specs, check_vma=False)
```

profile of v0, /device:TPU:1, one launch (start us, length us, event | category | flops | bytes accessed | tf_op | source)
XLA Modules:
  0.0 504.0 jit_solution(9159262592829590259)
XLA Ops:
  6.5 0.9 iota_compare_fusion.1
  7.4 4.2 fusion.38
  11.6 3.8 fusion.26
  15.3 0.3 copy.43
  15.6 22.5 %all_to_all.20 = bf16[2,128,512]{2,0,1:T(2,128)(2,1)S(1)} all-to-all(bf16[2,128,512]{2,0,1:T(2,128)(2,1)S(1)} %copy.43), channel_id=1, replica_groups=mesh['grp'=2,'dev'=64] {'grp','dev'}, dimensions={1} | all-to-all | bytes 524288 | tf_op jit(solution)/shard_map/all_to_all | solution.py:41
  38.1 0.1 reshape.118
  38.2 4.3 fusion.19
  42.6 156.1 %all-reduce.3.cloned.1.call-done = f32[256,7168]{1,0:T(8,128)} async-done(((f32[256,7168]{1,0:T(8,128)}), f32[256,7168]{1,0:T(8,128)}) %all-reduce.3.cloned.1.call-update) | async-done | bytes 7340048
  198.7 1.1 multiply_reduce_fusion
  199.8 1.6 fusion.34
  201.5 175.0 %all-gather = s32[128,2,8]{2,1,0:T(2,128)S(1)} all-gather(s32[1,2,8]{2,1,0:T(2,128)S(1)} %bitcast.48), channel_id=1, replica_groups=mesh['grp'=2,'dev'=64] {'grp','dev'}, dimensions={0}, use_global_device_ids=true | all-gather | bytes 8256 | tf_op jit(solution)/shard_map/all_gather | solution.py:62
  376.5 0.1 copy.44
  376.6 0.2 copy.46
  376.8 20.4 %all-gather.4.cloned.1.call-done = bf16[128,2,7168]{2,1,0:T(2,128)(2,1)} async-done(((bf16[1,2,7168]{2,1,0:T(2,128)(2,1)}), bf16[128,2,7168]{2,1,0:T(2,128)(2,1)}) %all-gather.4.cloned.1.call-update) | async-done | bytes 3670032 | tf_op jit(solution)/shard_map/all_gather | solution.py:61
  397.2 6.9 %convolution_convert_fusion.1 = bf16[128,2,7168]{2,1,0:T(2,128)(2,1)} fusion(pred[128,2,2]{2,1,0:T(4,128)(4,1)S(1)} %copy.46, bf16[128,2,7168]{2,1,0:T(2,128)(2,1)} %all-gather.4.cloned.1.call-done), kind=kOutput, calls=%fused_computation.2 | convolution fusion | flops 9175040 | bytes 7340544 | tf_op jit(solution)/shard_map/ncr,nrd->ncd/dot_general | solution.py:70
  404.1 8.4 %reshape.121 = bf16[256,7168]{1,0:T(8,128)(2,1)} reshape(bf16[128,2,7168]{2,1,0:T(2,128)(2,1)} %convolution_convert_fusion.1) | data formatting | bytes 7340032 | tf_op jit(solution)/shard_map/reshape | solution.py:76
  412.5 4.4 fusion.7
  416.9 0.9 copy-done.7
  417.8 1.1 fusion.16
  418.9 0.1 dot_general.36
  419.0 3.2 convolution_convert_fusion
  422.2 5.7 %copy.48 = bf16[128,2,7168]{2,1,0:T(2,128)(2,1)} copy(bf16[128,2,7168]{2,0,1:T(8,128)(2,1)S(1)} %convolution_convert_fusion) | data formatting | bytes 7340032 | tf_op jit(solution)/shard_map/convert_element_type | solution.py:83
  427.9 7.5 %all-to-all-start.1 = ((bf16[128,2,7168]{2,1,0:T(2,128)(2,1)}), bf16[128,2,7168]{2,1,0:T(2,128)(2,1)}, u32[]{:S(2)}, u32[]{:S(2)}) async-start(bf16[128,2,7168]{2,1,0:T(2,128)(2,1)} %copy.48), calls=%async_computation.1 | async-start | bytes 7340032 | tf_op jit(solution)/shard_map/all_to_all | solution.py:82
  435.4 0.1 eq.74
  435.4 0.1 fusion.37
  435.6 0.2 select_reduce_fusion.1
  435.7 0.1 reduce_sum.49
  435.8 0.1 select_reduce_fusion
  435.9 46.8 %all-to-all-done.1 = bf16[128,2,7168]{2,1,0:T(2,128)(2,1)} async-done(((bf16[128,2,7168]{2,1,0:T(2,128)(2,1)}), bf16[128,2,7168]{2,1,0:T(2,128)(2,1)}, u32[]{:S(2)}, u32[]{:S(2)}) %all-to-all-start.1) | async-done | bytes 3670048 | tf_op jit(solution)/shard_map/all_to_all | solution.py:82
  482.7 7.9 %convert_reduce_fusion = f32[32,2,7168]{2,1,0:T(2,128)} fusion(bf16[128,2,7168]{2,1,0:T(2,128)(2,1)} %all-to-all-done.1), kind=kLoop, calls=%fused_computation.5 | loop fusion | flops 3211264 | bytes 5505024 | tf_op jit(solution)/shard_map/reduce_sum | solution.py:85
  490.6 3.5 reshape.124
  494.0 3.1 fusion.1
  (25 shorter events, 0.2 us)
Async XLA Ops:
  6.5 31.7 %copy-start = (bf16[128,7168]{1,0:T(8,128)(2,1)S(1)}, bf16[128,7168]{1,0:T(8,128)(2,1)}, u32[]{:S(2)}) copy-start(bf16[128,7168]{1,0:T(8,128)(2,1)} %param.16) | copy-start | bytes 5505028
  6.5 192.1 %all-reduce.3.cloned.1.call-start = ((), (), s32[]{:S(2)}) async-start(), calls=%async_computation.3 | async-start | bytes 14680064
  11.6 26.7 %copy-start.3 = (bf16[1,512,128]{2,1,0:T(8,128)(2,1)S(1)}, bf16[1,512,128]{2,1,0:T(8,128)(2,1)}, u32[]{:S(2)}) copy-start(bf16[1,512,128]{2,1,0:T(8,128)(2,1)} %param.15) | copy-start | bytes 393220
  42.5 156.2 %copy-start.2 = (bf16[2,7168]{1,0:T(2,128)(2,1)S(1)}, bf16[2,7168]{1,0:T(2,128)(2,1)}, u32[]{:S(2)}) copy-start(bf16[2,7168]{1,0:T(2,128)(2,1)} %param.17) | copy-start | bytes 86020
  42.5 157.3 %copy-start.4 = (f32[7168]{0:T(1024)S(1)}, f32[7168]{0:T(1024)}, u32[]{:S(2)}) copy-start(f32[7168]{0:T(1024)} %param.18) | copy-start | bytes 86020
  42.5 159.0 %copy-start.5 = (s32[2,8]{1,0:T(2,128)S(1)}, s32[2,8]{1,0:T(2,128)}, u32[]{:S(2)}) copy-start(s32[2,8]{1,0:T(2,128)} %param.19) | copy-start | bytes 196
  42.5 354.6 %all-gather.4.cloned.1.call-start = ((), (), s32[]{:S(2)}) async-start(), calls=%async_computation.2 | async-start | bytes 3698688 | tf_op jit(solution)/shard_map/all_gather | solution.py:61
  412.5 4.4 copy-start.1
  412.5 5.3 %copy-start.7 = (bf16[1,7168,256]{2,1,0:T(8,128)(2,1)S(1)}, bf16[1,7168,256]{2,1,0:T(8,128)(2,1)}, u32[]{:S(2)}) copy-start(bf16[1,7168,256]{2,1,0:T(8,128)(2,1)} %param.22) | copy-start | bytes 11010052
  427.9 8.0 %copy-start.6 = (f32[2,8]{1,0:T(2,128)S(1)}, f32[2,8]{1,0:T(2,128)}, u32[]{:S(2)}) copy-start(f32[2,8]{1,0:T(2,128)} %param.20) | copy-start | bytes 196
  427.9 54.8 %all-to-all-start.1 = ((bf16[128,2,7168]{2,1,0:T(2,128)(2,1)}), bf16[128,2,7168]{2,1,0:T(2,128)(2,1)}, u32[]{:S(2)}, u32[]{:S(2)}) async-start(bf16[128,2,7168]{2,1,0:T(2,128)(2,1)} %copy.48), calls=%async_computation.1 | async-start | bytes 7340032 | tf_op jit(solution)/shard_map/all_to_all | solution.py:82
Sparse Core Ops, SparseCore 0:
  42.7 155.9 all-reduce.2
  201.6 195.5 all-gather.3
where the time goes:
time: 506 us; the launch traced here: 504 us
  waiting for transfers between devices  223 us (44%)
  blocking collectives  197 us (39%)
  matrix products  30.9 us (6%)
  local copies, waits for them, and re-layouts  19.3 us (4%)
  between operations  13.5 us (3%)
  other arithmetic  12 us (2%)
  starting transfers between devices  7.53 us (1%)
    all_gather x1, blocking collectives, shards(): every_ids = lax.all_gather(ids, ('grp', 'dev'), axis=0, tiled=True)  175 us
    unnamed x3, waiting for transfers between devices  156 us
    all_to_all x1, waiting for transfers between devices, shards(): lax.all_to_all(produced.astype(jnp.bfloat16), ('grp', 'dev'), split_axis=...  46.8 us
    all_to_all x1, blocking collectives, shards(): lax.all_to_all(latents, ('grp', 'dev'), split_axis=1, concat_axis=0, tile...  22.5 us
    all_gather x1, waiting for transfers between devices, shards(): every_rows = lax.all_gather(normed, ('grp', 'dev'), axis=0, tiled=True)  20.4 us
  transfers between devices with their start and end apart: 3, of which 3 were waited for; matrix products, arithmetic and copies ran while one was open for 0% of the time, Pallas kernels for 0%

commit v1 on v0

v1 whole, which is shorter than its diff:
```python
import functools

import jax
import jax.numpy as jnp
from jax import lax
from jax.experimental import pallas as pl
from jax.experimental.pallas import tpu as pltpu
from jax.sharding import PartitionSpec as P

LATENT = 512
VHEAD = 128
TOP = 8
AXES = ("grp", "dev")
F32 = jnp.float32
BF16 = jnp.bfloat16
I32 = jnp.int32
MIB = 1 << 20
CHUNK = 1024

softmax_scale = 192.0 ** (-0.5)


def device(y, z, x, c):
    return ((y * 4 + z) * 4 + x) * 2 + c


RINGS = [[device(y, z, x, 0) for x in range(4)] for y in range(4) for z in range(4)] + [
    [device(y, z, x, 1) for z in range(4)] for y in range(4) for x in range(4)
]
PLANES = [[device(y, z, x, 0) for y in range(4) for z in range(4)] for x in range(4)] + [
    [device(y, z, x, 1) for y in range(4) for x in range(4)] for z in range(4)
]
SIBLING = [(i, i ^ 1) for i in range(128)]


def swap(a):
    return lax.ppermute(a, AXES, SIBLING)


def ahead(a, step):
    return lax.ppermute(a, AXES, [(r[i], r[(i + step) % 4]) for r in RINGS for i in range(4)])


def plane(a):
    return lax.all_to_all(a, AXES, 0, 0, axis_index_groups=PLANES, tiled=True)


def exchange(blocks):
    return [blocks[0]] + [ahead(blocks[4 - j], 4 - j) for j in range(1, 4)]


def iota(shape, axis):
    return lax.broadcasted_iota(I32, shape, axis)


def pick(index, count):
    return jnp.where(index == iota((index.shape[0], count), 1), 1.0, 0.0).astype(BF16)


def coordinates():
    me = lax.axis_index("grp") * 64 + lax.axis_index("dev")
    core, z, x = me & 1, (me >> 3) & 3, (me >> 1) & 3
    return core, me >> 2, jnp.where(core == 0, x, z), jnp.where(core == 0, z, x)


HBM = pl.BlockSpec(memory_space=pltpu.HBM)
VMEM = pl.BlockSpec(memory_space=pltpu.VMEM)


def attend_kernel(
    lens, query, kv, w_out, sent, out_other, heads, peak, total, acc, both, held, sems
):
    r, j = pl.program_id(0), pl.program_id(1)
    step = r * pl.num_programs(1) + j
    core, _, me_t, _ = coordinates()
    half = held.shape[1]
    away = pl.ds(pl.multiple_of((1 - core) * half, 128), half)
    take = pltpu.make_async_copy(w_out.at[:, away], held, sems.at[0])
    give = pltpu.make_async_copy(held, out_other, sems.at[1])

    @pl.when(step == 0)
    def _():
        take.start()

    @pl.when(step == 1)
    def _():
        take.wait()
        give.start()

    @pl.when(j == 0)
    def _():
        i = iota((128, 1), 0)
        turned = lax.dot_general(
            pick(i, 128), query[0], (((1,), (1,)), ((), ())), preferred_element_type=F32
        )
        heads[...] = turned.astype(BF16)
        peak[...] = jnp.full_like(peak, -1e30)
        total[...] = jnp.zeros_like(total)
        acc[...] = jnp.zeros_like(acc)

    @pl.when(j * CHUNK < lens[r])
    def _():
        score = jnp.dot(heads[...], kv[0], preferred_element_type=F32)
        place = j * CHUNK + iota(score.shape, 1)
        score = jnp.where(place < lens[r], score * softmax_scale, -1e30)
        before = peak[...]
        now = jnp.maximum(before, jnp.max(score, axis=1, keepdims=True))
        fade = jnp.exp(before - now)
        weight = jnp.exp(score - now)
        peak[...] = now
        total[...] = total[...] * fade + jnp.sum(weight, axis=1, keepdims=True)
        acc[...] = acc[...] * fade + lax.dot_general(
            weight.astype(BF16),
            kv[0, :LATENT, :],
            (((1,), (1,)), ((), ())),
            preferred_element_type=F32,
        )

    @pl.when(j == pl.num_programs(1) - 1)
    def _():
        both[pl.ds(pl.multiple_of(r * 128, 128), 128), :] = (acc[...] / total[...]).astype(BF16)

    @pl.when(step == 2 * pl.num_programs(1) - 1)
    def _():
        i = iota((256, 1), 0)
        y, b, t = i >> 6, (i >> 4) & 3, (me_t + (i >> 2)) & 3
        z = jnp.where(core == 0, b, t)
        x = jnp.where(core == 0, t, b)
        head = device(y, z, x, ((i >> 1) & 1) ^ core)
        rows = jnp.dot(pick((i & 1) * 128 + head, 256), both[...], preferred_element_type=F32)
        sent[...] = rows.astype(BF16).reshape(sent.shape)
        give.wait()


def attend(lengths, queries, cache, w_out):
    _, size, heads = queries.shape
    half = w_out.shape[1] // 2
    chunks = cache.shape[2] // CHUNK

    def live(r, j, lens):
        return (r, 0, jnp.minimum(j, (lens[r] - 1) // CHUNK))

    return pl.pallas_call(
        attend_kernel,
        grid_spec=pltpu.PrefetchScalarGridSpec(
            num_scalar_prefetch=1,
            grid=(2, chunks),
            in_specs=[
                pl.BlockSpec((1, size, heads), lambda r, j, lens: (r, 0, 0)),
                pl.BlockSpec((1, size, CHUNK), live),
                HBM,
            ],
            out_specs=[
                pl.BlockSpec((16, 16, LATENT), lambda r, j, lens: (0, 0, 0)),
                HBM,
            ],
            scratch_shapes=[
                pltpu.VMEM((heads, size), BF16),
                pltpu.VMEM((heads, 1), F32),
                pltpu.VMEM((heads, 1), F32),
                pltpu.VMEM((heads, LATENT), F32),
                pltpu.VMEM((2 * heads, LATENT), BF16),
                pltpu.VMEM((VHEAD, half), BF16),
                pltpu.SemaphoreType.DMA((2,)),
            ],
        ),
        out_shape=[
            pltpu.VMEM((16, 16, LATENT), BF16),
            jax.ShapeDtypeStruct((VHEAD, half), BF16),
        ],
        compiler_params=pltpu.CompilerParams(vmem_limit_bytes=56 * MIB),
        name="attend",
    )(lengths, queries, cache, w_out)


def load_kernel(places, *refs):
    arrays, (out, sems) = refs[: len(places)], refs[len(places) :]
    core = coordinates()[0]
    copies = []
    for n, (array, (axis, rows, columns)) in enumerate(zip(arrays, places)):
        if axis == 0:
            start = pl.multiple_of(core * out.shape[0], 128)
            array = array.at[pl.ds(start, out.shape[0]), :]
        if axis == 1:
            start = pl.multiple_of(core * out.shape[1], 128)
            array = array.at[:, pl.ds(start, out.shape[1])]
        copies.append(pltpu.make_async_copy(array, out.at[rows, columns], sems.at[n]))
    for copy in copies:
        copy.start()
    for copy in copies:
        copy.wait()


def load(arrays, places, shape, name, limit):
    size = 2 * shape[0] * shape[1]
    return pl.pallas_call(
        functools.partial(load_kernel, places),
        in_specs=[HBM] * len(arrays),
        out_specs=VMEM,
        out_shape=pltpu.VMEM(shape, BF16),
        scratch_shapes=[pltpu.SemaphoreType.DMA((len(arrays),))],
        compiler_params=pltpu.CompilerParams(vmem_limit_bytes=limit * MIB),
        cost_estimate=pl.CostEstimate(flops=0, bytes_accessed=2 * size, transcendentals=0),
        name=name,
    )(*arrays)


def pack_kernel(gate, up, down, after, gate_out, up_out, down_out, mark, *scratch):
    held, sems = scratch[:3], scratch[3]
    core = coordinates()[0]
    half = down_out.shape[1]
    away = pl.ds(pl.multiple_of((1 - core) * half, 128), half)
    sources = (gate.at[away, :], up.at[away, :], down.at[:, away])
    outs = (gate_out, up_out, down_out)
    takes = [pltpu.make_async_copy(a, b, sems.at[n]) for n, (a, b) in enumerate(zip(sources, held))]
    gives = [pltpu.make_async_copy(a, b, sems.at[3 + n]) for n, (a, b) in enumerate(zip(held, outs))]
    for take in takes:
        take.start()
    mark[...] = jnp.zeros_like(mark)
    for take, give in zip(takes, gives):
        take.wait()
        give.start()
    for give in gives:
        give.wait()


def pack(gate, up, down, after):
    half = down.shape[1] // 2
    shapes = [(half, 256), (half, 256), (256, half)]
    return pl.pallas_call(
        pack_kernel,
        in_specs=[HBM] * 3 + [pl.BlockSpec(memory_space=pl.ANY)],
        out_specs=[HBM] * 3 + [VMEM],
        out_shape=[jax.ShapeDtypeStruct(shape, BF16) for shape in shapes]
        + [pltpu.VMEM((8, 128), F32)],
        scratch_shapes=[pltpu.VMEM(shape, BF16) for shape in shapes]
        + [pltpu.SemaphoreType.DMA((6,))],
        compiler_params=pltpu.CompilerParams(vmem_limit_bytes=56 * MIB),
        cost_estimate=pl.CostEstimate(flops=0, bytes_accessed=12 * MIB, transcendentals=0),
        name="pack",
    )(gate, up, down, after)


def call(kernel, args, outs, name, flops, scratch=()):
    return pl.pallas_call(
        kernel,
        in_specs=[VMEM] * len(args),
        out_specs=[VMEM] * len(outs),
        out_shape=[jax.ShapeDtypeStruct(*out) for out in outs],
        scratch_shapes=list(scratch),
        compiler_params=pltpu.CompilerParams(vmem_limit_bytes=24 * MIB),
        cost_estimate=pl.CostEstimate(flops=flops, bytes_accessed=1 << 20, transcendentals=0),
        name=name,
    )(*args)


def turn_kernel(got, mark, o0, o1, o2, o3):
    rows = got[...].reshape(256, got.shape[2])
    i = iota((256, 1), 0)
    index = (i & 15) * 16 + (i >> 6) * 4 + ((i >> 4) & 3)
    rows = jnp.dot(pick(index, 256), rows, preferred_element_type=F32).astype(BF16)
    for d, out in enumerate((o0, o1, o2, o3)):
        out[...] = rows[d * 64 : d * 64 + 64]


def values_kernel(p0, p1, p2, p3, uv_own, uv_other, out):
    for head, uv in enumerate((uv_own, uv_other)):
        rows = jnp.concatenate(
            [p[head * 32 : head * 32 + 32, :] for p in (p0, p1, p2, p3)], axis=0
        )
        val = jnp.dot(rows, uv[...], preferred_element_type=F32)
        out[:, head * VHEAD : head * VHEAD + VHEAD] = val.astype(BF16)


PARTS = ((0, 64), (64, 96), (96, 128), (128, 160), (160, 192), (192, 224), (224, 256))


LATE = PARTS[:3] + PARTS[5:] + PARTS[3:5]


def put_parts(full, outs, columns, parts):
    for ref, (lo, hi) in zip(outs, parts):
        ref[:, columns] = full[lo:hi].astype(BF16)


def project_kernel(mine, theirs, w, *refs):
    outs, val = refs[:-1], refs[-1]
    _, _, me_t, me_p = coordinates()
    i = iota((128, 1), 0)
    t, b = ((i >> 5) + me_t) & 3, i & 3
    index = ((b - me_p) & 3) * 32 + (i & 0x1C) + t
    sib = jnp.dot(pick(index, 128), theirs[...], preferred_element_type=F32).astype(BF16)
    for d in range(4):
        for s, rows in enumerate((mine[...], sib)):
            at = d * 64 + s * 32
            rows = rows[d * 32 : d * 32 + 32]
            val[at : at + 32, s * VHEAD : s * VHEAD + VHEAD] = rows[:, :VHEAD]
            val[at : at + 32, (1 - s) * VHEAD : (2 - s) * VHEAD] = rows[:, VHEAD:]
    quarter = w.shape[1] // 4
    for q in range(4):
        columns = slice(q * quarter, (q + 1) * quarter)
        full = jnp.dot(val[...], w[:, columns], preferred_element_type=F32)
        put_parts(full, outs, columns, PARTS)


def product_outs(half):
    return [((hi - lo, half), BF16) for lo, hi in PARTS]


def gate_up_kernel(first, *refs):
    before, refs = refs[: 4 if first else 0], refs[4 if first else 0 :]
    pieces, (back, w), outs = refs[:-6], refs[-6:-4], refs[-4:]
    for done, out in zip(before, outs):
        out[:first, :] = done[...]
    count = outs[0].shape[0] - first
    part, sent, squares, weight = (out.at[pl.ds(first, count), :] for out in outs)
    expert = coordinates()[1]
    half = w.shape[0]
    quarter = half // 4
    sq = jnp.zeros((count, 1), F32)
    for q in range(4):
        columns = slice(q * quarter, (q + 1) * quarter)
        a = jnp.concatenate([p[:, columns] for p in pieces], axis=0)
        share = jnp.dot(a, w[columns, :], preferred_element_type=F32)
        if q == 0:
            part[...] = share
        else:
            part[...] += share
        plain = a.astype(F32) * back[:, columns]
        sq += jnp.sum(plain * plain, axis=1, keepdims=True)
    squares[...] = sq
    sent[:, :1024] = part[...].astype(BF16)
    hi = sq.astype(BF16).astype(F32)
    mid = (sq - hi).astype(BF16).astype(F32)
    lo = sq - hi - mid
    lane = iota((count, 128), 1)
    sent[:, 1024:] = jnp.where(
        lane == 0, hi, jnp.where(lane == 1, mid, jnp.where(lane == 2, lo, 0.0))
    ).astype(BF16)
    n = jnp.concatenate([p[:, half:] for p in pieces], axis=0).astype(F32)
    high = pltpu.roll(n, 128 - TOP, 1)
    low = pltpu.roll(n, 128 - 2 * TOP, 1)
    hit = (lane < TOP) & (n == expert.astype(F32))
    weight[...] = jnp.sum(jnp.where(hit, high + low, 0.0), axis=1, keepdims=True)


def gate_up(before, pieces, back, w):
    first = before[0].shape[0] if before else 0
    fresh = sum(p.shape[0] for p in pieces)
    count = first + fresh
    return call(
        functools.partial(gate_up_kernel, first),
        (*before, *pieces, back, w),
        [((count, 1024), F32), ((count, 1152), BF16), ((count, 1), F32), ((count, 1), F32)],
        "gate_up",
        fresh << 23,
    )


def late(d):
    return d ^ (d >> 1)


def down_kernel(part, squares, got, weight, w, *refs):
    outs, hidden = refs[:-1], refs[-1]
    _, _, me_t, me_p = coordinates()
    i = iota((256, 1), 0)
    d, s, rest = late(i >> 6), (i >> 5) & 1, i & 0x1C
    t, b = (d + me_t) & 3, i & 3
    index = late((b - me_p) & 3) * 64 + (1 - s) * 32 + rest + t
    theirs = jnp.dot(pick(index, 256), got[...], preferred_element_type=F32)
    tail = theirs[:, 1024:]
    lane = iota(tail.shape, 1)
    sq = squares[...] + jnp.sum(jnp.where(lane < 3, tail, 0.0), axis=1, keepdims=True)
    scale = lax.rsqrt(sq / 7168.0 + 1e-06)
    for block in range(2):
        at, back = block * 512, 512 - block * 512
        gate = (part[:, at : at + 256] + theirs[:, back : back + 256]) * scale
        up = (part[:, at + 256 : at + 512] + theirs[:, back + 256 : back + 512]) * scale
        hidden[:, block * 256 : block * 256 + 256] = (
            gate / (1.0 + jnp.exp(-gate)) * up
        ).astype(BF16)
    quarter = w.shape[1] // 4
    for q in range(4):
        columns = slice(q * quarter, (q + 1) * quarter)
        full = jnp.dot(hidden[...], w[:, columns], preferred_element_type=F32)
        put_parts(full * weight[...], outs, columns, LATE)


def add(a, b):
    return (a.astype(F32) + b.astype(F32)).astype(BF16)


def reduce_rows(b0, b1t, b1b, b2t, b2b, b3t, b3b):
    far_left, far_right = ahead(b2t, 1), ahead(b2b, -1)
    left_b, right_t = ahead(b1b, 1), ahead(b3t, -1)
    left_t, right_b = ahead(add(b1t, far_left), 1), ahead(add(b3b, far_right), -1)
    left = jnp.concatenate([left_t, left_b])
    right = jnp.concatenate([right_t, right_b])
    mine = (b0.astype(F32) + left.astype(F32) + right.astype(F32)).astype(BF16)
    mine = mine.reshape(4, 16, mine.shape[1]).swapaxes(0, 1)
    return jnp.sum(plane(mine).astype(F32), axis=0)


def gather_rows(a):
    a0 = plane(jnp.broadcast_to(a, (16, *a.shape)))
    a0 = a0.swapaxes(0, 1).reshape(64, a.shape[1])
    top, bottom = a0[:32], a0[32:]
    left_t, right_b = ahead(top, 1), ahead(bottom, -1)
    left_b, right_t = ahead(bottom, 1), ahead(top, -1)
    return (a0, right_t, right_b, left_t, left_b), (ahead(left_t, 1), ahead(right_b, -1))


def shards(queries, cache, lengths, w_uv, w_out, residual, gain, ids, gates, w_gate, w_up, w_down):
    core = lax.axis_index(AXES) % 2
    half = residual.shape[1] // 2

    def own(w, axis):
        return lax.dynamic_slice_in_dim(w, core * half, half, axis)

    def away(w, axis):
        return lax.dynamic_slice_in_dim(w, (1 - core) * half, half, axis)

    sent, out_other = attend(lengths, queries.swapaxes(1, 2), cache.swapaxes(1, 2), w_out)
    uv_other = swap(w_uv[0])
    *packed, mark = pack(w_gate[0], w_up[0], w_down[0], out_other)
    blocks = pl.pallas_call(
        turn_kernel,
        in_specs=[VMEM, VMEM],
        out_specs=[VMEM] * 4,
        out_shape=[jax.ShapeDtypeStruct((64, LATENT), BF16)] * 4,
        compiler_params=pltpu.CompilerParams(vmem_limit_bytes=16 * MIB),
        name="turn",
    )(plane(sent), mark)
    blocks = exchange(blocks)
    out_other = swap(out_other)
    every = slice(None)
    w_out = load(
        (w_out, out_other),
        ((1, slice(0, VHEAD), every), (None, slice(VHEAD, 2 * VHEAD), every)),
        (2 * VHEAD, half),
        "load_out",
        8,
    )
    (mine,) = call(
        values_kernel,
        (*blocks, w_uv[0], uv_other),
        [((128, 2 * VHEAD), BF16)],
        "values",
        1 << 25,
    )
    gate_other, up_other, down_other = (swap(a) for a in packed)

    gates_hi = gates.astype(BF16)
    gates_lo = (gates - gates_hi.astype(F32)).astype(BF16)
    names = jnp.concatenate(
        [ids.astype(BF16), gates_hi, gates_lo, jnp.zeros((2, 128 - 3 * TOP), BF16)], axis=1
    )
    rows = jnp.concatenate(
        [
            jnp.concatenate([own(residual, 1), names], axis=1),
            swap(jnp.concatenate([away(residual, 1), names], axis=1)),
        ]
    )
    res, names = rows[:, :half].astype(F32), rows[:, half:]

    pieces = call(
        project_kernel,
        (mine, swap(mine), w_out),
        product_outs(half),
        "project",
        1 << 29,
        [pltpu.VMEM((256, 2 * VHEAD), BF16)],
    )
    mixed = res + reduce_rows(*pieces)

    scaled = (mixed * own(gain, 0)).astype(BF16)
    w_gu = load(
        (w_gate[0], w_up[0], gate_other, up_other),
        tuple((0 if n < 2 else None, every, slice(256 * n, 256 * n + 256)) for n in range(4)),
        (half, 1024),
        "load_gate_up",
        42,
    )
    near, far = gather_rows(jnp.concatenate([scaled, names], axis=1))
    back = (1.0 / own(gain, 0)).reshape(1, half)
    before = gate_up((), near, back, w_gu)
    part, sent, squares, weight = gate_up(before, far, back, w_gu)
    w_down = load(
        (w_down[0], down_other),
        ((1, slice(0, 256), every), (None, slice(256, 512), every)),
        (512, half),
        "load_down",
        46,
    )
    pieces = call(
        down_kernel,
        (part, squares, swap(sent), weight, w_down),
        product_outs(half),
        "down",
        1 << 30,
        [pltpu.VMEM((256, 512), BF16)],
    )
    result = (mixed + reduce_rows(*pieces)).astype(BF16)

    mine, other = result[:2], swap(result[2:])
    return jnp.where(
        core == 0, jnp.concatenate([mine, other], 1), jnp.concatenate([other, mine], 1)
    )


def solution(mesh):
    in_specs = (
        P(("grp", "dev"), None, None),
        P(("grp", "dev"), None, None),
        P(("grp", "dev")),
        P(("grp", "dev"), None, None),
        P(("grp", "dev"), None),
        P(("grp", "dev"), None),
        P(),
        P(("grp", "dev"), None),
        P(("grp", "dev"), None),
        P(("grp", "dev"), None, None),
        P(("grp", "dev"), None, None),
        P(("grp", "dev"), None, None),
    )
    out_specs = P(("grp", "dev"), None)
    return jax.shard_map(shards, mesh=mesh, in_specs=in_specs, out_specs=out_specs, check_vma=False)
```

time: 506 us -> 137 us (0.27)
  waiting for transfers between devices: 223 us -> 36.1 us
  blocking collectives: 197 us -> 12.8 us
  starting transfers between devices: 7.53 us -> 59.1 us
  matrix products: 30.9 us -> 0 us
  Pallas kernels: 0 us -> 23.7 us
  local copies, waits for them, and re-layouts: 19.3 us -> 3.15 us
  between operations: 13.5 us -> 0.34 us
  other arithmetic: 12 us -> 1.81 us
    all_gather x1 -> x0, blocking collectives: 175 us -> none  [shards(): every_ids = lax.all_gather(ids, ('grp', 'dev'), axis=0, tiled=True)]
    unnamed x3 -> x0, waiting for transfers between devices: 156 us -> none
    ppermute x0 -> x30, starting transfers between devices: none -> 45.2 us  [the longest x21 23 us: ahead(): lax.ppermute(a, AXES, [(r[i], r[(i + step) % 4]) for r in RINGS for i in...]
    all_to_all x1 -> x3, waiting for transfers between devices: 46.8 us -> 12.5 us  [plane(): return lax.all_to_all(a, AXES, 0, 0, axis_index_groups=PLANES, tiled=True)]
    dot_general x7 -> x0, matrix products: 26.7 us -> none  [the longest x1 6.95 us: shards(): jnp.einsum('ncr,nrd->ncd', chosen, every_rows.reshape(devices, rows_dev,...]
    pallas_call x0 -> x11, Pallas kernels: none -> 23.7 us  [the longest x1 7.42 us: attend(): pl.pallas_call(attend_kernel, grid_spec=pltpu.PrefetchScalarGridSpec(num_...]
    ppermute x0 -> x30, waiting for transfers between devices: none -> 23.6 us  [the longest x21 22.2 us: ahead(): lax.ppermute(a, AXES, [(r[i], r[(i + step) % 4]) for r in RINGS for i in...]
    all_gather x1 -> x0, waiting for transfers between devices: 20.4 us -> none  [shards(): every_rows = lax.all_gather(normed, ('grp', 'dev'), axis=0, tiled=True)]
  transfers between devices with their start and end apart: 3 -> 33, of which waited for: 3 -> 19; matrix products, arithmetic and copies ran while one was open for 0% -> 2% of each run, Pallas kernels for 0% -> 10%
where the time goes in v1:
time: 137 us
  starting transfers between devices  59.1 us (43%)
  waiting for transfers between devices  36.1 us (26%)
  Pallas kernels  23.7 us (17%)
  blocking collectives  12.8 us (9%)
  local copies, waits for them, and re-layouts  3.15 us (2%)
  other arithmetic  1.81 us (1%)
    ppermute x21, starting transfers between devices, ahead(): lax.ppermute(a, AXES, [(r[i], r[(i + step) % 4]) for r in RINGS for i in...  23 us
    ppermute x21, waiting for transfers between devices, ahead(): lax.ppermute(a, AXES, [(r[i], r[(i + step) % 4]) for r in RINGS for i in...  22.2 us
    ppermute x9, starting transfers between devices, swap(): return lax.ppermute(a, AXES, SIBLING)  22.2 us
    all_to_all x3, starting transfers between devices, plane(): return lax.all_to_all(a, AXES, 0, 0, axis_index_groups=PLANES, tiled=True)  14 us
    all_to_all x1, blocking collectives, plane(): return lax.all_to_all(a, AXES, 0, 0, axis_index_groups=PLANES, tiled=True)  12.8 us
    all_to_all x3, waiting for transfers between devices, plane(): return lax.all_to_all(a, AXES, 0, 0, axis_index_groups=PLANES, tiled=True)  12.5 us
    pallas_call x1, Pallas kernels, attend(): pl.pallas_call(attend_kernel, grid_spec=pltpu.PrefetchScalarGridSpec(num_...  7.42 us
    pallas_call x5, Pallas kernels, call(): pl.pallas_call(kernel, in_specs=[VMEM] * len(args), out_specs=[VMEM] * le...  6.59 us
  transfers between devices with their start and end apart: 33, of which 19 were waited for; matrix products, arithmetic and copies ran while one was open for 2% of the time, Pallas kernels for 10%

profile of v1, /device:TPU:1, one launch (start us, length us, event | category | flops | bytes accessed | tf_op | source)
XLA Modules:
  0.0 137.1 jit_solution(3677243850018859032)
XLA Ops:
  0.0 7.4 %attend.1 = (bf16[16,16,512]{2,1,0:T(8,128)(2,1)}, bf16[128,3584]{1,0:T(8,128)(2,1)}) custom-call(s32[2]{0:T(128)} %lens.1, bf16[2,576,128]{2,1,0:T(8,128)(2,1)} %bitcast.33, bf16[2,576,2048]{2,1,0:T(8,128)(2,1)} %bitcast.27, bf16[128,7168]{1,0:T(8,128)(2,1)} %refs_0_.1), custom_call_target="tpu_custom_call" | custom-call | tf_op jit(solution)/shard_map/attend/pallas_call | solution.py:143
  7.4 1.5 %collective-permute-start.6 = (bf16[128,3584]{1,0:T(8,128)(2,1)}, bf16[128,3584]{1,0:T(8,128)(2,1)S(1)}, u32[]{:S(2)}, u32[]{:S(2)}) collective-permute-start(bf16[128,3584]{1,0:T(8,128)(2,1)} %get-tuple-element.38.after), channel_id=1, source_target_pairs={{0,1},{1,0},{2,3},{3,2},{4,5},{5,4},{6,7},{7,6},{8,9},{9,8},{10,11... | collective-permute-start | bytes 2752520 | tf_op jit(solution)/shard_map/ppermute | solution.py:37
  8.9 6.8 %all-to-all-start = ((bf16[16,16,512]{2,1,0:T(8,128)(2,1)}), bf16[16,16,512]{2,1,0:T(8,128)(2,1)S(1)}, u32[]{:S(2)}, u32[]{:S(2)}) async-start(bf16[16,16,512]{2,1,0:T(8,128)(2,1)} %get-tuple-element.37), calls=%async_computation | async-start | bytes 524288 | tf_op jit(solution)/shard_map/all_to_all | solution.py:45
  17.2 4.4 %pack.1 = (bf16[3584,256]{1,0:T(8,128)(2,1)}, bf16[3584,256]{1,0:T(8,128)(2,1)}, bf16[256,3584]{1,0:T(8,128)(2,1)}, f32[8,128]{1,0:T(8,128)S(1)}) custom-call(bf16[7168,256]{1,0:T(8,128)(2,1)} %bitcast.23, bf16[7168,256]{1,0:T(8,128)(2,1)} %bitcast.25, bf16[256,7168]{1,0:T(8,128)(2,1)} %bitcast.21, bf16[128,3584]{1,0:T(8,128)(2,1)} %get-tuple-element.38.after), custom_call_target="tpu_custom_call" | custom-call | bytes 12582912 | tf_op jit(solution)/shard_map/pack/pallas_call | solution.py:230
  21.6 1.7 %all-to-all-done.got = bf16[16,16,512]{2,1,0:T(8,128)(2,1)S(1)} async-done(((bf16[16,16,512]{2,1,0:T(8,128)(2,1)}), bf16[16,16,512]{2,1,0:T(8,128)(2,1)S(1)}, u32[]{:S(2)}, u32[]{:S(2)}) %all-to-all-start) | async-done | bytes 262176 | tf_op jit(solution)/shard_map/all_to_all | solution.py:45
  23.6 4.6 %collective-permute-start.1 = (bf16[64,512]{1,0:T(8,128)(2,1)S(1)}, bf16[64,512]{1,0:T(8,128)(2,1)S(1)}, u32[]{:S(2)}, u32[]{:S(2)}) collective-permute-start(bf16[64,512]{1,0:T(8,128)(2,1)S(1)} %get-tuple-element.41), channel_id=1, source_target_pairs={{0,6},{2,0},{4,2},{6,4},{8,14},{10,8},{12,10},{14,12},{16,22},{18,... | collective-permute-start | bytes 196616 | tf_op jit(solution)/shard_map/ppermute | solution.py:41
  30.1 2.8 %collective-permute-done.2.p2 = bf16[64,512]{1,0:T(8,128)(2,1)S(1)} collective-permute-done((bf16[64,512]{1,0:T(8,128)(2,1)S(1)}, bf16[64,512]{1,0:T(8,128)(2,1)S(1)}, u32[]{:S(2)}, u32[]{:S(2)}) %collective-permute-start.2) | collective-permute-done | bytes 65568 | tf_op jit(solution)/shard_map/ppermute | solution.py:41
  33.4 3.9 %collective-permute-start.5 = (bf16[128,256]{1,0:T(8,128)(2,1)S(1)}, bf16[128,256]{1,0:T(8,128)(2,1)S(1)}, u32[]{:S(2)}, u32[]{:S(2)}) collective-permute-start(bf16[128,256]{1,0:T(8,128)(2,1)S(1)} %values.1.mine), channel_id=1, source_target_pairs={{0,1},{1,0},{2,3},{3,2},{4,5},{5,4},{6,7},{7,6},{8,9},{9,8},{10,11... | collective-permute-start | bytes 196616 | tf_op jit(solution)/shard_map/ppermute | solution.py:37
  42.0 2.2 %collective-permute-done.11 = bf16[32,3584]{1,0:T(8,128)(2,1)S(1)} collective-permute-done((bf16[32,3584]{1,0:T(8,128)(2,1)S(1)}, bf16[32,3584]{1,0:T(8,128)(2,1)S(1)}, u32[]{:S(2)}, u32[]{:S(2)}) %collective-permute-start.11) | collective-permute-done | bytes 229408 | tf_op jit(solution)/shard_map/ppermute | solution.py:41
  46.7 1.6 %collective-permute-done.9 = bf16[32,3584]{1,0:T(8,128)(2,1)S(1)} collective-permute-done((bf16[32,3584]{1,0:T(8,128)(2,1)S(1)}, bf16[32,3584]{1,0:T(8,128)(2,1)S(1)}, u32[]{:S(2)}, u32[]{:S(2)}) %collective-permute-start.9) | collective-permute-done | bytes 229408 | tf_op jit(solution)/shard_map/ppermute | solution.py:41
  49.5 2.7 %collective-permute-done.8 = bf16[32,3584]{1,0:T(8,128)(2,1)S(1)} collective-permute-done((bf16[32,3584]{1,0:T(8,128)(2,1)S(1)}, bf16[32,3584]{1,0:T(8,128)(2,1)S(1)}, u32[]{:S(2)}, u32[]{:S(2)}) %collective-permute-start.8) | collective-permute-done | bytes 229408 | tf_op jit(solution)/shard_map/ppermute | solution.py:41
  53.6 3.6 %all-to-all-start.1 = ((bf16[16,4,3584]{2,1,0:T(4,128)(2,1)}), bf16[16,4,3584]{2,1,0:T(4,128)(2,1)S(1)}, u32[]{:S(2)}, u32[]{:S(2)}) async-start(bf16[16,4,3584]{2,1,0:T(4,128)(2,1)} %bitcast.17), calls=%async_computation.1 | async-start | bytes 917504 | tf_op jit(solution)/shard_map/all_to_all | solution.py:45
  57.4 2.4 %collective-permute-start = (bf16[2,3712]{1,0:T(2,128)(2,1)S(1)}, bf16[2,3712]{1,0:T(2,128)(2,1)S(1)}, u32[]{:S(2)}, u32[]{:S(2)}) collective-permute-start(bf16[2,3712]{1,0:T(2,128)(2,1)S(1)} %concatenate.34), channel_id=1, source_target_pairs={{0,1},{1,0},{2,3},{3,2},{4,5},{5,4},{6,7},{7,6},{8,9},{9,8},{10,11... | collective-permute-start | bytes 44552 | tf_op jit(solution)/shard_map/ppermute | solution.py:37
  60.4 5.3 %all-to-all-done.1 = bf16[16,4,3584]{2,1,0:T(4,128)(2,1)S(1)} async-done(((bf16[16,4,3584]{2,1,0:T(4,128)(2,1)}), bf16[16,4,3584]{2,1,0:T(4,128)(2,1)S(1)}, u32[]{:S(2)}, u32[]{:S(2)}) %all-to-all-start.1) | async-done | bytes 458784 | tf_op jit(solution)/shard_map/all_to_all | solution.py:45
  67.0 3.6 %all-to-all-start.2 = ((bf16[16,4,3712]{2,1,0:T(4,128)(2,1)}), bf16[16,4,3712]{2,1,0:T(4,128)(2,1)S(1)}, u32[]{:S(2)}, u32[]{:S(2)}) async-start(bf16[16,4,3712]{2,1,0:T(4,128)(2,1)} %broadcast_in_dim.8), calls=%async_computation.2 | async-start | bytes 950272 | tf_op jit(solution)/shard_map/all_to_all | solution.py:45
  70.5 3.2 %collective-permute-start.22 = (bf16[256,3584]{1,0:T(8,128)(2,1)}, bf16[256,3584]{1,0:T(8,128)(2,1)}, u32[]{:S(2)}, u32[]{:S(2)}) collective-permute-start(bf16[256,3584]{1,0:T(8,128)(2,1)} %get-tuple-element.61), channel_id=1, source_target_pairs={{0,1},{1,0},{2,3},{3,2},{4,5},{5,4},{6,7},{7,6},{8,9},{9,8},{10,11... | collective-permute-start | bytes 5505032 | tf_op jit(solution)/shard_map/ppermute | solution.py:37
  73.7 5.4 %all-to-all-done.2 = bf16[16,4,3712]{2,1,0:T(4,128)(2,1)S(1)} async-done(((bf16[16,4,3712]{2,1,0:T(4,128)(2,1)}), bf16[16,4,3712]{2,1,0:T(4,128)(2,1)S(1)}, u32[]{:S(2)}, u32[]{:S(2)}) %all-to-all-start.2) | async-done | bytes 475168 | tf_op jit(solution)/shard_map/all_to_all | solution.py:45
  79.7 2.7 %collective-permute-start.14 = (bf16[32,3712]{1,0:T(8,128)(2,1)S(1)}, bf16[32,3712]{1,0:T(8,128)(2,1)S(1)}, u32[]{:S(2)}, u32[]{:S(2)}) collective-permute-start(bf16[32,3712]{1,0:T(8,128)(2,1)S(1)} %bitcast.34), channel_id=1, source_target_pairs={{0,6},{2,0},{4,2},{6,4},{8,14},{10,8},{12,10},{14,12},{16,22},{18,... | collective-permute-start | bytes 712712 | tf_op jit(solution)/shard_map/ppermute | solution.py:41
  83.8 2.0 %collective-permute-done.15.refs_3_ = bf16[32,3712]{1,0:T(8,128)(2,1)S(1)} collective-permute-done((bf16[32,3712]{1,0:T(8,128)(2,1)S(1)}, bf16[32,3712]{1,0:T(8,128)(2,1)S(1)}, u32[]{:S(2)}, u32[]{:S(2)}) %collective-permute-start.15) | collective-permute-done | bytes 237600 | tf_op jit(solution)/shard_map/ppermute | solution.py:41
  85.8 2.7 %collective-permute-start.20 = (bf16[32,3712]{1,0:T(8,128)(2,1)S(1)}, bf16[32,3712]{1,0:T(8,128)(2,1)S(1)}, u32[]{:S(2)}, u32[]{:S(2)}) collective-permute-start(bf16[32,3712]{1,0:T(8,128)(2,1)S(1)} %collective-permute-done.14.refs_2_), channel_id=1, source_target_pairs={{0,6},{2,0},{4,2},{6,4},{8,14},{10,8},{12,10},{14,12},{16,22},{18,... | collective-permute-start | bytes 712712 | tf_op jit(solution)/shard_map/ppermute | solution.py:41
  88.5 2.7 %load_gate_up.1.refs_6_.refs_7_ = bf16[3584,1024]{1,0:T(8,128)(2,1)S(1)} custom-call(bf16[7168,256]{1,0:T(8,128)(2,1)} %bitcast.24, bf16[7168,256]{1,0:T(8,128)(2,1)} %bitcast.26, bf16[3584,256]{1,0:T(8,128)(2,1)S(1)} %collective-permute-done.17.refs_2_, bf16[3584,256]{1,0:T(8,128)(2,1)} %collective-permute-done.18.refs_3_), custom_call_target="tpu_custom_call" | custom-call | bytes 14680064 | tf_op jit(solution)/shard_map/load_gate_up/pallas_call | solution.py:196
  91.3 2.1 %gate_up.2 = (f32[192,1024]{1,0:T(8,128)S(1)}, bf16[192,1152]{1,0:T(8,128)(2,1)S(1)}, f32[192,1]{1,0:T(8,128)S(1)}, f32[192,1]{1,0:T(8,128)S(1)}) custom-call(bf16[64,3712]{1,0:T(8,128)(2,1)S(1)} %bitcast.18, bf16[32,3712]{1,0:T(8,128)(2,1)S(1)} %collective-permute-done.13.refs_1_, bf16[32,3712]{1,0:T(8,128)(2,1)S(1)} %collective-permute-done.14.refs_2_, ...), custom_call_target="tpu_custom_call" | custom-call | flops 1610612736 | bytes 1048576 | tf_op jit(solution)/shard_map/gate_up/pallas_call | solution.py:245
  93.4 1.6 %gate_up.3 = (f32[256,1024]{1,0:T(8,128)S(1)}, bf16[256,1152]{1,0:T(8,128)(2,1)S(1)}, f32[256,1]{1,0:T(8,128)S(1)}, f32[256,1]{1,0:T(8,128)S(1)}) custom-call(f32[192,1024]{1,0:T(8,128)S(1)} %get-tuple-element.53.refs_0_, bf16[192,1152]{1,0:T(8,128)(2,1)S(1)} %get-tuple-element.54.refs_1_, f32[192,1]{1,0:T(8,128)S(1)} %get-tuple-element.55.refs_2_, ...), custom_call_target="tpu_custom_call" | custom-call | flops 536870912 | bytes 1048576 | tf_op jit(solution)/shard_map/gate_up/pallas_call | solution.py:245
  95.0 5.8 %collective-permute-start.21 = (bf16[256,1152]{1,0:T(8,128)(2,1)S(1)}, bf16[256,1152]{1,0:T(8,128)(2,1)S(1)}, u32[]{:S(2)}, u32[]{:S(2)}) collective-permute-start(bf16[256,1152]{1,0:T(8,128)(2,1)S(1)} %get-tuple-element.59), channel_id=1, source_target_pairs={{0,1},{1,0},{2,3},{3,2},{4,5},{5,4},{6,7},{7,6},{8,9},{9,8},{10,11... | collective-permute-start | bytes 1769480 | tf_op jit(solution)/shard_map/ppermute | solution.py:37
  100.9 2.1 %load_down.1.w = bf16[512,3584]{1,0:T(8,128)(2,1)S(1)} custom-call(bf16[256,7168]{1,0:T(8,128)(2,1)} %bitcast.22, bf16[256,3584]{1,0:T(8,128)(2,1)} %collective-permute-done.22.refs_1_), custom_call_target="tpu_custom_call" | custom-call | bytes 7340032 | tf_op jit(solution)/shard_map/load_down/pallas_call | solution.py:196
  103.0 1.9 %down.1 = (bf16[64,3584]{1,0:T(8,128)(2,1)S(1)}, bf16[32,3584]{1,0:T(8,128)(2,1)S(1)}, bf16[32,3584]{1,0:T(8,128)(2,1)S(1)}, bf16[32,3584]{1,0:T(8,128)(2,1)S(1)...) custom-call(f32[256,1024]{1,0:T(8,128)S(1)} %get-tuple-element.57.part, ...), custom_call_target="tpu_custom_call" | custom-call | flops 1073741824 | bytes 1048576 | tf_op jit(solution)/shard_map/down/pallas_call | solution.py:245
  106.7 2.3 %collective-permute-start.26 = (bf16[32,3584]{1,0:T(8,128)(2,1)S(1)}, bf16[32,3584]{1,0:T(8,128)(2,1)S(1)}, u32[]{:S(2)}, u32[]{:S(2)}) collective-permute-start(bf16[32,3584]{1,0:T(8,128)(2,1)S(1)} %get-tuple-element.66), channel_id=1, source_target_pairs={{0,6},{2,0},{4,2},{6,4},{8,14},{10,8},{12,10},{14,12},{16,22},{18,... | collective-permute-start | bytes 688136 | tf_op jit(solution)/shard_map/ppermute | solution.py:41
  110.1 2.0 %collective-permute-start.28 = (bf16[32,3584]{1,0:T(8,128)(2,1)S(1)}, bf16[32,3584]{1,0:T(8,128)(2,1)S(1)}, u32[]{:S(2)}, u32[]{:S(2)}) collective-permute-start(bf16[32,3584]{1,0:T(8,128)(2,1)S(1)} %add_convert_fusion.2), channel_id=1, source_target_pairs={{0,6},{2,0},{4,2},{6,4},{8,14},{10,8},{12,10},{14,12},{16,22},{18,... | collective-permute-start | bytes 688136 | tf_op jit(solution)/shard_map/ppermute | solution.py:41
  112.4 2.3 %collective-permute-done.25 = bf16[32,3584]{1,0:T(8,128)(2,1)S(1)} collective-permute-done((bf16[32,3584]{1,0:T(8,128)(2,1)S(1)}, bf16[32,3584]{1,0:T(8,128)(2,1)S(1)}, u32[]{:S(2)}, u32[]{:S(2)}) %collective-permute-start.25) | collective-permute-done | bytes 229408 | tf_op jit(solution)/shard_map/ppermute | solution.py:41
  115.4 3.1 %collective-permute-done.24 = bf16[32,3584]{1,0:T(8,128)(2,1)S(1)} collective-permute-done((bf16[32,3584]{1,0:T(8,128)(2,1)S(1)}, bf16[32,3584]{1,0:T(8,128)(2,1)S(1)}, u32[]{:S(2)}, u32[]{:S(2)}) %collective-permute-start.24) | collective-permute-done | bytes 229408 | tf_op jit(solution)/shard_map/ppermute | solution.py:41
  119.0 12.8 %all_to_all.20 = bf16[16,4,3584]{2,1,0:T(4,128)(2,1)S(1)} all-to-all(bf16[16,4,3584]{2,1,0:T(4,128)(2,1)S(1)} %bitcast.32), channel_id=1, replica_groups={{0,8,16,24,32,40,48,56,64,72,80,88,96,104,112,120},{2,10,18,26,34,42,50..., dimensions={0} | all-to-all | bytes 917504 | tf_op jit(solution)/shard_map/all_to_all | solution.py:45
  132.1 3.5 %collective-permute-start.29 = (bf16[2,3584]{1,0:T(2,128)(2,1)S(1)}, bf16[2,3584]{1,0:T(2,128)(2,1)S(1)}, u32[]{:S(2)}, u32[]{:S(2)}) collective-permute-start(bf16[2,3584]{1,0:T(2,128)(2,1)S(1)} %get-tuple-element.76), channel_id=1, source_target_pairs={{0,1},{1,0},{2,3},{3,2},{4,5},{5,4},{6,7},{7,6},{8,9},{9,8},{10,11... | collective-permute-start | bytes 43016 | tf_op jit(solution)/shard_map/ppermute | solution.py:37
  (86 shorter events, 24.0 us)
Async XLA Ops:
  7.4 29.8 %collective-permute-start.6 = (bf16[128,3584]{1,0:T(8,128)(2,1)}, bf16[128,3584]{1,0:T(8,128)(2,1)S(1)}, u32[]{:S(2)}, u32[]{:S(2)}) collective-permute-start(bf16[128,3584]{1,0:T(8,128)(2,1)} %get-tuple-element.38.after), channel_id=1, source_target_pairs={{0,1},{1,0},{2,3},{3,2},{4,5},{5,4},{6,7},{7,6},{8,9},{9,8},{10,11... | collective-permute-start | bytes 2752520 | tf_op jit(solution)/shard_map/ppermute | solution.py:37
  8.9 14.4 %all-to-all-start = ((bf16[16,16,512]{2,1,0:T(8,128)(2,1)}), bf16[16,16,512]{2,1,0:T(8,128)(2,1)S(1)}, u32[]{:S(2)}, u32[]{:S(2)}) async-start(bf16[16,16,512]{2,1,0:T(8,128)(2,1)} %get-tuple-element.37), calls=%async_computation | async-start | bytes 524288 | tf_op jit(solution)/shard_map/all_to_all | solution.py:45
  15.8 13.0 %collective-permute-start.4 = (bf16[512,128]{1,0:T(8,128)(2,1)S(1)}, bf16[512,128]{1,0:T(8,128)(2,1)S(1)}, u32[]{:S(2)}, u32[]{:S(2)}) collective-permute-start(bf16[512,128]{1,0:T(8,128)(2,1)S(1)} %bitcast.19), channel_id=1, source_target_pairs={{0,1},{1,0},{2,3},{3,2},{4,5},{5,4},{6,7},{7,6},{8,9},{9,8},{10,11... | collective-permute-start | bytes 393224 | tf_op jit(solution)/shard_map/ppermute | solution.py:37
  23.6 6.5 %collective-permute-start.1 = (bf16[64,512]{1,0:T(8,128)(2,1)S(1)}, bf16[64,512]{1,0:T(8,128)(2,1)S(1)}, u32[]{:S(2)}, u32[]{:S(2)}) collective-permute-start(bf16[64,512]{1,0:T(8,128)(2,1)S(1)} %get-tuple-element.41), channel_id=1, source_target_pairs={{0,6},{2,0},{4,2},{6,4},{8,14},{10,8},{12,10},{14,12},{16,22},{18,... | collective-permute-start | bytes 196616 | tf_op jit(solution)/shard_map/ppermute | solution.py:41
  28.2 4.7 %collective-permute-start.2 = (bf16[64,512]{1,0:T(8,128)(2,1)S(1)}, bf16[64,512]{1,0:T(8,128)(2,1)S(1)}, u32[]{:S(2)}, u32[]{:S(2)}) collective-permute-start(bf16[64,512]{1,0:T(8,128)(2,1)S(1)} %get-tuple-element.42), channel_id=1, source_target_pairs={{0,4},{2,6},{4,0},{6,2},{8,12},{10,14},{12,8},{14,10},{16,20},{18,... | collective-permute-start | bytes 196616 | tf_op jit(solution)/shard_map/ppermute | solution.py:41
  28.2 5.0 %collective-permute-start.3 = (bf16[64,512]{1,0:T(8,128)(2,1)S(1)}, bf16[64,512]{1,0:T(8,128)(2,1)S(1)}, u32[]{:S(2)}, u32[]{:S(2)}) collective-permute-start(bf16[64,512]{1,0:T(8,128)(2,1)S(1)} %get-tuple-element.43), channel_id=1, source_target_pairs={{0,2},{2,4},{4,6},{6,0},{8,10},{10,12},{12,14},{14,8},{16,18},{18,... | collective-permute-start | bytes 196616 | tf_op jit(solution)/shard_map/ppermute | solution.py:41
  33.4 4.8 %collective-permute-start.5 = (bf16[128,256]{1,0:T(8,128)(2,1)S(1)}, bf16[128,256]{1,0:T(8,128)(2,1)S(1)}, u32[]{:S(2)}, u32[]{:S(2)}) collective-permute-start(bf16[128,256]{1,0:T(8,128)(2,1)S(1)} %values.1.mine), channel_id=1, source_target_pairs={{0,1},{1,0},{2,3},{3,2},{4,5},{5,4},{6,7},{7,6},{8,9},{9,8},{10,11... | collective-permute-start | bytes 196616 | tf_op jit(solution)/shard_map/ppermute | solution.py:37
  39.0 5.2 %collective-permute-start.11 = (bf16[32,3584]{1,0:T(8,128)(2,1)S(1)}, bf16[32,3584]{1,0:T(8,128)(2,1)S(1)}, u32[]{:S(2)}, u32[]{:S(2)}) collective-permute-start(bf16[32,3584]{1,0:T(8,128)(2,1)S(1)} %get-tuple-element.50), channel_id=1, source_target_pairs={{0,6},{2,0},{4,2},{6,4},{8,14},{10,8},{12,10},{14,12},{16,22},{18,... | collective-permute-start | bytes 688136 | tf_op jit(solution)/shard_map/ppermute | solution.py:41
  39.2 6.5 %collective-permute-start.7 = (bf16[32,3584]{1,0:T(8,128)(2,1)S(1)}, bf16[32,3584]{1,0:T(8,128)(2,1)S(1)}, u32[]{:S(2)}, u32[]{:S(2)}) collective-permute-start(bf16[32,3584]{1,0:T(8,128)(2,1)S(1)} %get-tuple-element.46), channel_id=1, source_target_pairs={{0,2},{2,4},{4,6},{6,0},{8,10},{10,12},{12,14},{14,8},{16,18},{18,... | collective-permute-start | bytes 688136 | tf_op jit(solution)/shard_map/ppermute | solution.py:41
  40.5 6.2 %collective-permute-start.10 = (bf16[32,3584]{1,0:T(8,128)(2,1)S(1)}, bf16[32,3584]{1,0:T(8,128)(2,1)S(1)}, u32[]{:S(2)}, u32[]{:S(2)}) collective-permute-start(bf16[32,3584]{1,0:T(8,128)(2,1)S(1)} %get-tuple-element.48), channel_id=1, source_target_pairs={{0,6},{2,0},{4,2},{6,4},{8,14},{10,8},{12,10},{14,12},{16,22},{18,... | collective-permute-start | bytes 688136 | tf_op jit(solution)/shard_map/ppermute | solution.py:41
  41.9 6.4 %collective-permute-start.9 = (bf16[32,3584]{1,0:T(8,128)(2,1)S(1)}, bf16[32,3584]{1,0:T(8,128)(2,1)S(1)}, u32[]{:S(2)}, u32[]{:S(2)}) collective-permute-start(bf16[32,3584]{1,0:T(8,128)(2,1)S(1)} %get-tuple-element.47), channel_id=1, source_target_pairs={{0,2},{2,4},{4,6},{6,0},{8,10},{10,12},{12,14},{14,8},{16,18},{18,... | collective-permute-start | bytes 688136 | tf_op jit(solution)/shard_map/ppermute | solution.py:41
  44.3 5.2 %collective-permute-start.12 = (bf16[32,3584]{1,0:T(8,128)(2,1)S(1)}, bf16[32,3584]{1,0:T(8,128)(2,1)S(1)}, u32[]{:S(2)}, u32[]{:S(2)}) collective-permute-start(bf16[32,3584]{1,0:T(8,128)(2,1)S(1)} %add_convert_fusion.4), channel_id=1, source_target_pairs={{0,6},{2,0},{4,2},{6,4},{8,14},{10,8},{12,10},{14,12},{16,22},{18,... | collective-permute-start | bytes 688136 | tf_op jit(solution)/shard_map/ppermute | solution.py:41
  45.8 6.4 %collective-permute-start.8 = (bf16[32,3584]{1,0:T(8,128)(2,1)S(1)}, bf16[32,3584]{1,0:T(8,128)(2,1)S(1)}, u32[]{:S(2)}, u32[]{:S(2)}) collective-permute-start(bf16[32,3584]{1,0:T(8,128)(2,1)S(1)} %add_convert_fusion.5), channel_id=1, source_target_pairs={{0,2},{2,4},{4,6},{6,0},{8,10},{10,12},{12,14},{14,8},{16,18},{18,... | collective-permute-start | bytes 688136 | tf_op jit(solution)/shard_map/ppermute | solution.py:41
  53.6 12.2 %all-to-all-start.1 = ((bf16[16,4,3584]{2,1,0:T(4,128)(2,1)}), bf16[16,4,3584]{2,1,0:T(4,128)(2,1)S(1)}, u32[]{:S(2)}, u32[]{:S(2)}) async-start(bf16[16,4,3584]{2,1,0:T(4,128)(2,1)} %bitcast.17), calls=%async_computation.1 | async-start | bytes 917504 | tf_op jit(solution)/shard_map/all_to_all | solution.py:45
  57.4 8.6 %collective-permute-start = (bf16[2,3712]{1,0:T(2,128)(2,1)S(1)}, bf16[2,3712]{1,0:T(2,128)(2,1)S(1)}, u32[]{:S(2)}, u32[]{:S(2)}) collective-permute-start(bf16[2,3712]{1,0:T(2,128)(2,1)S(1)} %concatenate.34), channel_id=1, source_target_pairs={{0,1},{1,0},{2,3},{3,2},{4,5},{5,4},{6,7},{7,6},{8,9},{9,8},{10,11... | collective-permute-start | bytes 44552 | tf_op jit(solution)/shard_map/ppermute | solution.py:37
  59.7 22.6 %collective-permute-start.17 = (bf16[3584,256]{1,0:T(8,128)(2,1)}, bf16[3584,256]{1,0:T(8,128)(2,1)S(1)}, u32[]{:S(2)}, u32[]{:S(2)}) collective-permute-start(bf16[3584,256]{1,0:T(8,128)(2,1)} %get-tuple-element.51), channel_id=1, source_target_pairs={{0,1},{1,0},{2,3},{3,2},{4,5},{5,4},{6,7},{7,6},{8,9},{9,8},{10,11... | collective-permute-start | bytes 5505032 | tf_op jit(solution)/shard_map/ppermute | solution.py:37
  59.8 22.5 %collective-permute-start.18 = (bf16[3584,256]{1,0:T(8,128)(2,1)}, bf16[3584,256]{1,0:T(8,128)(2,1)}, u32[]{:S(2)}, u32[]{:S(2)}) collective-permute-start(bf16[3584,256]{1,0:T(8,128)(2,1)} %get-tuple-element.52), channel_id=1, source_target_pairs={{0,1},{1,0},{2,3},{3,2},{4,5},{5,4},{6,7},{7,6},{8,9},{9,8},{10,11... | collective-permute-start | bytes 5505032 | tf_op jit(solution)/shard_map/ppermute | solution.py:37
  67.0 12.2 %all-to-all-start.2 = ((bf16[16,4,3712]{2,1,0:T(4,128)(2,1)}), bf16[16,4,3712]{2,1,0:T(4,128)(2,1)S(1)}, u32[]{:S(2)}, u32[]{:S(2)}) async-start(bf16[16,4,3712]{2,1,0:T(4,128)(2,1)} %broadcast_in_dim.8), calls=%async_computation.2 | async-start | bytes 950272 | tf_op jit(solution)/shard_map/all_to_all | solution.py:45
  70.5 30.4 %collective-permute-start.22 = (bf16[256,3584]{1,0:T(8,128)(2,1)}, bf16[256,3584]{1,0:T(8,128)(2,1)}, u32[]{:S(2)}, u32[]{:S(2)}) collective-permute-start(bf16[256,3584]{1,0:T(8,128)(2,1)} %get-tuple-element.61), channel_id=1, source_target_pairs={{0,1},{1,0},{2,3},{3,2},{4,5},{5,4},{6,7},{7,6},{8,9},{9,8},{10,11... | collective-permute-start | bytes 5505032 | tf_op jit(solution)/shard_map/ppermute | solution.py:37
  79.6 6.2 %collective-permute-start.15 = (bf16[32,3712]{1,0:T(8,128)(2,1)S(1)}, bf16[32,3712]{1,0:T(8,128)(2,1)S(1)}, u32[]{:S(2)}, u32[]{:S(2)}) collective-permute-start(bf16[32,3712]{1,0:T(8,128)(2,1)S(1)} %bitcast.36), channel_id=1, source_target_pairs={{0,2},{2,4},{4,6},{6,0},{8,10},{10,12},{12,14},{14,8},{16,18},{18,... | collective-permute-start | bytes 712712 | tf_op jit(solution)/shard_map/ppermute | solution.py:41
  79.7 6.2 %collective-permute-start.14 = (bf16[32,3712]{1,0:T(8,128)(2,1)S(1)}, bf16[32,3712]{1,0:T(8,128)(2,1)S(1)}, u32[]{:S(2)}, u32[]{:S(2)}) collective-permute-start(bf16[32,3712]{1,0:T(8,128)(2,1)S(1)} %bitcast.34), channel_id=1, source_target_pairs={{0,6},{2,0},{4,2},{6,4},{8,14},{10,8},{12,10},{14,12},{16,22},{18,... | collective-permute-start | bytes 712712 | tf_op jit(solution)/shard_map/ppermute | solution.py:41
  82.3 9.0 %collective-permute-start.13 = (bf16[32,3712]{1,0:T(8,128)(2,1)S(1)}, bf16[32,3712]{1,0:T(8,128)(2,1)S(1)}, u32[]{:S(2)}, u32[]{:S(2)}) collective-permute-start(bf16[32,3712]{1,0:T(8,128)(2,1)S(1)} %bitcast.37), channel_id=1, source_target_pairs={{0,6},{2,0},{4,2},{6,4},{8,14},{10,8},{12,10},{14,12},{16,22},{18,... | collective-permute-start | bytes 712712 | tf_op jit(solution)/shard_map/ppermute | solution.py:41
  82.4 9.0 %collective-permute-start.16 = (bf16[32,3712]{1,0:T(8,128)(2,1)S(1)}, bf16[32,3712]{1,0:T(8,128)(2,1)S(1)}, u32[]{:S(2)}, u32[]{:S(2)}) collective-permute-start(bf16[32,3712]{1,0:T(8,128)(2,1)S(1)} %bitcast.35), channel_id=1, source_target_pairs={{0,2},{2,4},{4,6},{6,0},{8,10},{10,12},{12,14},{14,8},{16,18},{18,... | collective-permute-start | bytes 712712 | tf_op jit(solution)/shard_map/ppermute | solution.py:41
  85.8 7.6 %collective-permute-start.19 = (bf16[32,3712]{1,0:T(8,128)(2,1)S(1)}, bf16[32,3712]{1,0:T(8,128)(2,1)S(1)}, u32[]{:S(2)}, u32[]{:S(2)}) collective-permute-start(bf16[32,3712]{1,0:T(8,128)(2,1)S(1)} %collective-permute-done.15.refs_3_), channel_id=1, source_target_pairs={{0,2},{2,4},{4,6},{6,0},{8,10},{10,12},{12,14},{14,8},{16,18},{18,... | collective-permute-start | bytes 712712 | tf_op jit(solution)/shard_map/ppermute | solution.py:41
  85.8 7.6 %collective-permute-start.20 = (bf16[32,3712]{1,0:T(8,128)(2,1)S(1)}, bf16[32,3712]{1,0:T(8,128)(2,1)S(1)}, u32[]{:S(2)}, u32[]{:S(2)}) collective-permute-start(bf16[32,3712]{1,0:T(8,128)(2,1)S(1)} %collective-permute-done.14.refs_2_), channel_id=1, source_target_pairs={{0,6},{2,0},{4,2},{6,4},{8,14},{10,8},{12,10},{14,12},{16,22},{18,... | collective-permute-start | bytes 712712 | tf_op jit(solution)/shard_map/ppermute | solution.py:41
  95.0 7.9 %collective-permute-start.21 = (bf16[256,1152]{1,0:T(8,128)(2,1)S(1)}, bf16[256,1152]{1,0:T(8,128)(2,1)S(1)}, u32[]{:S(2)}, u32[]{:S(2)}) collective-permute-start(bf16[256,1152]{1,0:T(8,128)(2,1)S(1)} %get-tuple-element.59), channel_id=1, source_target_pairs={{0,1},{1,0},{2,3},{3,2},{4,5},{5,4},{6,7},{7,6},{8,9},{9,8},{10,11... | collective-permute-start | bytes 1769480 | tf_op jit(solution)/shard_map/ppermute | solution.py:37
  104.8 5.2 %collective-permute-start.27 = (bf16[32,3584]{1,0:T(8,128)(2,1)S(1)}, bf16[32,3584]{1,0:T(8,128)(2,1)S(1)}, u32[]{:S(2)}, u32[]{:S(2)}) collective-permute-start(bf16[32,3584]{1,0:T(8,128)(2,1)S(1)} %get-tuple-element.68), channel_id=1, source_target_pairs={{0,6},{2,0},{4,2},{6,4},{8,14},{10,8},{12,10},{14,12},{16,22},{18,... | collective-permute-start | bytes 688136 | tf_op jit(solution)/shard_map/ppermute | solution.py:41
  105.9 6.4 %collective-permute-start.23 = (bf16[32,3584]{1,0:T(8,128)(2,1)S(1)}, bf16[32,3584]{1,0:T(8,128)(2,1)S(1)}, u32[]{:S(2)}, u32[]{:S(2)}) collective-permute-start(bf16[32,3584]{1,0:T(8,128)(2,1)S(1)} %get-tuple-element.64), channel_id=1, source_target_pairs={{0,2},{2,4},{4,6},{6,0},{8,10},{10,12},{12,14},{14,8},{16,18},{18,... | collective-permute-start | bytes 688136 | tf_op jit(solution)/shard_map/ppermute | solution.py:41
  106.4 8.4 %collective-permute-start.25 = (bf16[32,3584]{1,0:T(8,128)(2,1)S(1)}, bf16[32,3584]{1,0:T(8,128)(2,1)S(1)}, u32[]{:S(2)}, u32[]{:S(2)}) collective-permute-start(bf16[32,3584]{1,0:T(8,128)(2,1)S(1)} %get-tuple-element.65), channel_id=1, source_target_pairs={{0,2},{2,4},{4,6},{6,0},{8,10},{10,12},{12,14},{14,8},{16,18},{18,... | collective-permute-start | bytes 688136 | tf_op jit(solution)/shard_map/ppermute | solution.py:41
  106.7 8.0 %collective-permute-start.26 = (bf16[32,3584]{1,0:T(8,128)(2,1)S(1)}, bf16[32,3584]{1,0:T(8,128)(2,1)S(1)}, u32[]{:S(2)}, u32[]{:S(2)}) collective-permute-start(bf16[32,3584]{1,0:T(8,128)(2,1)S(1)} %get-tuple-element.66), channel_id=1, source_target_pairs={{0,6},{2,0},{4,2},{6,4},{8,14},{10,8},{12,10},{14,12},{16,22},{18,... | collective-permute-start | bytes 688136 | tf_op jit(solution)/shard_map/ppermute | solution.py:41
  110.1 5.2 %collective-permute-start.28 = (bf16[32,3584]{1,0:T(8,128)(2,1)S(1)}, bf16[32,3584]{1,0:T(8,128)(2,1)S(1)}, u32[]{:S(2)}, u32[]{:S(2)}) collective-permute-start(bf16[32,3584]{1,0:T(8,128)(2,1)S(1)} %add_convert_fusion.2), channel_id=1, source_target_pairs={{0,6},{2,0},{4,2},{6,4},{8,14},{10,8},{12,10},{14,12},{16,22},{18,... | collective-permute-start | bytes 688136 | tf_op jit(solution)/shard_map/ppermute | solution.py:41
  112.4 6.2 %collective-permute-start.24 = (bf16[32,3584]{1,0:T(8,128)(2,1)S(1)}, bf16[32,3584]{1,0:T(8,128)(2,1)S(1)}, u32[]{:S(2)}, u32[]{:S(2)}) collective-permute-start(bf16[32,3584]{1,0:T(8,128)(2,1)S(1)} %add_convert_fusion.3), channel_id=1, source_target_pairs={{0,2},{2,4},{4,6},{6,0},{8,10},{10,12},{12,14},{14,8},{16,18},{18,... | collective-permute-start | bytes 688136 | tf_op jit(solution)/shard_map/ppermute | solution.py:41
  (7 other events, 63.2 us)

commit v2 on v1

--- a/solution.py
+++ b/solution.py
@@ -15,13 +15,13 @@
 BF16 = jnp.bfloat16
 I32 = jnp.int32
 MIB = 1 << 20
-CHUNK = 1024
+CHUNK = 512
 
 softmax_scale = 192.0 ** (-0.5)
 
 
 def device(y, z, x, c):
-    return ((y * 4 + z) * 4 + x) * 2 + c
+    return ((y * 4 + z) * 4 + x) * 2 + (c ^ ((x + z) & 1))
 
 
 RINGS = [[device(y, z, x, 0) for x in range(4)] for y in range(4) for z in range(4)] + [
@@ -59,7 +59,8 @@
 
 def coordinates():
     me = lax.axis_index("grp") * 64 + lax.axis_index("dev")
-    core, z, x = me & 1, (me >> 3) & 3, (me >> 1) & 3
+    z, x = (me >> 3) & 3, (me >> 1) & 3
+    core = (me ^ x ^ z) & 1
     return core, me >> 2, jnp.where(core == 0, x, z), jnp.where(core == 0, z, x)
 
 
@@ -68,105 +69,93 @@
 
 
 def attend_kernel(
-    lens, query, kv, w_out, sent, out_other, heads, peak, total, acc, both, held, sems
+    lens, query, cache, w_out, sent, out_other, q, kv, peak, total, acc, both, held, sems, kv_sems
 ):
-    r, j = pl.program_id(0), pl.program_id(1)
-    step = r * pl.num_programs(1) + j
     core, _, me_t, _ = coordinates()
     half = held.shape[1]
     away = pl.ds(pl.multiple_of((1 - core) * half, 128), half)
     take = pltpu.make_async_copy(w_out.at[:, away], held, sems.at[0])
     give = pltpu.make_async_copy(held, out_other, sems.at[1])
-
-    @pl.when(step == 0)
-    def _():
-        take.start()
-
-    @pl.when(step == 1)
-    def _():
-        take.wait()
-        give.start()
-
-    @pl.when(j == 0)
-    def _():
-        i = iota((128, 1), 0)
-        turned = lax.dot_general(
-            pick(i, 128), query[0], (((1,), (1,)), ((), ())), preferred_element_type=F32
-        )
-        heads[...] = turned.astype(BF16)
+    ask = pltpu.make_async_copy(query, q, sems.at[2])
+
+    def chunk(r, j):
+        slots = pl.ds(pl.multiple_of(j * CHUNK, CHUNK), CHUNK)
+        return pltpu.make_async_copy(cache.at[r, :, slots], kv.at[r, j], kv_sems.at[r, j])
+
+    live = [(lens[r] + CHUNK - 1) // CHUNK for r in range(2)]
+    ask.start()
+    for r in range(2):
+
+        @pl.loop(0, live[r])
+        def _(j, r=r):
+            chunk(r, j).start()
+
+    take.start()
+    ask.wait()
+    for r in range(2):
+        heads = lax.dot_general(
+            pick(iota((128, 1), 0), 128), q[r], (((1,), (1,)), ((), ())), preferred_element_type=F32
+        ).astype(BF16)
         peak[...] = jnp.full_like(peak, -1e30)
         total[...] = jnp.zeros_like(total)
         acc[...] = jnp.zeros_like(acc)
 
-    @pl.when(j * CHUNK < lens[r])
-    def _():
-        score = jnp.dot(heads[...], kv[0], preferred_element_type=F32)
-        place = j * CHUNK + iota(score.shape, 1)
-        score = jnp.where(place < lens[r], score * softmax_scale, -1e30)
-        before = peak[...]
-        now = jnp.maximum(before, jnp.max(score, axis=1, keepdims=True))
-        fade = jnp.exp(before - now)
-        weight = jnp.exp(score - now)
-        peak[...] = now
-        total[...] = total[...] * fade + jnp.sum(weight, axis=1, keepdims=True)
-        acc[...] = acc[...] * fade + lax.dot_general(
-            weight.astype(BF16),
-            kv[0, :LATENT, :],
-            (((1,), (1,)), ((), ())),
-            preferred_element_type=F32,
-        )
-
-    @pl.when(j == pl.num_programs(1) - 1)
-    def _():
-        both[pl.ds(pl.multiple_of(r * 128, 128), 128), :] = (acc[...] / total[...]).astype(BF16)
-
-    @pl.when(step == 2 * pl.num_programs(1) - 1)
-    def _():
-        i = iota((256, 1), 0)
-        y, b, t = i >> 6, (i >> 4) & 3, (me_t + (i >> 2)) & 3
-        z = jnp.where(core == 0, b, t)
-        x = jnp.where(core == 0, t, b)
-        head = device(y, z, x, ((i >> 1) & 1) ^ core)
-        rows = jnp.dot(pick((i & 1) * 128 + head, 256), both[...], preferred_element_type=F32)
-        sent[...] = rows.astype(BF16).reshape(sent.shape)
-        give.wait()
+        @pl.loop(0, live[r])
+        def _(j, r=r, heads=heads):
+            chunk(r, j).wait()
+            score = jnp.dot(heads, kv[r, j], preferred_element_type=F32)
+            place = j * CHUNK + iota(score.shape, 1)
+            score = jnp.where(place < lens[r], score * softmax_scale, -1e30)
+            before = peak[...]
+            now = jnp.maximum(before, jnp.max(score, axis=1, keepdims=True))
+            fade = jnp.exp(before - now)
+            weight = jnp.exp(score - now)
+            peak[...] = now
+            total[...] = total[...] * fade + jnp.sum(weight, axis=1, keepdims=True)
+            acc[...] = acc[...] * fade + lax.dot_general(
+                weight.astype(BF16),
+                kv[r, j, :LATENT, :],
+                (((1,), (1,)), ((), ())),
+                preferred_element_type=F32,
+            )
+
+        both[r * 128 : r * 128 + 128, :] = (acc[...] / total[...]).astype(BF16)
+        if r == 0:
+            take.wait()
+            give.start()
+
+    i = iota((256, 1), 0)
+    y, b, t = i >> 6, (i >> 4) & 3, (me_t + (i >> 2)) & 3
+    z = jnp.where(core == 0, b, t)
+    x = jnp.where(core == 0, t, b)
+    head = device(y, z, x, ((i >> 1) & 1) ^ core)
+    rows = jnp.dot(pick((i & 1) * 128 + head, 256), both[...], preferred_element_type=F32)
+    sent[...] = rows.astype(BF16).reshape(sent.shape)
+    give.wait()
 
 
 def attend(lengths, queries, cache, w_out):
     _, size, heads = queries.shape
     half = w_out.shape[1] // 2
     chunks = cache.shape[2] // CHUNK
-
-    def live(r, j, lens):
-        return (r, 0, jnp.minimum(j, (lens[r] - 1) // CHUNK))
-
     return pl.pallas_call(
         attend_kernel,
-        grid_spec=pltpu.PrefetchScalarGridSpec(
-            num_scalar_prefetch=1,
-            grid=(2, chunks),
-            in_specs=[
-                pl.BlockSpec((1, size, heads), lambda r, j, lens: (r, 0, 0)),
-                pl.BlockSpec((1, size, CHUNK), live),
-                HBM,
-            ],
-            out_specs=[
-                pl.BlockSpec((16, 16, LATENT), lambda r, j, lens: (0, 0, 0)),
-                HBM,
-            ],
-            scratch_shapes=[
-                pltpu.VMEM((heads, size), BF16),
-                pltpu.VMEM((heads, 1), F32),
-                pltpu.VMEM((heads, 1), F32),
-                pltpu.VMEM((heads, LATENT), F32),
-                pltpu.VMEM((2 * heads, LATENT), BF16),
-                pltpu.VMEM((VHEAD, half), BF16),
-                pltpu.SemaphoreType.DMA((2,)),
-            ],
-        ),
+        in_specs=[pl.BlockSpec(memory_space=pltpu.SMEM), HBM, HBM, HBM],
+        out_specs=[VMEM, HBM],
         out_shape=[
             pltpu.VMEM((16, 16, LATENT), BF16),
             jax.ShapeDtypeStruct((VHEAD, half), BF16),
+        ],
+        scratch_shapes=[
+            pltpu.VMEM((2, size, heads), BF16),
+            pltpu.VMEM((2, chunks, size, CHUNK), BF16),
+            pltpu.VMEM((heads, 1), F32),
+            pltpu.VMEM((heads, 1), F32),
+            pltpu.VMEM((heads, LATENT), F32),
+            pltpu.VMEM((2 * heads, LATENT), BF16),
+            pltpu.VMEM((VHEAD, half), BF16),
+            pltpu.SemaphoreType.DMA((3,)),
+            pltpu.SemaphoreType.DMA((2, chunks)),
         ],
         compiler_params=pltpu.CompilerParams(vmem_limit_bytes=56 * MIB),
         name="attend",
@@ -412,7 +401,8 @@
 
 
 def shards(queries, cache, lengths, w_uv, w_out, residual, gain, ids, gates, w_gate, w_up, w_down):
-    core = lax.axis_index(AXES) % 2
+    me = lax.axis_index(AXES)
+    core = (me ^ (me >> 1) ^ (me >> 3)) & 1
     half = residual.shape[1] // 2
 
     def own(w, axis):

time: 137 us -> 135 us (0.985); the launches traced: 137 us -> 133 us
  starting transfers between devices: 59.1 us -> 50.1 us
  waiting for transfers between devices: 36.1 us -> 42.4 us
    ppermute x9, starting transfers between devices: 22.2 us -> 9.82 us  [swap(): return lax.ppermute(a, AXES, SIBLING)]
    all_to_all x3, waiting for transfers between devices: 12.5 us -> 17.5 us  [plane(): return lax.all_to_all(a, AXES, 0, 0, axis_index_groups=PLANES, tiled=True)]
    ppermute x21, starting transfers between devices: 23 us -> 25.9 us  [ahead(): lax.ppermute(a, AXES, [(r[i], r[(i + step) % 4]) for r in RINGS for i in...]
  transfers between devices with their start and end apart: 33 -> 33, of which waited for: 19 -> 20; matrix products, arithmetic and copies ran while one was open for 2% -> 2% of each run, Pallas kernels for 10% -> 10%
where the time goes in v2:
time: 135 us; the launch traced here: 133 us
  starting transfers between devices  50.1 us (37%)
  waiting for transfers between devices  42.4 us (31%)
  Pallas kernels  23.4 us (17%)
  blocking collectives  12.1 us (9%)
  local copies, waits for them, and re-layouts  3.15 us (2%)
  other arithmetic  1.81 us (1%)
    ppermute x21, starting transfers between devices, ahead(): lax.ppermute(a, AXES, [(r[i], r[(i + step) % 4]) for r in RINGS for i in...  25.9 us
    ppermute x21, waiting for transfers between devices, ahead(): lax.ppermute(a, AXES, [(r[i], r[(i + step) % 4]) for r in RINGS for i in...  23.5 us
    all_to_all x3, waiting for transfers between devices, plane(): return lax.all_to_all(a, AXES, 0, 0, axis_index_groups=PLANES, tiled=True)  17.5 us
    all_to_all x3, starting transfers between devices, plane(): return lax.all_to_all(a, AXES, 0, 0, axis_index_groups=PLANES, tiled=True)  14.5 us
    all_to_all x1, blocking collectives, plane(): return lax.all_to_all(a, AXES, 0, 0, axis_index_groups=PLANES, tiled=True)  12.1 us
    ppermute x9, starting transfers between devices, swap(): return lax.ppermute(a, AXES, SIBLING)  9.82 us
    pallas_call x1, Pallas kernels, attend(): pl.pallas_call(attend_kernel, in_specs=[pl.BlockSpec(memory_space=pltpu.S...  7.06 us
    pallas_call x5, Pallas kernels, call(): pl.pallas_call(kernel, in_specs=[VMEM] * len(args), out_specs=[VMEM] * le...  6.59 us
  transfers between devices with their start and end apart: 33, of which 20 were waited for; matrix products, arithmetic and copies ran while one was open for 2% of the time, Pallas kernels for 10%

profile of v2, /device:TPU:1, one launch (start us, length us, event | category | flops | bytes accessed | tf_op | source)
XLA Modules:
  0.0 133.3 jit_solution(3164083236191675663)
XLA Ops:
  0.0 7.1 %attend.1 = (bf16[16,16,512]{2,1,0:T(8,128)(2,1)}, bf16[128,3584]{1,0:T(8,128)(2,1)}) custom-call(s32[2]{0:T(128)} %lens.1, bf16[2,576,128]{2,1,0:T(8,128)(2,1)} %bitcast.33, bf16[2,576,2048]{2,1,0:T(8,128)(2,1)} %bitcast.27, bf16[128,7168]{1,0:T(8,128)(2,1)} %refs_0_.1), custom_call_target="tpu_custom_call" | custom-call | tf_op jit(solution)/shard_map/attend/pallas_call | solution.py:141
  8.3 7.3 %all-to-all-start = ((bf16[16,16,512]{2,1,0:T(8,128)(2,1)}), bf16[16,16,512]{2,1,0:T(8,128)(2,1)S(1)}, u32[]{:S(2)}, u32[]{:S(2)}) async-start(bf16[16,16,512]{2,1,0:T(8,128)(2,1)} %get-tuple-element.37), calls=%async_computation | async-start | bytes 524288 | tf_op jit(solution)/shard_map/all_to_all | solution.py:45
  16.5 4.4 %pack.1 = (bf16[3584,256]{1,0:T(8,128)(2,1)}, bf16[3584,256]{1,0:T(8,128)(2,1)}, bf16[256,3584]{1,0:T(8,128)(2,1)}, f32[8,128]{1,0:T(8,128)S(1)}) custom-call(bf16[7168,256]{1,0:T(8,128)(2,1)} %bitcast.23, bf16[7168,256]{1,0:T(8,128)(2,1)} %bitcast.25, bf16[256,7168]{1,0:T(8,128)(2,1)} %bitcast.21, bf16[128,3584]{1,0:T(8,128)(2,1)} %get-tuple-element.38.after), custom_call_target="tpu_custom_call" | custom-call | bytes 12582912 | tf_op jit(solution)/shard_map/pack/pallas_call | solution.py:219
  20.9 2.5 %all-to-all-done.got = bf16[16,16,512]{2,1,0:T(8,128)(2,1)S(1)} async-done(((bf16[16,16,512]{2,1,0:T(8,128)(2,1)}), bf16[16,16,512]{2,1,0:T(8,128)(2,1)S(1)}, u32[]{:S(2)}, u32[]{:S(2)}) %all-to-all-start) | async-done | bytes 262176 | tf_op jit(solution)/shard_map/all_to_all | solution.py:45
  23.6 3.4 %collective-permute-start.1 = (bf16[64,512]{1,0:T(8,128)(2,1)S(1)}, bf16[64,512]{1,0:T(8,128)(2,1)S(1)}, u32[]{:S(2)}, u32[]{:S(2)}) collective-permute-start(bf16[64,512]{1,0:T(8,128)(2,1)S(1)} %get-tuple-element.41), channel_id=1, source_target_pairs={{0,7},{3,0},{4,3},{7,4},{9,14},{10,9},{13,10},{14,13},{16,23},{19,... | collective-permute-start | bytes 196616 | tf_op jit(solution)/shard_map/ppermute | solution.py:41
  28.4 3.3 %collective-permute-done.2.p2 = bf16[64,512]{1,0:T(8,128)(2,1)S(1)} collective-permute-done((bf16[64,512]{1,0:T(8,128)(2,1)S(1)}, bf16[64,512]{1,0:T(8,128)(2,1)S(1)}, u32[]{:S(2)}, u32[]{:S(2)}) %collective-permute-start.2) | collective-permute-done | bytes 65568 | tf_op jit(solution)/shard_map/ppermute | solution.py:41
  37.9 2.1 %collective-permute-start.10 = (bf16[32,3584]{1,0:T(8,128)(2,1)S(1)}, bf16[32,3584]{1,0:T(8,128)(2,1)S(1)}, u32[]{:S(2)}, u32[]{:S(2)}) collective-permute-start(bf16[32,3584]{1,0:T(8,128)(2,1)S(1)} %get-tuple-element.48), channel_id=1, source_target_pairs={{0,7},{3,0},{4,3},{7,4},{9,14},{10,9},{13,10},{14,13},{16,23},{19,... | collective-permute-start | bytes 688136 | tf_op jit(solution)/shard_map/ppermute | solution.py:41
  40.0 1.9 %collective-permute-done.11 = bf16[32,3584]{1,0:T(8,128)(2,1)S(1)} collective-permute-done((bf16[32,3584]{1,0:T(8,128)(2,1)S(1)}, bf16[32,3584]{1,0:T(8,128)(2,1)S(1)}, u32[]{:S(2)}, u32[]{:S(2)}) %collective-permute-start.11) | collective-permute-done | bytes 229408 | tf_op jit(solution)/shard_map/ppermute | solution.py:41
  41.9 1.9 %collective-permute-start.12 = (bf16[32,3584]{1,0:T(8,128)(2,1)S(1)}, bf16[32,3584]{1,0:T(8,128)(2,1)S(1)}, u32[]{:S(2)}, u32[]{:S(2)}) collective-permute-start(bf16[32,3584]{1,0:T(8,128)(2,1)S(1)} %add_convert_fusion.4), channel_id=1, source_target_pairs={{0,7},{3,0},{4,3},{7,4},{9,14},{10,9},{13,10},{14,13},{16,23},{19,... | collective-permute-start | bytes 688136 | tf_op jit(solution)/shard_map/ppermute | solution.py:41
  44.3 2.3 %collective-permute-done.9 = bf16[32,3584]{1,0:T(8,128)(2,1)S(1)} collective-permute-done((bf16[32,3584]{1,0:T(8,128)(2,1)S(1)}, bf16[32,3584]{1,0:T(8,128)(2,1)S(1)}, u32[]{:S(2)}, u32[]{:S(2)}) %collective-permute-start.9) | collective-permute-done | bytes 229408 | tf_op jit(solution)/shard_map/ppermute | solution.py:41
  47.7 3.0 %collective-permute-done.8 = bf16[32,3584]{1,0:T(8,128)(2,1)S(1)} collective-permute-done((bf16[32,3584]{1,0:T(8,128)(2,1)S(1)}, bf16[32,3584]{1,0:T(8,128)(2,1)S(1)}, u32[]{:S(2)}, u32[]{:S(2)}) %collective-permute-start.8) | collective-permute-done | bytes 229408 | tf_op jit(solution)/shard_map/ppermute | solution.py:41
  52.1 3.6 %all-to-all-start.1 = ((bf16[16,4,3584]{2,1,0:T(4,128)(2,1)}), bf16[16,4,3584]{2,1,0:T(4,128)(2,1)S(1)}, u32[]{:S(2)}, u32[]{:S(2)}) async-start(bf16[16,4,3584]{2,1,0:T(4,128)(2,1)} %bitcast.17), calls=%async_computation.1 | async-start | bytes 917504 | tf_op jit(solution)/shard_map/all_to_all | solution.py:45
  56.7 7.8 %all-to-all-done.1 = bf16[16,4,3584]{2,1,0:T(4,128)(2,1)S(1)} async-done(((bf16[16,4,3584]{2,1,0:T(4,128)(2,1)}), bf16[16,4,3584]{2,1,0:T(4,128)(2,1)S(1)}, u32[]{:S(2)}, u32[]{:S(2)}) %all-to-all-start.1) | async-done | bytes 458784 | tf_op jit(solution)/shard_map/all_to_all | solution.py:45
  65.7 3.6 %all-to-all-start.2 = ((bf16[16,4,3712]{2,1,0:T(4,128)(2,1)}), bf16[16,4,3712]{2,1,0:T(4,128)(2,1)S(1)}, u32[]{:S(2)}, u32[]{:S(2)}) async-start(bf16[16,4,3712]{2,1,0:T(4,128)(2,1)} %broadcast_in_dim.8), calls=%async_computation.2 | async-start | bytes 950272 | tf_op jit(solution)/shard_map/all_to_all | solution.py:45
  69.3 1.6 %collective-permute-start.22 = (bf16[256,3584]{1,0:T(8,128)(2,1)}, bf16[256,3584]{1,0:T(8,128)(2,1)}, u32[]{:S(2)}, u32[]{:S(2)}) collective-permute-start(bf16[256,3584]{1,0:T(8,128)(2,1)} %get-tuple-element.61), channel_id=1, source_target_pairs={{0,1},{1,0},{2,3},{3,2},{4,5},{5,4},{6,7},{7,6},{8,9},{9,8},{10,11... | collective-permute-start | bytes 5505032 | tf_op jit(solution)/shard_map/ppermute | solution.py:37
  70.9 7.2 %all-to-all-done.2 = bf16[16,4,3712]{2,1,0:T(4,128)(2,1)S(1)} async-done(((bf16[16,4,3712]{2,1,0:T(4,128)(2,1)}), bf16[16,4,3712]{2,1,0:T(4,128)(2,1)S(1)}, u32[]{:S(2)}, u32[]{:S(2)}) %all-to-all-start.2) | async-done | bytes 475168 | tf_op jit(solution)/shard_map/all_to_all | solution.py:45
  79.6 1.9 %collective-permute-start.14 = (bf16[32,3712]{1,0:T(8,128)(2,1)S(1)}, bf16[32,3712]{1,0:T(8,128)(2,1)S(1)}, u32[]{:S(2)}, u32[]{:S(2)}) collective-permute-start(bf16[32,3712]{1,0:T(8,128)(2,1)S(1)} %bitcast.34), channel_id=1, source_target_pairs={{0,7},{3,0},{4,3},{7,4},{9,14},{10,9},{13,10},{14,13},{16,23},{19,... | collective-permute-start | bytes 712712 | tf_op jit(solution)/shard_map/ppermute | solution.py:41
  83.3 2.3 %collective-permute-done.15.refs_3_ = bf16[32,3712]{1,0:T(8,128)(2,1)S(1)} collective-permute-done((bf16[32,3712]{1,0:T(8,128)(2,1)S(1)}, bf16[32,3712]{1,0:T(8,128)(2,1)S(1)}, u32[]{:S(2)}, u32[]{:S(2)}) %collective-permute-start.15) | collective-permute-done | bytes 237600 | tf_op jit(solution)/shard_map/ppermute | solution.py:41
  85.6 3.0 %collective-permute-start.20 = (bf16[32,3712]{1,0:T(8,128)(2,1)S(1)}, bf16[32,3712]{1,0:T(8,128)(2,1)S(1)}, u32[]{:S(2)}, u32[]{:S(2)}) collective-permute-start(bf16[32,3712]{1,0:T(8,128)(2,1)S(1)} %collective-permute-done.14.refs_2_), channel_id=1, source_target_pairs={{0,7},{3,0},{4,3},{7,4},{9,14},{10,9},{13,10},{14,13},{16,23},{19,... | collective-permute-start | bytes 712712 | tf_op jit(solution)/shard_map/ppermute | solution.py:41
  88.6 2.7 %load_gate_up.1.refs_6_.refs_7_ = bf16[3584,1024]{1,0:T(8,128)(2,1)S(1)} custom-call(bf16[7168,256]{1,0:T(8,128)(2,1)} %bitcast.24, bf16[7168,256]{1,0:T(8,128)(2,1)} %bitcast.26, bf16[3584,256]{1,0:T(8,128)(2,1)S(1)} %collective-permute-done.17.refs_2_, bf16[3584,256]{1,0:T(8,128)(2,1)} %collective-permute-done.18.refs_3_), custom_call_target="tpu_custom_call" | custom-call | bytes 14680064 | tf_op jit(solution)/shard_map/load_gate_up/pallas_call | solution.py:185
  91.4 2.1 %gate_up.2 = (f32[192,1024]{1,0:T(8,128)S(1)}, bf16[192,1152]{1,0:T(8,128)(2,1)S(1)}, f32[192,1]{1,0:T(8,128)S(1)}, f32[192,1]{1,0:T(8,128)S(1)}) custom-call(bf16[64,3712]{1,0:T(8,128)(2,1)S(1)} %bitcast.18, bf16[32,3712]{1,0:T(8,128)(2,1)S(1)} %collective-permute-done.13.refs_1_, bf16[32,3712]{1,0:T(8,128)(2,1)S(1)} %collective-permute-done.14.refs_2_, ...), custom_call_target="tpu_custom_call" | custom-call | flops 1610612736 | bytes 1048576 | tf_op jit(solution)/shard_map/gate_up/pallas_call | solution.py:234
  93.5 1.6 %gate_up.3 = (f32[256,1024]{1,0:T(8,128)S(1)}, bf16[256,1152]{1,0:T(8,128)(2,1)S(1)}, f32[256,1]{1,0:T(8,128)S(1)}, f32[256,1]{1,0:T(8,128)S(1)}) custom-call(f32[192,1024]{1,0:T(8,128)S(1)} %get-tuple-element.53.refs_0_, bf16[192,1152]{1,0:T(8,128)(2,1)S(1)} %get-tuple-element.54.refs_1_, f32[192,1]{1,0:T(8,128)S(1)} %get-tuple-element.55.refs_2_, ...), custom_call_target="tpu_custom_call" | custom-call | flops 536870912 | bytes 1048576 | tf_op jit(solution)/shard_map/gate_up/pallas_call | solution.py:234
  95.1 2.6 %collective-permute-start.21 = (bf16[256,1152]{1,0:T(8,128)(2,1)S(1)}, bf16[256,1152]{1,0:T(8,128)(2,1)S(1)}, u32[]{:S(2)}, u32[]{:S(2)}) collective-permute-start(bf16[256,1152]{1,0:T(8,128)(2,1)S(1)} %get-tuple-element.59), channel_id=1, source_target_pairs={{0,1},{1,0},{2,3},{3,2},{4,5},{5,4},{6,7},{7,6},{8,9},{9,8},{10,11... | collective-permute-start | bytes 1769480 | tf_op jit(solution)/shard_map/ppermute | solution.py:37
  97.7 2.1 %load_down.1.w = bf16[512,3584]{1,0:T(8,128)(2,1)S(1)} custom-call(bf16[256,7168]{1,0:T(8,128)(2,1)} %bitcast.22, bf16[256,3584]{1,0:T(8,128)(2,1)} %collective-permute-done.22.refs_1_), custom_call_target="tpu_custom_call" | custom-call | bytes 7340032 | tf_op jit(solution)/shard_map/load_down/pallas_call | solution.py:185
  99.8 1.9 %down.1 = (bf16[64,3584]{1,0:T(8,128)(2,1)S(1)}, bf16[32,3584]{1,0:T(8,128)(2,1)S(1)}, bf16[32,3584]{1,0:T(8,128)(2,1)S(1)}, bf16[32,3584]{1,0:T(8,128)(2,1)S(1)...) custom-call(f32[256,1024]{1,0:T(8,128)S(1)} %get-tuple-element.57.part, ...), custom_call_target="tpu_custom_call" | custom-call | flops 1073741824 | bytes 1048576 | tf_op jit(solution)/shard_map/down/pallas_call | solution.py:234
  101.7 1.9 %collective-permute-start.27 = (bf16[32,3584]{1,0:T(8,128)(2,1)S(1)}, bf16[32,3584]{1,0:T(8,128)(2,1)S(1)}, u32[]{:S(2)}, u32[]{:S(2)}) collective-permute-start(bf16[32,3584]{1,0:T(8,128)(2,1)S(1)} %get-tuple-element.68), channel_id=1, source_target_pairs={{0,7},{3,0},{4,3},{7,4},{9,14},{10,9},{13,10},{14,13},{16,23},{19,... | collective-permute-start | bytes 688136 | tf_op jit(solution)/shard_map/ppermute | solution.py:41
  103.6 3.0 %collective-permute-start.26 = (bf16[32,3584]{1,0:T(8,128)(2,1)S(1)}, bf16[32,3584]{1,0:T(8,128)(2,1)S(1)}, u32[]{:S(2)}, u32[]{:S(2)}) collective-permute-start(bf16[32,3584]{1,0:T(8,128)(2,1)S(1)} %get-tuple-element.66), channel_id=1, source_target_pairs={{0,7},{3,0},{4,3},{7,4},{9,14},{10,9},{13,10},{14,13},{16,23},{19,... | collective-permute-start | bytes 688136 | tf_op jit(solution)/shard_map/ppermute | solution.py:41
  107.6 2.9 %collective-permute-start.28 = (bf16[32,3584]{1,0:T(8,128)(2,1)S(1)}, bf16[32,3584]{1,0:T(8,128)(2,1)S(1)}, u32[]{:S(2)}, u32[]{:S(2)}) collective-permute-start(bf16[32,3584]{1,0:T(8,128)(2,1)S(1)} %add_convert_fusion.2), channel_id=1, source_target_pairs={{0,7},{3,0},{4,3},{7,4},{9,14},{10,9},{13,10},{14,13},{16,23},{19,... | collective-permute-start | bytes 688136 | tf_op jit(solution)/shard_map/ppermute | solution.py:41
  110.7 2.0 %collective-permute-done.25 = bf16[32,3584]{1,0:T(8,128)(2,1)S(1)} collective-permute-done((bf16[32,3584]{1,0:T(8,128)(2,1)S(1)}, bf16[32,3584]{1,0:T(8,128)(2,1)S(1)}, u32[]{:S(2)}, u32[]{:S(2)}) %collective-permute-start.25) | collective-permute-done | bytes 229408 | tf_op jit(solution)/shard_map/ppermute | solution.py:41
  113.4 4.0 %collective-permute-done.24 = bf16[32,3584]{1,0:T(8,128)(2,1)S(1)} collective-permute-done((bf16[32,3584]{1,0:T(8,128)(2,1)S(1)}, bf16[32,3584]{1,0:T(8,128)(2,1)S(1)}, u32[]{:S(2)}, u32[]{:S(2)}) %collective-permute-start.24) | collective-permute-done | bytes 229408 | tf_op jit(solution)/shard_map/ppermute | solution.py:41
  117.9 12.1 %all_to_all.20 = bf16[16,4,3584]{2,1,0:T(4,128)(2,1)S(1)} all-to-all(bf16[16,4,3584]{2,1,0:T(4,128)(2,1)S(1)} %bitcast.32), channel_id=1, replica_groups={{0,9,16,25,32,41,48,57,64,73,80,89,96,105,112,121},{3,10,19,26,35,42,51..., dimensions={0} | all-to-all | bytes 917504 | tf_op jit(solution)/shard_map/all_to_all | solution.py:45
  130.2 1.6 %collective-permute-start.29 = (bf16[2,3584]{1,0:T(2,128)(2,1)S(1)}, bf16[2,3584]{1,0:T(2,128)(2,1)S(1)}, u32[]{:S(2)}, u32[]{:S(2)}) collective-permute-start(bf16[2,3584]{1,0:T(2,128)(2,1)S(1)} %get-tuple-element.76), channel_id=1, source_target_pairs={{0,1},{1,0},{2,3},{3,2},{4,5},{5,4},{6,7},{7,6},{8,9},{9,8},{10,11... | collective-permute-start | bytes 43016 | tf_op jit(solution)/shard_map/ppermute | solution.py:37
  (86 shorter events, 22.4 us)
Async XLA Ops:
  7.1 27.2 %collective-permute-start.6 = (bf16[128,3584]{1,0:T(8,128)(2,1)}, bf16[128,3584]{1,0:T(8,128)(2,1)S(1)}, u32[]{:S(2)}, u32[]{:S(2)}) collective-permute-start(bf16[128,3584]{1,0:T(8,128)(2,1)} %get-tuple-element.38.after), channel_id=1, source_target_pairs={{0,1},{1,0},{2,3},{3,2},{4,5},{5,4},{6,7},{7,6},{8,9},{9,8},{10,11... | collective-permute-start | bytes 2752520 | tf_op jit(solution)/shard_map/ppermute | solution.py:37
  8.3 15.1 %all-to-all-start = ((bf16[16,16,512]{2,1,0:T(8,128)(2,1)}), bf16[16,16,512]{2,1,0:T(8,128)(2,1)S(1)}, u32[]{:S(2)}, u32[]{:S(2)}) async-start(bf16[16,16,512]{2,1,0:T(8,128)(2,1)} %get-tuple-element.37), calls=%async_computation | async-start | bytes 524288 | tf_op jit(solution)/shard_map/all_to_all | solution.py:45
  15.7 12.3 %collective-permute-start.4 = (bf16[512,128]{1,0:T(8,128)(2,1)S(1)}, bf16[512,128]{1,0:T(8,128)(2,1)S(1)}, u32[]{:S(2)}, u32[]{:S(2)}) collective-permute-start(bf16[512,128]{1,0:T(8,128)(2,1)S(1)} %bitcast.19), channel_id=1, source_target_pairs={{0,1},{1,0},{2,3},{3,2},{4,5},{5,4},{6,7},{7,6},{8,9},{9,8},{10,11... | collective-permute-start | bytes 393224 | tf_op jit(solution)/shard_map/ppermute | solution.py:37
  23.6 4.8 %collective-permute-start.1 = (bf16[64,512]{1,0:T(8,128)(2,1)S(1)}, bf16[64,512]{1,0:T(8,128)(2,1)S(1)}, u32[]{:S(2)}, u32[]{:S(2)}) collective-permute-start(bf16[64,512]{1,0:T(8,128)(2,1)S(1)} %get-tuple-element.41), channel_id=1, source_target_pairs={{0,7},{3,0},{4,3},{7,4},{9,14},{10,9},{13,10},{14,13},{16,23},{19,... | collective-permute-start | bytes 196616 | tf_op jit(solution)/shard_map/ppermute | solution.py:41
  27.1 4.6 %collective-permute-start.2 = (bf16[64,512]{1,0:T(8,128)(2,1)S(1)}, bf16[64,512]{1,0:T(8,128)(2,1)S(1)}, u32[]{:S(2)}, u32[]{:S(2)}) collective-permute-start(bf16[64,512]{1,0:T(8,128)(2,1)S(1)} %get-tuple-element.42), channel_id=1, source_target_pairs={{0,4},{3,7},{4,0},{7,3},{9,13},{10,14},{13,9},{14,10},{16,20},{19,... | collective-permute-start | bytes 196616 | tf_op jit(solution)/shard_map/ppermute | solution.py:41
  27.6 5.2 %collective-permute-start.3 = (bf16[64,512]{1,0:T(8,128)(2,1)S(1)}, bf16[64,512]{1,0:T(8,128)(2,1)S(1)}, u32[]{:S(2)}, u32[]{:S(2)}) collective-permute-start(bf16[64,512]{1,0:T(8,128)(2,1)S(1)} %get-tuple-element.43), channel_id=1, source_target_pairs={{0,3},{3,4},{4,7},{7,0},{9,10},{10,13},{13,14},{14,9},{16,19},{19,... | collective-permute-start | bytes 196616 | tf_op jit(solution)/shard_map/ppermute | solution.py:41
  36.0 5.8 %collective-permute-start.11 = (bf16[32,3584]{1,0:T(8,128)(2,1)S(1)}, bf16[32,3584]{1,0:T(8,128)(2,1)S(1)}, u32[]{:S(2)}, u32[]{:S(2)}) collective-permute-start(bf16[32,3584]{1,0:T(8,128)(2,1)S(1)} %get-tuple-element.50), channel_id=1, source_target_pairs={{0,7},{3,0},{4,3},{7,4},{9,14},{10,9},{13,10},{14,13},{16,23},{19,... | collective-permute-start | bytes 688136 | tf_op jit(solution)/shard_map/ppermute | solution.py:41
  37.0 7.0 %collective-permute-start.7 = (bf16[32,3584]{1,0:T(8,128)(2,1)S(1)}, bf16[32,3584]{1,0:T(8,128)(2,1)S(1)}, u32[]{:S(2)}, u32[]{:S(2)}) collective-permute-start(bf16[32,3584]{1,0:T(8,128)(2,1)S(1)} %get-tuple-element.46), channel_id=1, source_target_pairs={{0,3},{3,4},{4,7},{7,0},{9,10},{10,13},{13,14},{14,9},{16,19},{19,... | collective-permute-start | bytes 688136 | tf_op jit(solution)/shard_map/ppermute | solution.py:41
  37.9 6.5 %collective-permute-start.10 = (bf16[32,3584]{1,0:T(8,128)(2,1)S(1)}, bf16[32,3584]{1,0:T(8,128)(2,1)S(1)}, u32[]{:S(2)}, u32[]{:S(2)}) collective-permute-start(bf16[32,3584]{1,0:T(8,128)(2,1)S(1)} %get-tuple-element.48), channel_id=1, source_target_pairs={{0,7},{3,0},{4,3},{7,4},{9,14},{10,9},{13,10},{14,13},{16,23},{19,... | collective-permute-start | bytes 688136 | tf_op jit(solution)/shard_map/ppermute | solution.py:41
  40.0 6.7 %collective-permute-start.9 = (bf16[32,3584]{1,0:T(8,128)(2,1)S(1)}, bf16[32,3584]{1,0:T(8,128)(2,1)S(1)}, u32[]{:S(2)}, u32[]{:S(2)}) collective-permute-start(bf16[32,3584]{1,0:T(8,128)(2,1)S(1)} %get-tuple-element.47), channel_id=1, source_target_pairs={{0,3},{3,4},{4,7},{7,0},{9,10},{10,13},{13,14},{14,9},{16,19},{19,... | collective-permute-start | bytes 688136 | tf_op jit(solution)/shard_map/ppermute | solution.py:41
  41.9 5.8 %collective-permute-start.12 = (bf16[32,3584]{1,0:T(8,128)(2,1)S(1)}, bf16[32,3584]{1,0:T(8,128)(2,1)S(1)}, u32[]{:S(2)}, u32[]{:S(2)}) collective-permute-start(bf16[32,3584]{1,0:T(8,128)(2,1)S(1)} %add_convert_fusion.4), channel_id=1, source_target_pairs={{0,7},{3,0},{4,3},{7,4},{9,14},{10,9},{13,10},{14,13},{16,23},{19,... | collective-permute-start | bytes 688136 | tf_op jit(solution)/shard_map/ppermute | solution.py:41
  44.0 6.7 %collective-permute-start.8 = (bf16[32,3584]{1,0:T(8,128)(2,1)S(1)}, bf16[32,3584]{1,0:T(8,128)(2,1)S(1)}, u32[]{:S(2)}, u32[]{:S(2)}) collective-permute-start(bf16[32,3584]{1,0:T(8,128)(2,1)S(1)} %add_convert_fusion.5), channel_id=1, source_target_pairs={{0,3},{3,4},{4,7},{7,0},{9,10},{10,13},{13,14},{14,9},{16,19},{19,... | collective-permute-start | bytes 688136 | tf_op jit(solution)/shard_map/ppermute | solution.py:41
  52.1 12.4 %all-to-all-start.1 = ((bf16[16,4,3584]{2,1,0:T(4,128)(2,1)}), bf16[16,4,3584]{2,1,0:T(4,128)(2,1)S(1)}, u32[]{:S(2)}, u32[]{:S(2)}) async-start(bf16[16,4,3584]{2,1,0:T(4,128)(2,1)} %bitcast.17), calls=%async_computation.1 | async-start | bytes 917504 | tf_op jit(solution)/shard_map/all_to_all | solution.py:45
  55.9 8.9 %collective-permute-start = (bf16[2,3712]{1,0:T(2,128)(2,1)S(1)}, bf16[2,3712]{1,0:T(2,128)(2,1)S(1)}, u32[]{:S(2)}, u32[]{:S(2)}) collective-permute-start(bf16[2,3712]{1,0:T(2,128)(2,1)S(1)} %concatenate.34), channel_id=1, source_target_pairs={{0,1},{1,0},{2,3},{3,2},{4,5},{5,4},{6,7},{7,6},{8,9},{9,8},{10,11... | collective-permute-start | bytes 44552 | tf_op jit(solution)/shard_map/ppermute | solution.py:37
  55.9 25.6 %collective-permute-start.17 = (bf16[3584,256]{1,0:T(8,128)(2,1)}, bf16[3584,256]{1,0:T(8,128)(2,1)S(1)}, u32[]{:S(2)}, u32[]{:S(2)}) collective-permute-start(bf16[3584,256]{1,0:T(8,128)(2,1)} %get-tuple-element.51), channel_id=1, source_target_pairs={{0,1},{1,0},{2,3},{3,2},{4,5},{5,4},{6,7},{7,6},{8,9},{9,8},{10,11... | collective-permute-start | bytes 5505032 | tf_op jit(solution)/shard_map/ppermute | solution.py:37
  56.4 26.2 %collective-permute-start.18 = (bf16[3584,256]{1,0:T(8,128)(2,1)}, bf16[3584,256]{1,0:T(8,128)(2,1)}, u32[]{:S(2)}, u32[]{:S(2)}) collective-permute-start(bf16[3584,256]{1,0:T(8,128)(2,1)} %get-tuple-element.52), channel_id=1, source_target_pairs={{0,1},{1,0},{2,3},{3,2},{4,5},{5,4},{6,7},{7,6},{8,9},{9,8},{10,11... | collective-permute-start | bytes 5505032 | tf_op jit(solution)/shard_map/ppermute | solution.py:37
  65.7 12.4 %all-to-all-start.2 = ((bf16[16,4,3712]{2,1,0:T(4,128)(2,1)}), bf16[16,4,3712]{2,1,0:T(4,128)(2,1)S(1)}, u32[]{:S(2)}, u32[]{:S(2)}) async-start(bf16[16,4,3712]{2,1,0:T(4,128)(2,1)} %broadcast_in_dim.8), calls=%async_computation.2 | async-start | bytes 950272 | tf_op jit(solution)/shard_map/all_to_all | solution.py:45
  69.3 28.4 %collective-permute-start.22 = (bf16[256,3584]{1,0:T(8,128)(2,1)}, bf16[256,3584]{1,0:T(8,128)(2,1)}, u32[]{:S(2)}, u32[]{:S(2)}) collective-permute-start(bf16[256,3584]{1,0:T(8,128)(2,1)} %get-tuple-element.61), channel_id=1, source_target_pairs={{0,1},{1,0},{2,3},{3,2},{4,5},{5,4},{6,7},{7,6},{8,9},{9,8},{10,11... | collective-permute-start | bytes 5505032 | tf_op jit(solution)/shard_map/ppermute | solution.py:37
  78.5 7.1 %collective-permute-start.15 = (bf16[32,3712]{1,0:T(8,128)(2,1)S(1)}, bf16[32,3712]{1,0:T(8,128)(2,1)S(1)}, u32[]{:S(2)}, u32[]{:S(2)}) collective-permute-start(bf16[32,3712]{1,0:T(8,128)(2,1)S(1)} %bitcast.36), channel_id=1, source_target_pairs={{0,3},{3,4},{4,7},{7,0},{9,10},{10,13},{13,14},{14,9},{16,19},{19,... | collective-permute-start | bytes 712712 | tf_op jit(solution)/shard_map/ppermute | solution.py:41
  79.6 6.0 %collective-permute-start.14 = (bf16[32,3712]{1,0:T(8,128)(2,1)S(1)}, bf16[32,3712]{1,0:T(8,128)(2,1)S(1)}, u32[]{:S(2)}, u32[]{:S(2)}) collective-permute-start(bf16[32,3712]{1,0:T(8,128)(2,1)S(1)} %bitcast.34), channel_id=1, source_target_pairs={{0,7},{3,0},{4,3},{7,4},{9,14},{10,9},{13,10},{14,13},{16,23},{19,... | collective-permute-start | bytes 712712 | tf_op jit(solution)/shard_map/ppermute | solution.py:41
  81.5 9.8 %collective-permute-start.13 = (bf16[32,3712]{1,0:T(8,128)(2,1)S(1)}, bf16[32,3712]{1,0:T(8,128)(2,1)S(1)}, u32[]{:S(2)}, u32[]{:S(2)}) collective-permute-start(bf16[32,3712]{1,0:T(8,128)(2,1)S(1)} %bitcast.37), channel_id=1, source_target_pairs={{0,7},{3,0},{4,3},{7,4},{9,14},{10,9},{13,10},{14,13},{16,23},{19,... | collective-permute-start | bytes 712712 | tf_op jit(solution)/shard_map/ppermute | solution.py:41
  82.6 8.8 %collective-permute-start.16 = (bf16[32,3712]{1,0:T(8,128)(2,1)S(1)}, bf16[32,3712]{1,0:T(8,128)(2,1)S(1)}, u32[]{:S(2)}, u32[]{:S(2)}) collective-permute-start(bf16[32,3712]{1,0:T(8,128)(2,1)S(1)} %bitcast.35), channel_id=1, source_target_pairs={{0,3},{3,4},{4,7},{7,0},{9,10},{10,13},{13,14},{14,9},{16,19},{19,... | collective-permute-start | bytes 712712 | tf_op jit(solution)/shard_map/ppermute | solution.py:41
  85.6 7.9 %collective-permute-start.19 = (bf16[32,3712]{1,0:T(8,128)(2,1)S(1)}, bf16[32,3712]{1,0:T(8,128)(2,1)S(1)}, u32[]{:S(2)}, u32[]{:S(2)}) collective-permute-start(bf16[32,3712]{1,0:T(8,128)(2,1)S(1)} %collective-permute-done.15.refs_3_), channel_id=1, source_target_pairs={{0,3},{3,4},{4,7},{7,0},{9,10},{10,13},{13,14},{14,9},{16,19},{19,... | collective-permute-start | bytes 712712 | tf_op jit(solution)/shard_map/ppermute | solution.py:41
  85.6 7.9 %collective-permute-start.20 = (bf16[32,3712]{1,0:T(8,128)(2,1)S(1)}, bf16[32,3712]{1,0:T(8,128)(2,1)S(1)}, u32[]{:S(2)}, u32[]{:S(2)}) collective-permute-start(bf16[32,3712]{1,0:T(8,128)(2,1)S(1)} %collective-permute-done.14.refs_2_), channel_id=1, source_target_pairs={{0,7},{3,0},{4,3},{7,4},{9,14},{10,9},{13,10},{14,13},{16,23},{19,... | collective-permute-start | bytes 712712 | tf_op jit(solution)/shard_map/ppermute | solution.py:41
  95.1 4.7 %collective-permute-start.21 = (bf16[256,1152]{1,0:T(8,128)(2,1)S(1)}, bf16[256,1152]{1,0:T(8,128)(2,1)S(1)}, u32[]{:S(2)}, u32[]{:S(2)}) collective-permute-start(bf16[256,1152]{1,0:T(8,128)(2,1)S(1)} %get-tuple-element.59), channel_id=1, source_target_pairs={{0,1},{1,0},{2,3},{3,2},{4,5},{5,4},{6,7},{7,6},{8,9},{9,8},{10,11... | collective-permute-start | bytes 1769480 | tf_op jit(solution)/shard_map/ppermute | solution.py:37
  101.7 5.8 %collective-permute-start.27 = (bf16[32,3584]{1,0:T(8,128)(2,1)S(1)}, bf16[32,3584]{1,0:T(8,128)(2,1)S(1)}, u32[]{:S(2)}, u32[]{:S(2)}) collective-permute-start(bf16[32,3584]{1,0:T(8,128)(2,1)S(1)} %get-tuple-element.68), channel_id=1, source_target_pairs={{0,7},{3,0},{4,3},{7,4},{9,14},{10,9},{13,10},{14,13},{16,23},{19,... | collective-permute-start | bytes 688136 | tf_op jit(solution)/shard_map/ppermute | solution.py:41
  103.6 7.0 %collective-permute-start.23 = (bf16[32,3584]{1,0:T(8,128)(2,1)S(1)}, bf16[32,3584]{1,0:T(8,128)(2,1)S(1)}, u32[]{:S(2)}, u32[]{:S(2)}) collective-permute-start(bf16[32,3584]{1,0:T(8,128)(2,1)S(1)} %get-tuple-element.64), channel_id=1, source_target_pairs={{0,3},{3,4},{4,7},{7,0},{9,10},{10,13},{13,14},{14,9},{16,19},{19,... | collective-permute-start | bytes 688136 | tf_op jit(solution)/shard_map/ppermute | solution.py:41
  103.6 9.1 %collective-permute-start.25 = (bf16[32,3584]{1,0:T(8,128)(2,1)S(1)}, bf16[32,3584]{1,0:T(8,128)(2,1)S(1)}, u32[]{:S(2)}, u32[]{:S(2)}) collective-permute-start(bf16[32,3584]{1,0:T(8,128)(2,1)S(1)} %get-tuple-element.65), channel_id=1, source_target_pairs={{0,3},{3,4},{4,7},{7,0},{9,10},{10,13},{13,14},{14,9},{16,19},{19,... | collective-permute-start | bytes 688136 | tf_op jit(solution)/shard_map/ppermute | solution.py:41
  103.6 9.1 %collective-permute-start.26 = (bf16[32,3584]{1,0:T(8,128)(2,1)S(1)}, bf16[32,3584]{1,0:T(8,128)(2,1)S(1)}, u32[]{:S(2)}, u32[]{:S(2)}) collective-permute-start(bf16[32,3584]{1,0:T(8,128)(2,1)S(1)} %get-tuple-element.66), channel_id=1, source_target_pairs={{0,7},{3,0},{4,3},{7,4},{9,14},{10,9},{13,10},{14,13},{16,23},{19,... | collective-permute-start | bytes 688136 | tf_op jit(solution)/shard_map/ppermute | solution.py:41
  107.6 5.8 %collective-permute-start.28 = (bf16[32,3584]{1,0:T(8,128)(2,1)S(1)}, bf16[32,3584]{1,0:T(8,128)(2,1)S(1)}, u32[]{:S(2)}, u32[]{:S(2)}) collective-permute-start(bf16[32,3584]{1,0:T(8,128)(2,1)S(1)} %add_convert_fusion.2), channel_id=1, source_target_pairs={{0,7},{3,0},{4,3},{7,4},{9,14},{10,9},{13,10},{14,13},{16,23},{19,... | collective-permute-start | bytes 688136 | tf_op jit(solution)/shard_map/ppermute | solution.py:41
  110.6 6.7 %collective-permute-start.24 = (bf16[32,3584]{1,0:T(8,128)(2,1)S(1)}, bf16[32,3584]{1,0:T(8,128)(2,1)S(1)}, u32[]{:S(2)}, u32[]{:S(2)}) collective-permute-start(bf16[32,3584]{1,0:T(8,128)(2,1)S(1)} %add_convert_fusion.3), channel_id=1, source_target_pairs={{0,3},{3,4},{4,7},{7,0},{9,10},{10,13},{13,14},{14,9},{16,19},{19,... | collective-permute-start | bytes 688136 | tf_op jit(solution)/shard_map/ppermute | solution.py:41
  130.2 2.4 %collective-permute-start.29 = (bf16[2,3584]{1,0:T(2,128)(2,1)S(1)}, bf16[2,3584]{1,0:T(2,128)(2,1)S(1)}, u32[]{:S(2)}, u32[]{:S(2)}) collective-permute-start(bf16[2,3584]{1,0:T(2,128)(2,1)S(1)} %get-tuple-element.76), channel_id=1, source_target_pairs={{0,1},{1,0},{2,3},{3,2},{4,5},{5,4},{6,7},{7,6},{8,9},{9,8},{10,11... | collective-permute-start | bytes 43016 | tf_op jit(solution)/shard_map/ppermute | solution.py:37
  (7 other events, 56.5 us)

commit v3 on v2

--- a/solution.py
+++ b/solution.py
@@ -15,7 +15,7 @@
 BF16 = jnp.bfloat16
 I32 = jnp.int32
 MIB = 1 << 20
-CHUNK = 512
+CHUNK = 1024
 
 softmax_scale = 192.0 ** (-0.5)
 
@@ -46,7 +46,8 @@
 
 
 def exchange(blocks):
-    return [blocks[0]] + [ahead(blocks[4 - j], 4 - j) for j in range(1, 4)]
+    far = ahead(blocks[2], 2)
+    return [blocks[0], ahead(blocks[3], 3), far, ahead(blocks[1], 1)]
 
 
 def iota(shape, axis):
@@ -296,13 +297,15 @@
     return [((hi - lo, half), BF16) for lo, hi in PARTS]
 
 
-def gate_up_kernel(first, *refs):
-    before, refs = refs[: 4 if first else 0], refs[4 if first else 0 :]
-    pieces, (back, w), outs = refs[:-6], refs[-6:-4], refs[-4:]
-    for done, out in zip(before, outs):
-        out[:first, :] = done[...]
-    count = outs[0].shape[0] - first
-    part, sent, squares, weight = (out.at[pl.ds(first, count), :] for out in outs)
+def gate_up_kernel(*refs):
+    *refs, back, w, part, sent, squares, weight = refs
+    count = part.shape[0]
+    first = sent.shape[0] - count
+    pieces = refs
+    if first:
+        before, *pieces = refs
+        sent[:first, :] = before[...]
+    sent = sent.at[pl.ds(first, count), :]
     expert = coordinates()[1]
     half = w.shape[0]
     quarter = half // 4
@@ -334,15 +337,14 @@
 
 
 def gate_up(before, pieces, back, w):
-    first = before[0].shape[0] if before else 0
-    fresh = sum(p.shape[0] for p in pieces)
-    count = first + fresh
+    count = sum(p.shape[0] for p in pieces)
+    rows = count + sum(b.shape[0] for b in before)
     return call(
-        functools.partial(gate_up_kernel, first),
+        gate_up_kernel,
         (*before, *pieces, back, w),
-        [((count, 1024), F32), ((count, 1152), BF16), ((count, 1), F32), ((count, 1), F32)],
+        [((count, 1024), F32), ((rows, 1152), BF16), ((count, 1), F32), ((count, 1), F32)],
         "gate_up",
-        fresh << 23,
+        count << 23,
     )
 
 
@@ -350,7 +352,7 @@
     return d ^ (d >> 1)
 
 
-def down_kernel(part, squares, got, weight, w, *refs):
+def down_kernel(p0, q0, w0, p1, q1, w1, got, w, *refs):
     outs, hidden = refs[:-1], refs[-1]
     _, _, me_t, me_p = coordinates()
     i = iota((256, 1), 0)
@@ -358,22 +360,28 @@
     t, b = (d + me_t) & 3, i & 3
     index = late((b - me_p) & 3) * 64 + (1 - s) * 32 + rest + t
     theirs = jnp.dot(pick(index, 256), got[...], preferred_element_type=F32)
-    tail = theirs[:, 1024:]
-    lane = iota(tail.shape, 1)
-    sq = squares[...] + jnp.sum(jnp.where(lane < 3, tail, 0.0), axis=1, keepdims=True)
-    scale = lax.rsqrt(sq / 7168.0 + 1e-06)
-    for block in range(2):
-        at, back = block * 512, 512 - block * 512
-        gate = (part[:, at : at + 256] + theirs[:, back : back + 256]) * scale
-        up = (part[:, at + 256 : at + 512] + theirs[:, back + 256 : back + 512]) * scale
-        hidden[:, block * 256 : block * 256 + 256] = (
-            gate / (1.0 + jnp.exp(-gate)) * up
-        ).astype(BF16)
+    at = 0
+    for part, squares in ((p0, q0), (p1, q1)):
+        rows = slice(at, at + part.shape[0])
+        at += part.shape[0]
+        tail = theirs[rows, 1024:]
+        lane = iota(tail.shape, 1)
+        sq = squares[...] + jnp.sum(jnp.where(lane < 3, tail, 0.0), axis=1, keepdims=True)
+        scale = lax.rsqrt(sq / 7168.0 + 1e-06)
+        for block in range(2):
+            left, right = block * 512, 512 - block * 512
+            gate = (part[:, left : left + 256] + theirs[rows, right : right + 256]) * scale
+            left, right = left + 256, right + 256
+            up = (part[:, left : left + 256] + theirs[rows, right : right + 256]) * scale
+            hidden[rows, block * 256 : block * 256 + 256] = (
+                gate / (1.0 + jnp.exp(-gate)) * up
+            ).astype(BF16)
+    weight = jnp.concatenate([w0[...], w1[...]], axis=0)
     quarter = w.shape[1] // 4
     for q in range(4):
         columns = slice(q * quarter, (q + 1) * quarter)
         full = jnp.dot(hidden[...], w[:, columns], preferred_element_type=F32)
-        put_parts(full * weight[...], outs, columns, LATE)
+        put_parts(full * weight, outs, columns, LATE)
 
 
 def add(a, b):
@@ -474,8 +482,8 @@
     )
     near, far = gather_rows(jnp.concatenate([scaled, names], axis=1))
     back = (1.0 / own(gain, 0)).reshape(1, half)
-    before = gate_up((), near, back, w_gu)
-    part, sent, squares, weight = gate_up(before, far, back, w_gu)
+    p0, sent, q0, w0 = gate_up((), near, back, w_gu)
+    p1, sent, q1, w1 = gate_up((sent,), far, back, w_gu)
     w_down = load(
         (w_down[0], down_other),
         ((1, slice(0, 256), every), (None, slice(256, 512), every)),
@@ -485,7 +493,7 @@
     )
     pieces = call(
         down_kernel,
-        (part, squares, swap(sent), weight, w_down),
+        (p0, q0, w0, p1, q1, w1, swap(sent), w_down),
         product_outs(half),
         "down",
         1 << 30,

time: 135 us -> 134 us (level)
  starting transfers between devices: 50.1 us -> 51.8 us
    ppermute x21, starting transfers between devices: 25.9 us -> 27.7 us  [ahead(): lax.ppermute(a, AXES, [(r[i], r[(i + step) % 4]) for r in RINGS for i in...]
where the time goes in v3:
time: 134 us; the launch traced here: 133 us
  starting transfers between devices  51.8 us (39%)
  waiting for transfers between devices  41.5 us (31%)
  Pallas kernels  22.6 us (17%)
  blocking collectives  12.1 us (9%)
  local copies, waits for them, and re-layouts  3.15 us (2%)
  other arithmetic  1.8 us (1%)
    ppermute x21, starting transfers between devices, ahead(): lax.ppermute(a, AXES, [(r[i], r[(i + step) % 4]) for r in RINGS for i in...  27.7 us
    ppermute x21, waiting for transfers between devices, ahead(): lax.ppermute(a, AXES, [(r[i], r[(i + step) % 4]) for r in RINGS for i in...  23.3 us
    all_to_all x3, waiting for transfers between devices, plane(): return lax.all_to_all(a, AXES, 0, 0, axis_index_groups=PLANES, tiled=True)  16.8 us
    all_to_all x3, starting transfers between devices, plane(): return lax.all_to_all(a, AXES, 0, 0, axis_index_groups=PLANES, tiled=True)  14.6 us
    all_to_all x1, blocking collectives, plane(): return lax.all_to_all(a, AXES, 0, 0, axis_index_groups=PLANES, tiled=True)  12.1 us
    ppermute x9, starting transfers between devices, swap(): return lax.ppermute(a, AXES, SIBLING)  9.57 us
    pallas_call x1, Pallas kernels, attend(): pl.pallas_call(attend_kernel, in_specs=[pl.BlockSpec(memory_space=pltpu.S...  6.45 us
    pallas_call x5, Pallas kernels, call(): pl.pallas_call(kernel, in_specs=[VMEM] * len(args), out_specs=[VMEM] * le...  6.44 us
  transfers between devices with their start and end apart: 33, of which 20 were waited for; matrix products, arithmetic and copies ran while one was open for 2% of the time, Pallas kernels for 10%

profile of v3, /device:TPU:1, one launch (start us, length us, event | category | flops | bytes accessed | tf_op | source)
XLA Modules:
  0.0 133.3 jit_solution(11017907624123951206)
XLA Ops:
  0.0 6.5 %attend.1 = (bf16[16,16,512]{2,1,0:T(8,128)(2,1)}, bf16[128,3584]{1,0:T(8,128)(2,1)}) custom-call(s32[2]{0:T(128)} %lens.1, bf16[2,576,128]{2,1,0:T(8,128)(2,1)} %bitcast.33, bf16[2,576,2048]{2,1,0:T(8,128)(2,1)} %bitcast.27, bf16[128,7168]{1,0:T(8,128)(2,1)} %refs_0_.1), custom_call_target="tpu_custom_call" | custom-call | tf_op jit(solution)/shard_map/attend/pallas_call | solution.py:142
  7.0 7.4 %all-to-all-start = ((bf16[16,16,512]{2,1,0:T(8,128)(2,1)}), bf16[16,16,512]{2,1,0:T(8,128)(2,1)S(1)}, u32[]{:S(2)}, u32[]{:S(2)}) async-start(bf16[16,16,512]{2,1,0:T(8,128)(2,1)} %get-tuple-element.37), calls=%async_computation | async-start | bytes 524288 | tf_op jit(solution)/shard_map/all_to_all | solution.py:45
  14.5 1.7 %collective-permute-start.4 = (bf16[512,128]{1,0:T(8,128)(2,1)S(1)}, bf16[512,128]{1,0:T(8,128)(2,1)S(1)}, u32[]{:S(2)}, u32[]{:S(2)}) collective-permute-start(bf16[512,128]{1,0:T(8,128)(2,1)S(1)} %bitcast.19), channel_id=1, source_target_pairs={{0,1},{1,0},{2,3},{3,2},{4,5},{5,4},{6,7},{7,6},{8,9},{9,8},{10,11... | collective-permute-start | bytes 393224 | tf_op jit(solution)/shard_map/ppermute | solution.py:37
  16.1 4.4 %pack.1 = (bf16[3584,256]{1,0:T(8,128)(2,1)}, bf16[3584,256]{1,0:T(8,128)(2,1)}, bf16[256,3584]{1,0:T(8,128)(2,1)}, f32[8,128]{1,0:T(8,128)S(1)}) custom-call(bf16[7168,256]{1,0:T(8,128)(2,1)} %bitcast.23, bf16[7168,256]{1,0:T(8,128)(2,1)} %bitcast.25, bf16[256,7168]{1,0:T(8,128)(2,1)} %bitcast.21, bf16[128,3584]{1,0:T(8,128)(2,1)} %get-tuple-element.38.after), custom_call_target="tpu_custom_call" | custom-call | bytes 12582912 | tf_op jit(solution)/shard_map/pack/pallas_call | solution.py:220
  20.5 1.6 %all-to-all-done.got = bf16[16,16,512]{2,1,0:T(8,128)(2,1)S(1)} async-done(((bf16[16,16,512]{2,1,0:T(8,128)(2,1)}), bf16[16,16,512]{2,1,0:T(8,128)(2,1)S(1)}, u32[]{:S(2)}, u32[]{:S(2)}) %all-to-all-start) | async-done | bytes 262176 | tf_op jit(solution)/shard_map/all_to_all | solution.py:45
  22.4 5.2 %collective-permute-start.1 = (bf16[64,512]{1,0:T(8,128)(2,1)S(1)}, bf16[64,512]{1,0:T(8,128)(2,1)S(1)}, u32[]{:S(2)}, u32[]{:S(2)}) collective-permute-start(bf16[64,512]{1,0:T(8,128)(2,1)S(1)} %get-tuple-element.41), channel_id=1, source_target_pairs={{0,7},{3,0},{4,3},{7,4},{9,14},{10,9},{13,10},{14,13},{16,23},{19,... | collective-permute-start | bytes 196616 | tf_op jit(solution)/shard_map/ppermute | solution.py:41
  28.9 3.3 %collective-permute-done.2.p2 = bf16[64,512]{1,0:T(8,128)(2,1)S(1)} collective-permute-done((bf16[64,512]{1,0:T(8,128)(2,1)S(1)}, bf16[64,512]{1,0:T(8,128)(2,1)S(1)}, u32[]{:S(2)}, u32[]{:S(2)}) %collective-permute-start.2) | collective-permute-done | bytes 65568 | tf_op jit(solution)/shard_map/ppermute | solution.py:41
  38.1 2.1 %collective-permute-start.10 = (bf16[32,3584]{1,0:T(8,128)(2,1)S(1)}, bf16[32,3584]{1,0:T(8,128)(2,1)S(1)}, u32[]{:S(2)}, u32[]{:S(2)}) collective-permute-start(bf16[32,3584]{1,0:T(8,128)(2,1)S(1)} %get-tuple-element.48), channel_id=1, source_target_pairs={{0,7},{3,0},{4,3},{7,4},{9,14},{10,9},{13,10},{14,13},{16,23},{19,... | collective-permute-start | bytes 688136 | tf_op jit(solution)/shard_map/ppermute | solution.py:41
  40.2 1.9 %collective-permute-done.11 = bf16[32,3584]{1,0:T(8,128)(2,1)S(1)} collective-permute-done((bf16[32,3584]{1,0:T(8,128)(2,1)S(1)}, bf16[32,3584]{1,0:T(8,128)(2,1)S(1)}, u32[]{:S(2)}, u32[]{:S(2)}) %collective-permute-start.11) | collective-permute-done | bytes 229408 | tf_op jit(solution)/shard_map/ppermute | solution.py:41
  42.1 1.9 %collective-permute-start.12 = (bf16[32,3584]{1,0:T(8,128)(2,1)S(1)}, bf16[32,3584]{1,0:T(8,128)(2,1)S(1)}, u32[]{:S(2)}, u32[]{:S(2)}) collective-permute-start(bf16[32,3584]{1,0:T(8,128)(2,1)S(1)} %add_convert_fusion.4), channel_id=1, source_target_pairs={{0,7},{3,0},{4,3},{7,4},{9,14},{10,9},{13,10},{14,13},{16,23},{19,... | collective-permute-start | bytes 688136 | tf_op jit(solution)/shard_map/ppermute | solution.py:41
  44.5 2.3 %collective-permute-done.9 = bf16[32,3584]{1,0:T(8,128)(2,1)S(1)} collective-permute-done((bf16[32,3584]{1,0:T(8,128)(2,1)S(1)}, bf16[32,3584]{1,0:T(8,128)(2,1)S(1)}, u32[]{:S(2)}, u32[]{:S(2)}) %collective-permute-start.9) | collective-permute-done | bytes 229408 | tf_op jit(solution)/shard_map/ppermute | solution.py:41
  47.9 3.0 %collective-permute-done.8 = bf16[32,3584]{1,0:T(8,128)(2,1)S(1)} collective-permute-done((bf16[32,3584]{1,0:T(8,128)(2,1)S(1)}, bf16[32,3584]{1,0:T(8,128)(2,1)S(1)}, u32[]{:S(2)}, u32[]{:S(2)}) %collective-permute-start.8) | collective-permute-done | bytes 229408 | tf_op jit(solution)/shard_map/ppermute | solution.py:41
  52.3 3.6 %all-to-all-start.1 = ((bf16[16,4,3584]{2,1,0:T(4,128)(2,1)}), bf16[16,4,3584]{2,1,0:T(4,128)(2,1)S(1)}, u32[]{:S(2)}, u32[]{:S(2)}) async-start(bf16[16,4,3584]{2,1,0:T(4,128)(2,1)} %bitcast.17), calls=%async_computation.1 | async-start | bytes 917504 | tf_op jit(solution)/shard_map/all_to_all | solution.py:45
  56.9 7.8 %all-to-all-done.1 = bf16[16,4,3584]{2,1,0:T(4,128)(2,1)S(1)} async-done(((bf16[16,4,3584]{2,1,0:T(4,128)(2,1)}), bf16[16,4,3584]{2,1,0:T(4,128)(2,1)S(1)}, u32[]{:S(2)}, u32[]{:S(2)}) %all-to-all-start.1) | async-done | bytes 458784 | tf_op jit(solution)/shard_map/all_to_all | solution.py:45
  65.9 3.6 %all-to-all-start.2 = ((bf16[16,4,3712]{2,1,0:T(4,128)(2,1)}), bf16[16,4,3712]{2,1,0:T(4,128)(2,1)S(1)}, u32[]{:S(2)}, u32[]{:S(2)}) async-start(bf16[16,4,3712]{2,1,0:T(4,128)(2,1)} %broadcast_in_dim.8), calls=%async_computation.2 | async-start | bytes 950272 | tf_op jit(solution)/shard_map/all_to_all | solution.py:45
  69.5 1.6 %collective-permute-start.22 = (bf16[256,3584]{1,0:T(8,128)(2,1)}, bf16[256,3584]{1,0:T(8,128)(2,1)}, u32[]{:S(2)}, u32[]{:S(2)}) collective-permute-start(bf16[256,3584]{1,0:T(8,128)(2,1)} %get-tuple-element.61), channel_id=1, source_target_pairs={{0,1},{1,0},{2,3},{3,2},{4,5},{5,4},{6,7},{7,6},{8,9},{9,8},{10,11... | collective-permute-start | bytes 5505032 | tf_op jit(solution)/shard_map/ppermute | solution.py:37
  71.1 7.3 %all-to-all-done.2 = bf16[16,4,3712]{2,1,0:T(4,128)(2,1)S(1)} async-done(((bf16[16,4,3712]{2,1,0:T(4,128)(2,1)}), bf16[16,4,3712]{2,1,0:T(4,128)(2,1)S(1)}, u32[]{:S(2)}, u32[]{:S(2)}) %all-to-all-start.2) | async-done | bytes 475168 | tf_op jit(solution)/shard_map/all_to_all | solution.py:45
  79.8 2.0 %collective-permute-start.14 = (bf16[32,3712]{1,0:T(8,128)(2,1)S(1)}, bf16[32,3712]{1,0:T(8,128)(2,1)S(1)}, u32[]{:S(2)}, u32[]{:S(2)}) collective-permute-start(bf16[32,3712]{1,0:T(8,128)(2,1)S(1)} %bitcast.34), channel_id=1, source_target_pairs={{0,7},{3,0},{4,3},{7,4},{9,14},{10,9},{13,10},{14,13},{16,23},{19,... | collective-permute-start | bytes 712712 | tf_op jit(solution)/shard_map/ppermute | solution.py:41
  83.6 2.3 %collective-permute-done.15.refs_3_ = bf16[32,3712]{1,0:T(8,128)(2,1)S(1)} collective-permute-done((bf16[32,3712]{1,0:T(8,128)(2,1)S(1)}, bf16[32,3712]{1,0:T(8,128)(2,1)S(1)}, u32[]{:S(2)}, u32[]{:S(2)}) %collective-permute-start.15) | collective-permute-done | bytes 237600 | tf_op jit(solution)/shard_map/ppermute | solution.py:41
  85.9 3.0 %collective-permute-start.20 = (bf16[32,3712]{1,0:T(8,128)(2,1)S(1)}, bf16[32,3712]{1,0:T(8,128)(2,1)S(1)}, u32[]{:S(2)}, u32[]{:S(2)}) collective-permute-start(bf16[32,3712]{1,0:T(8,128)(2,1)S(1)} %collective-permute-done.14.refs_2_), channel_id=1, source_target_pairs={{0,7},{3,0},{4,3},{7,4},{9,14},{10,9},{13,10},{14,13},{16,23},{19,... | collective-permute-start | bytes 712712 | tf_op jit(solution)/shard_map/ppermute | solution.py:41
  88.9 2.7 %load_gate_up.1.refs_6_.refs_4_ = bf16[3584,1024]{1,0:T(8,128)(2,1)S(1)} custom-call(bf16[7168,256]{1,0:T(8,128)(2,1)} %bitcast.24, bf16[7168,256]{1,0:T(8,128)(2,1)} %bitcast.26, bf16[3584,256]{1,0:T(8,128)(2,1)S(1)} %collective-permute-done.17.refs_2_, bf16[3584,256]{1,0:T(8,128)(2,1)} %collective-permute-done.18.refs_3_), custom_call_target="tpu_custom_call" | custom-call | bytes 14680064 | tf_op jit(solution)/shard_map/load_gate_up/pallas_call | solution.py:186
  91.7 2.1 %gate_up.2 = (f32[192,1024]{1,0:T(8,128)S(1)}, bf16[192,1152]{1,0:T(8,128)(2,1)S(1)}, f32[192,1]{1,0:T(8,128)S(1)}, f32[192,1]{1,0:T(8,128)S(1)}) custom-call(bf16[64,3712]{1,0:T(8,128)(2,1)S(1)} %bitcast.18, bf16[32,3712]{1,0:T(8,128)(2,1)S(1)} %collective-permute-done.13.refs_1_, bf16[32,3712]{1,0:T(8,128)(2,1)S(1)} %collective-permute-done.14.refs_2_, ...), custom_call_target="tpu_custom_call" | custom-call | flops 1610612736 | bytes 1048576 | tf_op jit(solution)/shard_map/gate_up/pallas_call | solution.py:235
  95.3 2.5 %collective-permute-start.21 = (bf16[256,1152]{1,0:T(8,128)(2,1)S(1)}, bf16[256,1152]{1,0:T(8,128)(2,1)S(1)}, u32[]{:S(2)}, u32[]{:S(2)}) collective-permute-start(bf16[256,1152]{1,0:T(8,128)(2,1)S(1)} %get-tuple-element.60), channel_id=1, source_target_pairs={{0,1},{1,0},{2,3},{3,2},{4,5},{5,4},{6,7},{7,6},{8,9},{9,8},{10,11... | collective-permute-start | bytes 1769480 | tf_op jit(solution)/shard_map/ppermute | solution.py:37
  97.7 2.1 %load_down.1.w = bf16[512,3584]{1,0:T(8,128)(2,1)S(1)} custom-call(bf16[256,7168]{1,0:T(8,128)(2,1)} %bitcast.22, bf16[256,3584]{1,0:T(8,128)(2,1)} %collective-permute-done.22.refs_1_), custom_call_target="tpu_custom_call" | custom-call | bytes 7340032 | tf_op jit(solution)/shard_map/load_down/pallas_call | solution.py:186
  99.8 1.8 %down.1 = (bf16[64,3584]{1,0:T(8,128)(2,1)S(1)}, bf16[32,3584]{1,0:T(8,128)(2,1)S(1)}, bf16[32,3584]{1,0:T(8,128)(2,1)S(1)}, bf16[32,3584]{1,0:T(8,128)(2,1)S(1)...) custom-call(f32[192,1024]{1,0:T(8,128)S(1)} %get-tuple-element.53.p0, ...), custom_call_target="tpu_custom_call" | custom-call | flops 1073741824 | bytes 1048576 | tf_op jit(solution)/shard_map/down/pallas_call | solution.py:235
  101.7 2.0 %collective-permute-start.27 = (bf16[32,3584]{1,0:T(8,128)(2,1)S(1)}, bf16[32,3584]{1,0:T(8,128)(2,1)S(1)}, u32[]{:S(2)}, u32[]{:S(2)}) collective-permute-start(bf16[32,3584]{1,0:T(8,128)(2,1)S(1)} %get-tuple-element.68), channel_id=1, source_target_pairs={{0,7},{3,0},{4,3},{7,4},{9,14},{10,9},{13,10},{14,13},{16,23},{19,... | collective-permute-start | bytes 688136 | tf_op jit(solution)/shard_map/ppermute | solution.py:41
  103.6 3.0 %collective-permute-start.26 = (bf16[32,3584]{1,0:T(8,128)(2,1)S(1)}, bf16[32,3584]{1,0:T(8,128)(2,1)S(1)}, u32[]{:S(2)}, u32[]{:S(2)}) collective-permute-start(bf16[32,3584]{1,0:T(8,128)(2,1)S(1)} %get-tuple-element.66), channel_id=1, source_target_pairs={{0,7},{3,0},{4,3},{7,4},{9,14},{10,9},{13,10},{14,13},{16,23},{19,... | collective-permute-start | bytes 688136 | tf_op jit(solution)/shard_map/ppermute | solution.py:41
  107.5 2.9 %collective-permute-start.28 = (bf16[32,3584]{1,0:T(8,128)(2,1)S(1)}, bf16[32,3584]{1,0:T(8,128)(2,1)S(1)}, u32[]{:S(2)}, u32[]{:S(2)}) collective-permute-start(bf16[32,3584]{1,0:T(8,128)(2,1)S(1)} %add_convert_fusion.2), channel_id=1, source_target_pairs={{0,7},{3,0},{4,3},{7,4},{9,14},{10,9},{13,10},{14,13},{16,23},{19,... | collective-permute-start | bytes 688136 | tf_op jit(solution)/shard_map/ppermute | solution.py:41
  110.7 2.0 %collective-permute-done.25 = bf16[32,3584]{1,0:T(8,128)(2,1)S(1)} collective-permute-done((bf16[32,3584]{1,0:T(8,128)(2,1)S(1)}, bf16[32,3584]{1,0:T(8,128)(2,1)S(1)}, u32[]{:S(2)}, u32[]{:S(2)}) %collective-permute-start.25) | collective-permute-done | bytes 229408 | tf_op jit(solution)/shard_map/ppermute | solution.py:41
  113.4 4.0 %collective-permute-done.24 = bf16[32,3584]{1,0:T(8,128)(2,1)S(1)} collective-permute-done((bf16[32,3584]{1,0:T(8,128)(2,1)S(1)}, bf16[32,3584]{1,0:T(8,128)(2,1)S(1)}, u32[]{:S(2)}, u32[]{:S(2)}) %collective-permute-start.24) | collective-permute-done | bytes 229408 | tf_op jit(solution)/shard_map/ppermute | solution.py:41
  117.9 12.1 %all_to_all.20 = bf16[16,4,3584]{2,1,0:T(4,128)(2,1)S(1)} all-to-all(bf16[16,4,3584]{2,1,0:T(4,128)(2,1)S(1)} %bitcast.32), channel_id=1, replica_groups={{0,9,16,25,32,41,48,57,64,73,80,89,96,105,112,121},{3,10,19,26,35,42,51..., dimensions={0} | all-to-all | bytes 917504 | tf_op jit(solution)/shard_map/all_to_all | solution.py:45
  130.2 1.6 %collective-permute-start.29 = (bf16[2,3584]{1,0:T(2,128)(2,1)S(1)}, bf16[2,3584]{1,0:T(2,128)(2,1)S(1)}, u32[]{:S(2)}, u32[]{:S(2)}) collective-permute-start(bf16[2,3584]{1,0:T(2,128)(2,1)S(1)} %get-tuple-element.76), channel_id=1, source_target_pairs={{0,1},{1,0},{2,3},{3,2},{4,5},{5,4},{6,7},{7,6},{8,9},{9,8},{10,11... | collective-permute-start | bytes 43016 | tf_op jit(solution)/shard_map/ppermute | solution.py:37
  (86 shorter events, 21.8 us)
Async XLA Ops:
  6.5 28.0 %collective-permute-start.6 = (bf16[128,3584]{1,0:T(8,128)(2,1)}, bf16[128,3584]{1,0:T(8,128)(2,1)S(1)}, u32[]{:S(2)}, u32[]{:S(2)}) collective-permute-start(bf16[128,3584]{1,0:T(8,128)(2,1)} %get-tuple-element.38.after), channel_id=1, source_target_pairs={{0,1},{1,0},{2,3},{3,2},{4,5},{5,4},{6,7},{7,6},{8,9},{9,8},{10,11... | collective-permute-start | bytes 2752520 | tf_op jit(solution)/shard_map/ppermute | solution.py:37
  7.0 15.2 %all-to-all-start = ((bf16[16,16,512]{2,1,0:T(8,128)(2,1)}), bf16[16,16,512]{2,1,0:T(8,128)(2,1)S(1)}, u32[]{:S(2)}, u32[]{:S(2)}) async-start(bf16[16,16,512]{2,1,0:T(8,128)(2,1)} %get-tuple-element.37), calls=%async_computation | async-start | bytes 524288 | tf_op jit(solution)/shard_map/all_to_all | solution.py:45
  14.5 14.1 %collective-permute-start.4 = (bf16[512,128]{1,0:T(8,128)(2,1)S(1)}, bf16[512,128]{1,0:T(8,128)(2,1)S(1)}, u32[]{:S(2)}, u32[]{:S(2)}) collective-permute-start(bf16[512,128]{1,0:T(8,128)(2,1)S(1)} %bitcast.19), channel_id=1, source_target_pairs={{0,1},{1,0},{2,3},{3,2},{4,5},{5,4},{6,7},{7,6},{8,9},{9,8},{10,11... | collective-permute-start | bytes 393224 | tf_op jit(solution)/shard_map/ppermute | solution.py:37
  22.4 6.5 %collective-permute-start.1 = (bf16[64,512]{1,0:T(8,128)(2,1)S(1)}, bf16[64,512]{1,0:T(8,128)(2,1)S(1)}, u32[]{:S(2)}, u32[]{:S(2)}) collective-permute-start(bf16[64,512]{1,0:T(8,128)(2,1)S(1)} %get-tuple-element.41), channel_id=1, source_target_pairs={{0,7},{3,0},{4,3},{7,4},{9,14},{10,9},{13,10},{14,13},{16,23},{19,... | collective-permute-start | bytes 196616 | tf_op jit(solution)/shard_map/ppermute | solution.py:41
  27.6 4.7 %collective-permute-start.2 = (bf16[64,512]{1,0:T(8,128)(2,1)S(1)}, bf16[64,512]{1,0:T(8,128)(2,1)S(1)}, u32[]{:S(2)}, u32[]{:S(2)}) collective-permute-start(bf16[64,512]{1,0:T(8,128)(2,1)S(1)} %get-tuple-element.42), channel_id=1, source_target_pairs={{0,4},{3,7},{4,0},{7,3},{9,13},{10,14},{13,9},{14,10},{16,20},{19,... | collective-permute-start | bytes 196616 | tf_op jit(solution)/shard_map/ppermute | solution.py:41
  27.6 5.6 %collective-permute-start.3 = (bf16[64,512]{1,0:T(8,128)(2,1)S(1)}, bf16[64,512]{1,0:T(8,128)(2,1)S(1)}, u32[]{:S(2)}, u32[]{:S(2)}) collective-permute-start(bf16[64,512]{1,0:T(8,128)(2,1)S(1)} %get-tuple-element.43), channel_id=1, source_target_pairs={{0,3},{3,4},{4,7},{7,0},{9,10},{10,13},{13,14},{14,9},{16,19},{19,... | collective-permute-start | bytes 196616 | tf_op jit(solution)/shard_map/ppermute | solution.py:41
  36.2 5.8 %collective-permute-start.11 = (bf16[32,3584]{1,0:T(8,128)(2,1)S(1)}, bf16[32,3584]{1,0:T(8,128)(2,1)S(1)}, u32[]{:S(2)}, u32[]{:S(2)}) collective-permute-start(bf16[32,3584]{1,0:T(8,128)(2,1)S(1)} %get-tuple-element.50), channel_id=1, source_target_pairs={{0,7},{3,0},{4,3},{7,4},{9,14},{10,9},{13,10},{14,13},{16,23},{19,... | collective-permute-start | bytes 688136 | tf_op jit(solution)/shard_map/ppermute | solution.py:41
  37.2 7.0 %collective-permute-start.7 = (bf16[32,3584]{1,0:T(8,128)(2,1)S(1)}, bf16[32,3584]{1,0:T(8,128)(2,1)S(1)}, u32[]{:S(2)}, u32[]{:S(2)}) collective-permute-start(bf16[32,3584]{1,0:T(8,128)(2,1)S(1)} %get-tuple-element.46), channel_id=1, source_target_pairs={{0,3},{3,4},{4,7},{7,0},{9,10},{10,13},{13,14},{14,9},{16,19},{19,... | collective-permute-start | bytes 688136 | tf_op jit(solution)/shard_map/ppermute | solution.py:41
  38.1 6.5 %collective-permute-start.10 = (bf16[32,3584]{1,0:T(8,128)(2,1)S(1)}, bf16[32,3584]{1,0:T(8,128)(2,1)S(1)}, u32[]{:S(2)}, u32[]{:S(2)}) collective-permute-start(bf16[32,3584]{1,0:T(8,128)(2,1)S(1)} %get-tuple-element.48), channel_id=1, source_target_pairs={{0,7},{3,0},{4,3},{7,4},{9,14},{10,9},{13,10},{14,13},{16,23},{19,... | collective-permute-start | bytes 688136 | tf_op jit(solution)/shard_map/ppermute | solution.py:41
  40.2 6.7 %collective-permute-start.9 = (bf16[32,3584]{1,0:T(8,128)(2,1)S(1)}, bf16[32,3584]{1,0:T(8,128)(2,1)S(1)}, u32[]{:S(2)}, u32[]{:S(2)}) collective-permute-start(bf16[32,3584]{1,0:T(8,128)(2,1)S(1)} %get-tuple-element.47), channel_id=1, source_target_pairs={{0,3},{3,4},{4,7},{7,0},{9,10},{10,13},{13,14},{14,9},{16,19},{19,... | collective-permute-start | bytes 688136 | tf_op jit(solution)/shard_map/ppermute | solution.py:41
  42.1 5.8 %collective-permute-start.12 = (bf16[32,3584]{1,0:T(8,128)(2,1)S(1)}, bf16[32,3584]{1,0:T(8,128)(2,1)S(1)}, u32[]{:S(2)}, u32[]{:S(2)}) collective-permute-start(bf16[32,3584]{1,0:T(8,128)(2,1)S(1)} %add_convert_fusion.4), channel_id=1, source_target_pairs={{0,7},{3,0},{4,3},{7,4},{9,14},{10,9},{13,10},{14,13},{16,23},{19,... | collective-permute-start | bytes 688136 | tf_op jit(solution)/shard_map/ppermute | solution.py:41
  44.2 6.7 %collective-permute-start.8 = (bf16[32,3584]{1,0:T(8,128)(2,1)S(1)}, bf16[32,3584]{1,0:T(8,128)(2,1)S(1)}, u32[]{:S(2)}, u32[]{:S(2)}) collective-permute-start(bf16[32,3584]{1,0:T(8,128)(2,1)S(1)} %add_convert_fusion.5), channel_id=1, source_target_pairs={{0,3},{3,4},{4,7},{7,0},{9,10},{10,13},{13,14},{14,9},{16,19},{19,... | collective-permute-start | bytes 688136 | tf_op jit(solution)/shard_map/ppermute | solution.py:41
  52.3 12.4 %all-to-all-start.1 = ((bf16[16,4,3584]{2,1,0:T(4,128)(2,1)}), bf16[16,4,3584]{2,1,0:T(4,128)(2,1)S(1)}, u32[]{:S(2)}, u32[]{:S(2)}) async-start(bf16[16,4,3584]{2,1,0:T(4,128)(2,1)} %bitcast.17), calls=%async_computation.1 | async-start | bytes 917504 | tf_op jit(solution)/shard_map/all_to_all | solution.py:45
  56.1 8.9 %collective-permute-start = (bf16[2,3712]{1,0:T(2,128)(2,1)S(1)}, bf16[2,3712]{1,0:T(2,128)(2,1)S(1)}, u32[]{:S(2)}, u32[]{:S(2)}) collective-permute-start(bf16[2,3712]{1,0:T(2,128)(2,1)S(1)} %concatenate.34), channel_id=1, source_target_pairs={{0,1},{1,0},{2,3},{3,2},{4,5},{5,4},{6,7},{7,6},{8,9},{9,8},{10,11... | collective-permute-start | bytes 44552 | tf_op jit(solution)/shard_map/ppermute | solution.py:37
  56.2 25.7 %collective-permute-start.17 = (bf16[3584,256]{1,0:T(8,128)(2,1)}, bf16[3584,256]{1,0:T(8,128)(2,1)S(1)}, u32[]{:S(2)}, u32[]{:S(2)}) collective-permute-start(bf16[3584,256]{1,0:T(8,128)(2,1)} %get-tuple-element.51), channel_id=1, source_target_pairs={{0,1},{1,0},{2,3},{3,2},{4,5},{5,4},{6,7},{7,6},{8,9},{9,8},{10,11... | collective-permute-start | bytes 5505032 | tf_op jit(solution)/shard_map/ppermute | solution.py:37
  56.6 26.1 %collective-permute-start.18 = (bf16[3584,256]{1,0:T(8,128)(2,1)}, bf16[3584,256]{1,0:T(8,128)(2,1)}, u32[]{:S(2)}, u32[]{:S(2)}) collective-permute-start(bf16[3584,256]{1,0:T(8,128)(2,1)} %get-tuple-element.52), channel_id=1, source_target_pairs={{0,1},{1,0},{2,3},{3,2},{4,5},{5,4},{6,7},{7,6},{8,9},{9,8},{10,11... | collective-permute-start | bytes 5505032 | tf_op jit(solution)/shard_map/ppermute | solution.py:37
  65.9 12.5 %all-to-all-start.2 = ((bf16[16,4,3712]{2,1,0:T(4,128)(2,1)}), bf16[16,4,3712]{2,1,0:T(4,128)(2,1)S(1)}, u32[]{:S(2)}, u32[]{:S(2)}) async-start(bf16[16,4,3712]{2,1,0:T(4,128)(2,1)} %broadcast_in_dim.8), calls=%async_computation.2 | async-start | bytes 950272 | tf_op jit(solution)/shard_map/all_to_all | solution.py:45
  69.5 28.2 %collective-permute-start.22 = (bf16[256,3584]{1,0:T(8,128)(2,1)}, bf16[256,3584]{1,0:T(8,128)(2,1)}, u32[]{:S(2)}, u32[]{:S(2)}) collective-permute-start(bf16[256,3584]{1,0:T(8,128)(2,1)} %get-tuple-element.61), channel_id=1, source_target_pairs={{0,1},{1,0},{2,3},{3,2},{4,5},{5,4},{6,7},{7,6},{8,9},{9,8},{10,11... | collective-permute-start | bytes 5505032 | tf_op jit(solution)/shard_map/ppermute | solution.py:37
  78.8 7.1 %collective-permute-start.15 = (bf16[32,3712]{1,0:T(8,128)(2,1)S(1)}, bf16[32,3712]{1,0:T(8,128)(2,1)S(1)}, u32[]{:S(2)}, u32[]{:S(2)}) collective-permute-start(bf16[32,3712]{1,0:T(8,128)(2,1)S(1)} %bitcast.36), channel_id=1, source_target_pairs={{0,3},{3,4},{4,7},{7,0},{9,10},{10,13},{13,14},{14,9},{16,19},{19,... | collective-permute-start | bytes 712712 | tf_op jit(solution)/shard_map/ppermute | solution.py:41
  79.8 6.1 %collective-permute-start.14 = (bf16[32,3712]{1,0:T(8,128)(2,1)S(1)}, bf16[32,3712]{1,0:T(8,128)(2,1)S(1)}, u32[]{:S(2)}, u32[]{:S(2)}) collective-permute-start(bf16[32,3712]{1,0:T(8,128)(2,1)S(1)} %bitcast.34), channel_id=1, source_target_pairs={{0,7},{3,0},{4,3},{7,4},{9,14},{10,9},{13,10},{14,13},{16,23},{19,... | collective-permute-start | bytes 712712 | tf_op jit(solution)/shard_map/ppermute | solution.py:41
  81.8 9.8 %collective-permute-start.13 = (bf16[32,3712]{1,0:T(8,128)(2,1)S(1)}, bf16[32,3712]{1,0:T(8,128)(2,1)S(1)}, u32[]{:S(2)}, u32[]{:S(2)}) collective-permute-start(bf16[32,3712]{1,0:T(8,128)(2,1)S(1)} %bitcast.37), channel_id=1, source_target_pairs={{0,7},{3,0},{4,3},{7,4},{9,14},{10,9},{13,10},{14,13},{16,23},{19,... | collective-permute-start | bytes 712712 | tf_op jit(solution)/shard_map/ppermute | solution.py:41
  82.7 8.9 %collective-permute-start.16 = (bf16[32,3712]{1,0:T(8,128)(2,1)S(1)}, bf16[32,3712]{1,0:T(8,128)(2,1)S(1)}, u32[]{:S(2)}, u32[]{:S(2)}) collective-permute-start(bf16[32,3712]{1,0:T(8,128)(2,1)S(1)} %bitcast.35), channel_id=1, source_target_pairs={{0,3},{3,4},{4,7},{7,0},{9,10},{10,13},{13,14},{14,9},{16,19},{19,... | collective-permute-start | bytes 712712 | tf_op jit(solution)/shard_map/ppermute | solution.py:41
  85.9 7.9 %collective-permute-start.19 = (bf16[32,3712]{1,0:T(8,128)(2,1)S(1)}, bf16[32,3712]{1,0:T(8,128)(2,1)S(1)}, u32[]{:S(2)}, u32[]{:S(2)}) collective-permute-start(bf16[32,3712]{1,0:T(8,128)(2,1)S(1)} %collective-permute-done.15.refs_3_), channel_id=1, source_target_pairs={{0,3},{3,4},{4,7},{7,0},{9,10},{10,13},{13,14},{14,9},{16,19},{19,... | collective-permute-start | bytes 712712 | tf_op jit(solution)/shard_map/ppermute | solution.py:41
  85.9 7.9 %collective-permute-start.20 = (bf16[32,3712]{1,0:T(8,128)(2,1)S(1)}, bf16[32,3712]{1,0:T(8,128)(2,1)S(1)}, u32[]{:S(2)}, u32[]{:S(2)}) collective-permute-start(bf16[32,3712]{1,0:T(8,128)(2,1)S(1)} %collective-permute-done.14.refs_2_), channel_id=1, source_target_pairs={{0,7},{3,0},{4,3},{7,4},{9,14},{10,9},{13,10},{14,13},{16,23},{19,... | collective-permute-start | bytes 712712 | tf_op jit(solution)/shard_map/ppermute | solution.py:41
  95.3 4.5 %collective-permute-start.21 = (bf16[256,1152]{1,0:T(8,128)(2,1)S(1)}, bf16[256,1152]{1,0:T(8,128)(2,1)S(1)}, u32[]{:S(2)}, u32[]{:S(2)}) collective-permute-start(bf16[256,1152]{1,0:T(8,128)(2,1)S(1)} %get-tuple-element.60), channel_id=1, source_target_pairs={{0,1},{1,0},{2,3},{3,2},{4,5},{5,4},{6,7},{7,6},{8,9},{9,8},{10,11... | collective-permute-start | bytes 1769480 | tf_op jit(solution)/shard_map/ppermute | solution.py:37
  101.7 5.8 %collective-permute-start.27 = (bf16[32,3584]{1,0:T(8,128)(2,1)S(1)}, bf16[32,3584]{1,0:T(8,128)(2,1)S(1)}, u32[]{:S(2)}, u32[]{:S(2)}) collective-permute-start(bf16[32,3584]{1,0:T(8,128)(2,1)S(1)} %get-tuple-element.68), channel_id=1, source_target_pairs={{0,7},{3,0},{4,3},{7,4},{9,14},{10,9},{13,10},{14,13},{16,23},{19,... | collective-permute-start | bytes 688136 | tf_op jit(solution)/shard_map/ppermute | solution.py:41
  103.6 7.0 %collective-permute-start.23 = (bf16[32,3584]{1,0:T(8,128)(2,1)S(1)}, bf16[32,3584]{1,0:T(8,128)(2,1)S(1)}, u32[]{:S(2)}, u32[]{:S(2)}) collective-permute-start(bf16[32,3584]{1,0:T(8,128)(2,1)S(1)} %get-tuple-element.64), channel_id=1, source_target_pairs={{0,3},{3,4},{4,7},{7,0},{9,10},{10,13},{13,14},{14,9},{16,19},{19,... | collective-permute-start | bytes 688136 | tf_op jit(solution)/shard_map/ppermute | solution.py:41
  103.6 9.1 %collective-permute-start.25 = (bf16[32,3584]{1,0:T(8,128)(2,1)S(1)}, bf16[32,3584]{1,0:T(8,128)(2,1)S(1)}, u32[]{:S(2)}, u32[]{:S(2)}) collective-permute-start(bf16[32,3584]{1,0:T(8,128)(2,1)S(1)} %get-tuple-element.65), channel_id=1, source_target_pairs={{0,3},{3,4},{4,7},{7,0},{9,10},{10,13},{13,14},{14,9},{16,19},{19,... | collective-permute-start | bytes 688136 | tf_op jit(solution)/shard_map/ppermute | solution.py:41
  103.6 9.1 %collective-permute-start.26 = (bf16[32,3584]{1,0:T(8,128)(2,1)S(1)}, bf16[32,3584]{1,0:T(8,128)(2,1)S(1)}, u32[]{:S(2)}, u32[]{:S(2)}) collective-permute-start(bf16[32,3584]{1,0:T(8,128)(2,1)S(1)} %get-tuple-element.66), channel_id=1, source_target_pairs={{0,7},{3,0},{4,3},{7,4},{9,14},{10,9},{13,10},{14,13},{16,23},{19,... | collective-permute-start | bytes 688136 | tf_op jit(solution)/shard_map/ppermute | solution.py:41
  107.5 5.8 %collective-permute-start.28 = (bf16[32,3584]{1,0:T(8,128)(2,1)S(1)}, bf16[32,3584]{1,0:T(8,128)(2,1)S(1)}, u32[]{:S(2)}, u32[]{:S(2)}) collective-permute-start(bf16[32,3584]{1,0:T(8,128)(2,1)S(1)} %add_convert_fusion.2), channel_id=1, source_target_pairs={{0,7},{3,0},{4,3},{7,4},{9,14},{10,9},{13,10},{14,13},{16,23},{19,... | collective-permute-start | bytes 688136 | tf_op jit(solution)/shard_map/ppermute | solution.py:41
  110.6 6.7 %collective-permute-start.24 = (bf16[32,3584]{1,0:T(8,128)(2,1)S(1)}, bf16[32,3584]{1,0:T(8,128)(2,1)S(1)}, u32[]{:S(2)}, u32[]{:S(2)}) collective-permute-start(bf16[32,3584]{1,0:T(8,128)(2,1)S(1)} %add_convert_fusion.3), channel_id=1, source_target_pairs={{0,3},{3,4},{4,7},{7,0},{9,10},{10,13},{13,14},{14,9},{16,19},{19,... | collective-permute-start | bytes 688136 | tf_op jit(solution)/shard_map/ppermute | solution.py:41
  130.2 2.4 %collective-permute-start.29 = (bf16[2,3584]{1,0:T(2,128)(2,1)S(1)}, bf16[2,3584]{1,0:T(2,128)(2,1)S(1)}, u32[]{:S(2)}, u32[]{:S(2)}) collective-permute-start(bf16[2,3584]{1,0:T(2,128)(2,1)S(1)} %get-tuple-element.76), channel_id=1, source_target_pairs={{0,1},{1,0},{2,3},{3,2},{4,5},{5,4},{6,7},{7,6},{8,9},{9,8},{10,11... | collective-permute-start | bytes 43016 | tf_op jit(solution)/shard_map/ppermute | solution.py:37
  (7 other events, 55.6 us)

commit v4 on v3

--- a/solution.py
+++ b/solution.py
@@ -164,16 +164,19 @@
 
 
 def load_kernel(places, *refs):
-    arrays, (out, sems) = refs[: len(places)], refs[len(places) :]
+    *arrays, out, sems = refs
     core = coordinates()[0]
     copies = []
-    for n, (array, (axis, rows, columns)) in enumerate(zip(arrays, places)):
-        if axis == 0:
+    for n, (which, part, rows, columns) in enumerate(places):
+        array = arrays[which]
+        if part == 0:
             start = pl.multiple_of(core * out.shape[0], 128)
             array = array.at[pl.ds(start, out.shape[0]), :]
-        if axis == 1:
+        elif part == 1:
             start = pl.multiple_of(core * out.shape[1], 128)
             array = array.at[:, pl.ds(start, out.shape[1])]
+        else:
+            array = array.at[part, :]
         copies.append(pltpu.make_async_copy(array, out.at[rows, columns], sems.at[n]))
     for copy in copies:
         copy.start()
@@ -188,43 +191,54 @@
         in_specs=[HBM] * len(arrays),
         out_specs=VMEM,
         out_shape=pltpu.VMEM(shape, BF16),
-        scratch_shapes=[pltpu.SemaphoreType.DMA((len(arrays),))],
+        scratch_shapes=[pltpu.SemaphoreType.DMA((len(places),))],
         compiler_params=pltpu.CompilerParams(vmem_limit_bytes=limit * MIB),
         cost_estimate=pl.CostEstimate(flops=0, bytes_accessed=2 * size, transcendentals=0),
         name=name,
     )(*arrays)
 
 
-def pack_kernel(gate, up, down, after, gate_out, up_out, down_out, mark, *scratch):
-    held, sems = scratch[:3], scratch[3]
+def pack_kernel(gate, up, down, after, out, mark, held, sems):
     core = coordinates()[0]
-    half = down_out.shape[1]
-    away = pl.ds(pl.multiple_of((1 - core) * half, 128), half)
-    sources = (gate.at[away, :], up.at[away, :], down.at[:, away])
-    outs = (gate_out, up_out, down_out)
-    takes = [pltpu.make_async_copy(a, b, sems.at[n]) for n, (a, b) in enumerate(zip(sources, held))]
-    gives = [pltpu.make_async_copy(a, b, sems.at[3 + n]) for n, (a, b) in enumerate(zip(held, outs))]
+    half = gate.shape[0] // 2
+    start = (1 - core) * half
+    away = pl.ds(pl.multiple_of(start, 128), half)
+    takes = [
+        pltpu.make_async_copy(gate.at[away, :], held.at[pl.ds(0, half), :], sems.at[0]),
+        pltpu.make_async_copy(up.at[away, :], held.at[pl.ds(half, half), :], sems.at[1]),
+    ]
+    for n in range(half // 256):
+        columns = pl.ds(pl.multiple_of(start + n * 256, 128), 256)
+        rows = pl.ds(2 * half + n * 256, 256)
+        takes.append(pltpu.make_async_copy(down.at[:, columns], held.at[rows, :], sems.at[2 + n]))
+    gives = []
+    for n in range(3):
+        rows = pl.ds(n * half, half)
+        gives.append(
+            pltpu.make_async_copy(held.at[rows, :], out.at[rows, :], sems.at[len(takes) + n])
+        )
     for take in takes:
         take.start()
     mark[...] = jnp.zeros_like(mark)
-    for take, give in zip(takes, gives):
-        take.wait()
+    for n, give in enumerate(gives):
+        for take in takes[n : n + 1] if n < 2 else takes[2:]:
+            take.wait()
         give.start()
     for give in gives:
         give.wait()
 
 
 def pack(gate, up, down, after):
-    half = down.shape[1] // 2
-    shapes = [(half, 256), (half, 256), (256, half)]
+    half = gate.shape[0] // 2
     return pl.pallas_call(
         pack_kernel,
         in_specs=[HBM] * 3 + [pl.BlockSpec(memory_space=pl.ANY)],
-        out_specs=[HBM] * 3 + [VMEM],
-        out_shape=[jax.ShapeDtypeStruct(shape, BF16) for shape in shapes]
-        + [pltpu.VMEM((8, 128), F32)],
-        scratch_shapes=[pltpu.VMEM(shape, BF16) for shape in shapes]
-        + [pltpu.SemaphoreType.DMA((6,))],
+        out_specs=[HBM, VMEM],
+        out_shape=[jax.ShapeDtypeStruct((3 * half, 256), BF16), pltpu.VMEM((8, 128), F32)],
+        scratch_shapes=[
+            pltpu.VMEM((3 * half, 256), BF16),
+            pltpu.SemaphoreType.DMA((5 + half // 256,)),
+        ],
         compiler_params=pltpu.CompilerParams(vmem_limit_bytes=56 * MIB),
         cost_estimate=pl.CostEstimate(flops=0, bytes_accessed=12 * MIB, transcendentals=0),
         name="pack",
@@ -421,7 +435,7 @@
 
     sent, out_other = attend(lengths, queries.swapaxes(1, 2), cache.swapaxes(1, 2), w_out)
     uv_other = swap(w_uv[0])
-    *packed, mark = pack(w_gate[0], w_up[0], w_down[0], out_other)
+    packed, mark = pack(w_gate[0], w_up[0], w_down[0], out_other)
     blocks = pl.pallas_call(
         turn_kernel,
         in_specs=[VMEM, VMEM],
@@ -435,7 +449,7 @@
     every = slice(None)
     w_out = load(
         (w_out, out_other),
-        ((1, slice(0, VHEAD), every), (None, slice(VHEAD, 2 * VHEAD), every)),
+        ((0, 1, slice(0, VHEAD), every), (1, every, slice(VHEAD, 2 * VHEAD), every)),
         (2 * VHEAD, half),
         "load_out",
         8,
@@ -447,7 +461,7 @@
         "values",
         1 << 25,
     )
-    gate_other, up_other, down_other = (swap(a) for a in packed)
+    packed = swap(packed)
 
     gates_hi = gates.astype(BF16)
     gates_lo = (gates - gates_hi.astype(F32)).astype(BF16)
@@ -474,8 +488,13 @@
 
     scaled = (mixed * own(gain, 0)).astype(BF16)
     w_gu = load(
-        (w_gate[0], w_up[0], gate_other, up_other),
-        tuple((0 if n < 2 else None, every, slice(256 * n, 256 * n + 256)) for n in range(4)),
+        (w_gate[0], w_up[0], packed),
+        (
+            (0, 0, every, slice(0, 256)),
+            (1, 0, every, slice(256, 512)),
+            (2, slice(0, half), every, slice(512, 768)),
+            (2, slice(half, 2 * half), every, slice(768, 1024)),
+        ),
         (half, 1024),
         "load_gate_up",
         42,
@@ -485,8 +504,14 @@
     p0, sent, q0, w0 = gate_up((), near, back, w_gu)
     p1, sent, q1, w1 = gate_up((sent,), far, back, w_gu)
     w_down = load(
-        (w_down[0], down_other),
-        ((1, slice(0, 256), every), (None, slice(256, 512), every)),
+        (w_down[0], packed),
+        (
+            (0, 1, slice(0, 256), every),
+            *(
+                (1, slice(2 * half + n, 2 * half + n + 256), slice(256, 512), slice(n, n + 256))
+                for n in range(0, half, 256)
+            ),
+        ),
         (512, half),
         "load_down",
         46,

time: 134 us -> 132 us (0.985)
  blocking collectives: 12.1 us -> 24.1 us
  waiting for transfers between devices: 41.5 us -> 34.2 us
  starting transfers between devices: 51.8 us -> 46.9 us
    all_to_all x1 -> x2, blocking collectives: 12.1 us -> 24.1 us  [plane(): return lax.all_to_all(a, AXES, 0, 0, axis_index_groups=PLANES, tiled=True)]
    all_to_all x3 -> x2, waiting for transfers between devices: 16.8 us -> 9.22 us  [plane(): return lax.all_to_all(a, AXES, 0, 0, axis_index_groups=PLANES, tiled=True)]
    all_to_all x3 -> x2, starting transfers between devices: 14.6 us -> 11.2 us  [plane(): return lax.all_to_all(a, AXES, 0, 0, axis_index_groups=PLANES, tiled=True)]
    ppermute x9 -> x7, starting transfers between devices: 9.57 us -> 8.97 us  [swap(): return lax.ppermute(a, AXES, SIBLING)]
  transfers between devices with their start and end apart: 33 -> 30, of which waited for: 20 -> 19; matrix products, arithmetic and copies ran while one was open for 2% -> 2% of each run, Pallas kernels for 10% -> 9%
where the time goes in v4:
time: 132 us; the launch traced here: 131 us
  starting transfers between devices  46.9 us (36%)
  waiting for transfers between devices  34.2 us (26%)
  blocking collectives  24.1 us (18%)
  Pallas kernels  21.6 us (16%)
  local copies, waits for them, and re-layouts  2.35 us (2%)
  other arithmetic  1.79 us (1%)
    ppermute x21, starting transfers between devices, ahead(): lax.ppermute(a, AXES, [(r[i], r[(i + step) % 4]) for r in RINGS for i in...  26.7 us
    all_to_all x2, blocking collectives, plane(): return lax.all_to_all(a, AXES, 0, 0, axis_index_groups=PLANES, tiled=True)  24.1 us
    ppermute x21, waiting for transfers between devices, ahead(): lax.ppermute(a, AXES, [(r[i], r[(i + step) % 4]) for r in RINGS for i in...  23.6 us
    all_to_all x2, starting transfers between devices, plane(): return lax.all_to_all(a, AXES, 0, 0, axis_index_groups=PLANES, tiled=True)  11.2 us
    all_to_all x2, waiting for transfers between devices, plane(): return lax.all_to_all(a, AXES, 0, 0, axis_index_groups=PLANES, tiled=True)  9.22 us
    ppermute x7, starting transfers between devices, swap(): return lax.ppermute(a, AXES, SIBLING)  8.97 us
    pallas_call x5, Pallas kernels, call(): pl.pallas_call(kernel, in_specs=[VMEM] * len(args), out_specs=[VMEM] * le...  6.42 us
    pallas_call x1, Pallas kernels, attend(): pl.pallas_call(attend_kernel, in_specs=[pl.BlockSpec(memory_space=pltpu.S...  5.48 us
  transfers between devices with their start and end apart: 30, of which 19 were waited for; matrix products, arithmetic and copies ran while one was open for 2% of the time, Pallas kernels for 9%

profile of v4, /device:TPU:1, one launch (start us, length us, event | category | flops | bytes accessed | tf_op | source)
XLA Modules:
  0.0 131.3 jit_solution(10140689493408788293)
XLA Ops:
  0.0 5.5 %attend.1 = (bf16[16,16,512]{2,1,0:T(8,128)(2,1)}, bf16[128,3584]{1,0:T(8,128)(2,1)}) custom-call(s32[2]{0:T(128)} %lens.1, bf16[2,576,128]{2,1,0:T(8,128)(2,1)} %bitcast.33, bf16[2,576,2048]{2,1,0:T(8,128)(2,1)} %bitcast.27, bf16[128,7168]{1,0:T(8,128)(2,1)} %refs_0_.1), custom_call_target="tpu_custom_call" | custom-call | tf_op jit(solution)/shard_map/attend/pallas_call | solution.py:142
  5.5 1.5 %collective-permute-start.6 = (bf16[128,3584]{1,0:T(8,128)(2,1)}, bf16[128,3584]{1,0:T(8,128)(2,1)S(1)}, u32[]{:S(2)}, u32[]{:S(2)}) collective-permute-start(bf16[128,3584]{1,0:T(8,128)(2,1)} %get-tuple-element.36.after), channel_id=1, source_target_pairs={{0,1},{1,0},{2,3},{3,2},{4,5},{5,4},{6,7},{7,6},{8,9},{9,8},{10,11... | collective-permute-start | bytes 2752520 | tf_op jit(solution)/shard_map/ppermute | solution.py:37
  7.0 7.6 %all-to-all-start = ((bf16[16,16,512]{2,1,0:T(8,128)(2,1)}), bf16[16,16,512]{2,1,0:T(8,128)(2,1)S(1)}, u32[]{:S(2)}, u32[]{:S(2)}) async-start(bf16[16,16,512]{2,1,0:T(8,128)(2,1)} %get-tuple-element.35), calls=%async_computation | async-start | bytes 524288 | tf_op jit(solution)/shard_map/all_to_all | solution.py:45
  14.6 1.7 %collective-permute-start.4 = (bf16[512,128]{1,0:T(8,128)(2,1)S(1)}, bf16[512,128]{1,0:T(8,128)(2,1)S(1)}, u32[]{:S(2)}, u32[]{:S(2)}) collective-permute-start(bf16[512,128]{1,0:T(8,128)(2,1)S(1)} %bitcast.23), channel_id=1, source_target_pairs={{0,1},{1,0},{2,3},{3,2},{4,5},{5,4},{6,7},{7,6},{8,9},{9,8},{10,11... | collective-permute-start | bytes 393224 | tf_op jit(solution)/shard_map/ppermute | solution.py:37
  16.3 4.5 %pack.1 = (bf16[10752,256]{1,0:T(8,128)(2,1)}, f32[8,128]{1,0:T(8,128)S(1)}) custom-call(bf16[7168,256]{1,0:T(8,128)(2,1)} %bitcast.18, bf16[7168,256]{1,0:T(8,128)(2,1)} %bitcast.25, bf16[256,7168]{1,0:T(8,128)(2,1)} %bitcast.20, bf16[128,3584]{1,0:T(8,128)(2,1)} %get-tuple-element.36.after), custom_call_target="tpu_custom_call" | custom-call | bytes 12582912 | tf_op jit(solution)/shard_map/pack/pallas_call | solution.py:233
  20.8 1.5 %all-to-all-done.got = bf16[16,16,512]{2,1,0:T(8,128)(2,1)S(1)} async-done(((bf16[16,16,512]{2,1,0:T(8,128)(2,1)}), bf16[16,16,512]{2,1,0:T(8,128)(2,1)S(1)}, u32[]{:S(2)}, u32[]{:S(2)}) %all-to-all-start) | async-done | bytes 262176 | tf_op jit(solution)/shard_map/all_to_all | solution.py:45
  22.6 5.0 %collective-permute-start.1 = (bf16[64,512]{1,0:T(8,128)(2,1)S(1)}, bf16[64,512]{1,0:T(8,128)(2,1)S(1)}, u32[]{:S(2)}, u32[]{:S(2)}) collective-permute-start(bf16[64,512]{1,0:T(8,128)(2,1)S(1)} %get-tuple-element.39), channel_id=1, source_target_pairs={{0,7},{3,0},{4,3},{7,4},{9,14},{10,9},{13,10},{14,13},{16,23},{19,... | collective-permute-start | bytes 196616 | tf_op jit(solution)/shard_map/ppermute | solution.py:41
  28.9 3.3 %collective-permute-done.2.p2 = bf16[64,512]{1,0:T(8,128)(2,1)S(1)} collective-permute-done((bf16[64,512]{1,0:T(8,128)(2,1)S(1)}, bf16[64,512]{1,0:T(8,128)(2,1)S(1)}, u32[]{:S(2)}, u32[]{:S(2)}) %collective-permute-start.2) | collective-permute-done | bytes 65568 | tf_op jit(solution)/shard_map/ppermute | solution.py:41
  38.3 1.7 %collective-permute-start.10 = (bf16[32,3584]{1,0:T(8,128)(2,1)S(1)}, bf16[32,3584]{1,0:T(8,128)(2,1)S(1)}, u32[]{:S(2)}, u32[]{:S(2)}) collective-permute-start(bf16[32,3584]{1,0:T(8,128)(2,1)S(1)} %get-tuple-element.46), channel_id=1, source_target_pairs={{0,7},{3,0},{4,3},{7,4},{9,14},{10,9},{13,10},{14,13},{16,23},{19,... | collective-permute-start | bytes 688136 | tf_op jit(solution)/shard_map/ppermute | solution.py:41
  40.0 2.2 %collective-permute-done.11 = bf16[32,3584]{1,0:T(8,128)(2,1)S(1)} collective-permute-done((bf16[32,3584]{1,0:T(8,128)(2,1)S(1)}, bf16[32,3584]{1,0:T(8,128)(2,1)S(1)}, u32[]{:S(2)}, u32[]{:S(2)}) %collective-permute-start.11) | collective-permute-done | bytes 229408 | tf_op jit(solution)/shard_map/ppermute | solution.py:41
  44.7 1.9 %collective-permute-done.9 = bf16[32,3584]{1,0:T(8,128)(2,1)S(1)} collective-permute-done((bf16[32,3584]{1,0:T(8,128)(2,1)S(1)}, bf16[32,3584]{1,0:T(8,128)(2,1)S(1)}, u32[]{:S(2)}, u32[]{:S(2)}) %collective-permute-start.9) | collective-permute-done | bytes 229408 | tf_op jit(solution)/shard_map/ppermute | solution.py:41
  46.6 1.5 %collective-permute-done.12 = bf16[32,3584]{1,0:T(8,128)(2,1)S(1)} collective-permute-done((bf16[32,3584]{1,0:T(8,128)(2,1)S(1)}, bf16[32,3584]{1,0:T(8,128)(2,1)S(1)}, u32[]{:S(2)}, u32[]{:S(2)}) %collective-permute-start.12) | collective-permute-done | bytes 229408 | tf_op jit(solution)/shard_map/ppermute | solution.py:41
  48.1 2.6 %collective-permute-done.8 = bf16[32,3584]{1,0:T(8,128)(2,1)S(1)} collective-permute-done((bf16[32,3584]{1,0:T(8,128)(2,1)S(1)}, bf16[32,3584]{1,0:T(8,128)(2,1)S(1)}, u32[]{:S(2)}, u32[]{:S(2)}) %collective-permute-start.8) | collective-permute-done | bytes 229408 | tf_op jit(solution)/shard_map/ppermute | solution.py:41
  52.0 3.6 %all-to-all-start.1 = ((bf16[16,4,3584]{2,1,0:T(4,128)(2,1)}), bf16[16,4,3584]{2,1,0:T(4,128)(2,1)S(1)}, u32[]{:S(2)}, u32[]{:S(2)}) async-start(bf16[16,4,3584]{2,1,0:T(4,128)(2,1)} %bitcast.17), calls=%async_computation.1 | async-start | bytes 917504 | tf_op jit(solution)/shard_map/all_to_all | solution.py:45
  56.5 7.7 %all-to-all-done.1 = bf16[16,4,3584]{2,1,0:T(4,128)(2,1)S(1)} async-done(((bf16[16,4,3584]{2,1,0:T(4,128)(2,1)}), bf16[16,4,3584]{2,1,0:T(4,128)(2,1)S(1)}, u32[]{:S(2)}, u32[]{:S(2)}) %all-to-all-start.1) | async-done | bytes 458784 | tf_op jit(solution)/shard_map/all_to_all | solution.py:45
  64.6 12.5 %all_to_all.20 = bf16[16,4,3712]{2,1,0:T(4,128)(2,1)S(1)} all-to-all(bf16[16,4,3712]{2,1,0:T(4,128)(2,1)S(1)} %broadcast_in_dim.8), channel_id=1, replica_groups={{0,9,16,25,32,41,48,57,64,73,80,89,96,105,112,121},{3,10,19,26,35,42,51..., dimensions={0} | all-to-all | bytes 950272 | tf_op jit(solution)/shard_map/all_to_all | solution.py:45
  78.4 2.2 %collective-permute-start.14 = (bf16[32,3712]{1,0:T(8,128)(2,1)S(1)}, bf16[32,3712]{1,0:T(8,128)(2,1)S(1)}, u32[]{:S(2)}, u32[]{:S(2)}) collective-permute-start(bf16[32,3712]{1,0:T(8,128)(2,1)S(1)} %bitcast.34), channel_id=1, source_target_pairs={{0,7},{3,0},{4,3},{7,4},{9,14},{10,9},{13,10},{14,13},{16,23},{19,... | collective-permute-start | bytes 712712 | tf_op jit(solution)/shard_map/ppermute | solution.py:41
  82.3 2.3 %collective-permute-done.15.refs_3_ = bf16[32,3712]{1,0:T(8,128)(2,1)S(1)} collective-permute-done((bf16[32,3712]{1,0:T(8,128)(2,1)S(1)}, bf16[32,3712]{1,0:T(8,128)(2,1)S(1)}, u32[]{:S(2)}, u32[]{:S(2)}) %collective-permute-start.15) | collective-permute-done | bytes 237600 | tf_op jit(solution)/shard_map/ppermute | solution.py:41
  84.7 3.0 %collective-permute-start.19 = (bf16[32,3712]{1,0:T(8,128)(2,1)S(1)}, bf16[32,3712]{1,0:T(8,128)(2,1)S(1)}, u32[]{:S(2)}, u32[]{:S(2)}) collective-permute-start(bf16[32,3712]{1,0:T(8,128)(2,1)S(1)} %collective-permute-done.14.refs_2_), channel_id=1, source_target_pairs={{0,7},{3,0},{4,3},{7,4},{9,14},{10,9},{13,10},{14,13},{16,23},{19,... | collective-permute-start | bytes 712712 | tf_op jit(solution)/shard_map/ppermute | solution.py:41
  87.7 2.9 %load_gate_up.1.refs_6_.refs_4_ = bf16[3584,1024]{1,0:T(8,128)(2,1)S(1)} custom-call(bf16[7168,256]{1,0:T(8,128)(2,1)S(1)} %bitcast.19, bf16[7168,256]{1,0:T(8,128)(2,1)} %bitcast.26, bf16[10752,256]{1,0:T(8,128)(2,1)} %collective-permute-done.17.refs_2_.refs_1_), custom_call_target="tpu_custom_call" | custom-call | bytes 14680064 | tf_op jit(solution)/shard_map/load_gate_up/pallas_call | solution.py:189
  90.7 2.1 %gate_up.2 = (f32[192,1024]{1,0:T(8,128)S(1)}, bf16[192,1152]{1,0:T(8,128)(2,1)S(1)}, f32[192,1]{1,0:T(8,128)S(1)}, f32[192,1]{1,0:T(8,128)S(1)}) custom-call(bf16[64,3712]{1,0:T(8,128)(2,1)S(1)} %bitcast.22, bf16[32,3712]{1,0:T(8,128)(2,1)S(1)} %collective-permute-done.13.refs_1_, bf16[32,3712]{1,0:T(8,128)(2,1)S(1)} %collective-permute-done.14.refs_2_, ...), custom_call_target="tpu_custom_call" | custom-call | flops 1610612736 | bytes 1048576 | tf_op jit(solution)/shard_map/gate_up/pallas_call | solution.py:249
  92.8 1.5 %gate_up.3 = (f32[64,1024]{1,0:T(8,128)S(1)}, bf16[256,1152]{1,0:T(8,128)(2,1)S(1)}, f32[64,1]{1,0:T(8,128)S(1)}, f32[64,1]{1,0:T(8,128)S(1)}) custom-call(bf16[192,1152]{1,0:T(8,128)(2,1)S(1)} %get-tuple-element.53.refs_0_, bf16[32,3712]{1,0:T(8,128)(2,1)S(1)} %collective-permute-done.18.refs_1_, bf16[32,3712]{1,0:T(8,128)(2,1)S(1)} %collective-permute-done.19.refs_2_, ...), custom_call_target="tpu_custom_call" | custom-call | flops 536870912 | bytes 1048576 | tf_op jit(solution)/shard_map/gate_up/pallas_call | solution.py:249
  94.3 1.9 %collective-permute-start.20 = (bf16[256,1152]{1,0:T(8,128)(2,1)S(1)}, bf16[256,1152]{1,0:T(8,128)(2,1)S(1)}, u32[]{:S(2)}, u32[]{:S(2)}) collective-permute-start(bf16[256,1152]{1,0:T(8,128)(2,1)S(1)} %get-tuple-element.57), channel_id=1, source_target_pairs={{0,1},{1,0},{2,3},{3,2},{4,5},{5,4},{6,7},{7,6},{8,9},{9,8},{10,11... | collective-permute-start | bytes 1769480 | tf_op jit(solution)/shard_map/ppermute | solution.py:37
  96.2 1.8 %load_down.1.w = bf16[512,3584]{1,0:T(8,128)(2,1)S(1)} custom-call(bf16[256,7168]{1,0:T(8,128)(2,1)S(1)} %bitcast.21, bf16[10752,256]{1,0:T(8,128)(2,1)} %collective-permute-done.17.refs_2_.refs_1_), custom_call_target="tpu_custom_call" | custom-call | bytes 7340032 | tf_op jit(solution)/shard_map/load_down/pallas_call | solution.py:189
  97.9 1.8 %down.1 = (bf16[64,3584]{1,0:T(8,128)(2,1)S(1)}, bf16[32,3584]{1,0:T(8,128)(2,1)S(1)}, bf16[32,3584]{1,0:T(8,128)(2,1)S(1)}, bf16[32,3584]{1,0:T(8,128)(2,1)S(1)...) custom-call(f32[192,1024]{1,0:T(8,128)S(1)} %get-tuple-element.50.p0, ...), custom_call_target="tpu_custom_call" | custom-call | flops 1073741824 | bytes 1048576 | tf_op jit(solution)/shard_map/down/pallas_call | solution.py:249
  99.8 2.3 %collective-permute-start.25 = (bf16[32,3584]{1,0:T(8,128)(2,1)S(1)}, bf16[32,3584]{1,0:T(8,128)(2,1)S(1)}, u32[]{:S(2)}, u32[]{:S(2)}) collective-permute-start(bf16[32,3584]{1,0:T(8,128)(2,1)S(1)} %get-tuple-element.64), channel_id=1, source_target_pairs={{0,7},{3,0},{4,3},{7,4},{9,14},{10,9},{13,10},{14,13},{16,23},{19,... | collective-permute-start | bytes 688136 | tf_op jit(solution)/shard_map/ppermute | solution.py:41
  102.1 3.0 %collective-permute-start.24 = (bf16[32,3584]{1,0:T(8,128)(2,1)S(1)}, bf16[32,3584]{1,0:T(8,128)(2,1)S(1)}, u32[]{:S(2)}, u32[]{:S(2)}) collective-permute-start(bf16[32,3584]{1,0:T(8,128)(2,1)S(1)} %get-tuple-element.62), channel_id=1, source_target_pairs={{0,7},{3,0},{4,3},{7,4},{9,14},{10,9},{13,10},{14,13},{16,23},{19,... | collective-permute-start | bytes 688136 | tf_op jit(solution)/shard_map/ppermute | solution.py:41
  105.6 3.3 %collective-permute-start.26 = (bf16[32,3584]{1,0:T(8,128)(2,1)S(1)}, bf16[32,3584]{1,0:T(8,128)(2,1)S(1)}, u32[]{:S(2)}, u32[]{:S(2)}) collective-permute-start(bf16[32,3584]{1,0:T(8,128)(2,1)S(1)} %add_convert_fusion.2), channel_id=1, source_target_pairs={{0,7},{3,0},{4,3},{7,4},{9,14},{10,9},{13,10},{14,13},{16,23},{19,... | collective-permute-start | bytes 688136 | tf_op jit(solution)/shard_map/ppermute | solution.py:41
  109.2 2.0 %collective-permute-done.23 = bf16[32,3584]{1,0:T(8,128)(2,1)S(1)} collective-permute-done((bf16[32,3584]{1,0:T(8,128)(2,1)S(1)}, bf16[32,3584]{1,0:T(8,128)(2,1)S(1)}, u32[]{:S(2)}, u32[]{:S(2)}) %collective-permute-start.23) | collective-permute-done | bytes 229408 | tf_op jit(solution)/shard_map/ppermute | solution.py:41
  111.9 4.0 %collective-permute-done.22 = bf16[32,3584]{1,0:T(8,128)(2,1)S(1)} collective-permute-done((bf16[32,3584]{1,0:T(8,128)(2,1)S(1)}, bf16[32,3584]{1,0:T(8,128)(2,1)S(1)}, u32[]{:S(2)}, u32[]{:S(2)}) %collective-permute-start.22) | collective-permute-done | bytes 229408 | tf_op jit(solution)/shard_map/ppermute | solution.py:41
  116.4 11.6 %all_to_all.21 = bf16[16,4,3584]{2,1,0:T(4,128)(2,1)S(1)} all-to-all(bf16[16,4,3584]{2,1,0:T(4,128)(2,1)S(1)} %bitcast.32), channel_id=1, replica_groups={{0,9,16,25,32,41,48,57,64,73,80,89,96,105,112,121},{3,10,19,26,35,42,51..., dimensions={0} | all-to-all | bytes 917504 | tf_op jit(solution)/shard_map/all_to_all | solution.py:45
  128.2 1.6 %collective-permute-start.27 = (bf16[2,3584]{1,0:T(2,128)(2,1)S(1)}, bf16[2,3584]{1,0:T(2,128)(2,1)S(1)}, u32[]{:S(2)}, u32[]{:S(2)}) collective-permute-start(bf16[2,3584]{1,0:T(2,128)(2,1)S(1)} %get-tuple-element.72), channel_id=1, source_target_pairs={{0,1},{1,0},{2,3},{3,2},{4,5},{5,4},{6,7},{7,6},{8,9},{9,8},{10,11... | collective-permute-start | bytes 43016 | tf_op jit(solution)/shard_map/ppermute | solution.py:37
  (85 shorter events, 19.4 us)
Async XLA Ops:
  5.5 29.2 %collective-permute-start.6 = (bf16[128,3584]{1,0:T(8,128)(2,1)}, bf16[128,3584]{1,0:T(8,128)(2,1)S(1)}, u32[]{:S(2)}, u32[]{:S(2)}) collective-permute-start(bf16[128,3584]{1,0:T(8,128)(2,1)} %get-tuple-element.36.after), channel_id=1, source_target_pairs={{0,1},{1,0},{2,3},{3,2},{4,5},{5,4},{6,7},{7,6},{8,9},{9,8},{10,11... | collective-permute-start | bytes 2752520 | tf_op jit(solution)/shard_map/ppermute | solution.py:37
  7.0 15.3 %all-to-all-start = ((bf16[16,16,512]{2,1,0:T(8,128)(2,1)}), bf16[16,16,512]{2,1,0:T(8,128)(2,1)S(1)}, u32[]{:S(2)}, u32[]{:S(2)}) async-start(bf16[16,16,512]{2,1,0:T(8,128)(2,1)} %get-tuple-element.35), calls=%async_computation | async-start | bytes 524288 | tf_op jit(solution)/shard_map/all_to_all | solution.py:45
  14.6 13.9 %collective-permute-start.4 = (bf16[512,128]{1,0:T(8,128)(2,1)S(1)}, bf16[512,128]{1,0:T(8,128)(2,1)S(1)}, u32[]{:S(2)}, u32[]{:S(2)}) collective-permute-start(bf16[512,128]{1,0:T(8,128)(2,1)S(1)} %bitcast.23), channel_id=1, source_target_pairs={{0,1},{1,0},{2,3},{3,2},{4,5},{5,4},{6,7},{7,6},{8,9},{9,8},{10,11... | collective-permute-start | bytes 393224 | tf_op jit(solution)/shard_map/ppermute | solution.py:37
  22.6 6.3 %collective-permute-start.1 = (bf16[64,512]{1,0:T(8,128)(2,1)S(1)}, bf16[64,512]{1,0:T(8,128)(2,1)S(1)}, u32[]{:S(2)}, u32[]{:S(2)}) collective-permute-start(bf16[64,512]{1,0:T(8,128)(2,1)S(1)} %get-tuple-element.39), channel_id=1, source_target_pairs={{0,7},{3,0},{4,3},{7,4},{9,14},{10,9},{13,10},{14,13},{16,23},{19,... | collective-permute-start | bytes 196616 | tf_op jit(solution)/shard_map/ppermute | solution.py:41
  27.6 4.7 %collective-permute-start.2 = (bf16[64,512]{1,0:T(8,128)(2,1)S(1)}, bf16[64,512]{1,0:T(8,128)(2,1)S(1)}, u32[]{:S(2)}, u32[]{:S(2)}) collective-permute-start(bf16[64,512]{1,0:T(8,128)(2,1)S(1)} %get-tuple-element.40), channel_id=1, source_target_pairs={{0,4},{3,7},{4,0},{7,3},{9,13},{10,14},{13,9},{14,10},{16,20},{19,... | collective-permute-start | bytes 196616 | tf_op jit(solution)/shard_map/ppermute | solution.py:41
  27.6 5.6 %collective-permute-start.3 = (bf16[64,512]{1,0:T(8,128)(2,1)S(1)}, bf16[64,512]{1,0:T(8,128)(2,1)S(1)}, u32[]{:S(2)}, u32[]{:S(2)}) collective-permute-start(bf16[64,512]{1,0:T(8,128)(2,1)S(1)} %get-tuple-element.41), channel_id=1, source_target_pairs={{0,3},{3,4},{4,7},{7,0},{9,10},{10,13},{13,14},{14,9},{16,19},{19,... | collective-permute-start | bytes 196616 | tf_op jit(solution)/shard_map/ppermute | solution.py:41
  33.4 2.2 %collective-permute-start.5 = (bf16[128,256]{1,0:T(8,128)(2,1)S(1)}, bf16[128,256]{1,0:T(8,128)(2,1)S(1)}, u32[]{:S(2)}, u32[]{:S(2)}) collective-permute-start(bf16[128,256]{1,0:T(8,128)(2,1)S(1)} %values.1.mine), channel_id=1, source_target_pairs={{0,1},{1,0},{2,3},{3,2},{4,5},{5,4},{6,7},{7,6},{8,9},{9,8},{10,11... | collective-permute-start | bytes 196616 | tf_op jit(solution)/shard_map/ppermute | solution.py:37
  35.1 21.4 %copy-start.5 = (f32[7168]{0:T(1024)S(1)}, f32[7168]{0:T(1024)}, u32[]{:S(2)}) copy-start(f32[7168]{0:T(1024)} %param.18) | copy-start | bytes 86020
  36.4 5.8 %collective-permute-start.11 = (bf16[32,3584]{1,0:T(8,128)(2,1)S(1)}, bf16[32,3584]{1,0:T(8,128)(2,1)S(1)}, u32[]{:S(2)}, u32[]{:S(2)}) collective-permute-start(bf16[32,3584]{1,0:T(8,128)(2,1)S(1)} %get-tuple-element.48), channel_id=1, source_target_pairs={{0,7},{3,0},{4,3},{7,4},{9,14},{10,9},{13,10},{14,13},{16,23},{19,... | collective-permute-start | bytes 688136 | tf_op jit(solution)/shard_map/ppermute | solution.py:41
  36.5 51.2 %collective-permute-start.17 = (bf16[10752,256]{1,0:T(8,128)(2,1)}, bf16[10752,256]{1,0:T(8,128)(2,1)}, u32[]{:S(2)}, u32[]{:S(2)}) collective-permute-start(bf16[10752,256]{1,0:T(8,128)(2,1)} %get-tuple-element.49), channel_id=1, source_target_pairs={{0,1},{1,0},{2,3},{3,2},{4,5},{5,4},{6,7},{7,6},{8,9},{9,8},{10,11... | collective-permute-start | bytes 16515080 | tf_op jit(solution)/shard_map/ppermute | solution.py:37
  37.0 7.0 %collective-permute-start.7 = (bf16[32,3584]{1,0:T(8,128)(2,1)S(1)}, bf16[32,3584]{1,0:T(8,128)(2,1)S(1)}, u32[]{:S(2)}, u32[]{:S(2)}) collective-permute-start(bf16[32,3584]{1,0:T(8,128)(2,1)S(1)} %get-tuple-element.44), channel_id=1, source_target_pairs={{0,3},{3,4},{4,7},{7,0},{9,10},{10,13},{13,14},{14,9},{16,19},{19,... | collective-permute-start | bytes 688136 | tf_op jit(solution)/shard_map/ppermute | solution.py:41
  38.3 6.4 %collective-permute-start.10 = (bf16[32,3584]{1,0:T(8,128)(2,1)S(1)}, bf16[32,3584]{1,0:T(8,128)(2,1)S(1)}, u32[]{:S(2)}, u32[]{:S(2)}) collective-permute-start(bf16[32,3584]{1,0:T(8,128)(2,1)S(1)} %get-tuple-element.46), channel_id=1, source_target_pairs={{0,7},{3,0},{4,3},{7,4},{9,14},{10,9},{13,10},{14,13},{16,23},{19,... | collective-permute-start | bytes 688136 | tf_op jit(solution)/shard_map/ppermute | solution.py:41
  39.9 6.7 %collective-permute-start.9 = (bf16[32,3584]{1,0:T(8,128)(2,1)S(1)}, bf16[32,3584]{1,0:T(8,128)(2,1)S(1)}, u32[]{:S(2)}, u32[]{:S(2)}) collective-permute-start(bf16[32,3584]{1,0:T(8,128)(2,1)S(1)} %get-tuple-element.45), channel_id=1, source_target_pairs={{0,3},{3,4},{4,7},{7,0},{9,10},{10,13},{13,14},{14,9},{16,19},{19,... | collective-permute-start | bytes 688136 | tf_op jit(solution)/shard_map/ppermute | solution.py:41
  42.3 5.8 %collective-permute-start.12 = (bf16[32,3584]{1,0:T(8,128)(2,1)S(1)}, bf16[32,3584]{1,0:T(8,128)(2,1)S(1)}, u32[]{:S(2)}, u32[]{:S(2)}) collective-permute-start(bf16[32,3584]{1,0:T(8,128)(2,1)S(1)} %add_convert_fusion.4), channel_id=1, source_target_pairs={{0,7},{3,0},{4,3},{7,4},{9,14},{10,9},{13,10},{14,13},{16,23},{19,... | collective-permute-start | bytes 688136 | tf_op jit(solution)/shard_map/ppermute | solution.py:41
  44.0 6.7 %collective-permute-start.8 = (bf16[32,3584]{1,0:T(8,128)(2,1)S(1)}, bf16[32,3584]{1,0:T(8,128)(2,1)S(1)}, u32[]{:S(2)}, u32[]{:S(2)}) collective-permute-start(bf16[32,3584]{1,0:T(8,128)(2,1)S(1)} %add_convert_fusion.5), channel_id=1, source_target_pairs={{0,3},{3,4},{4,7},{7,0},{9,10},{10,13},{13,14},{14,9},{16,19},{19,... | collective-permute-start | bytes 688136 | tf_op jit(solution)/shard_map/ppermute | solution.py:41
  52.0 12.2 %all-to-all-start.1 = ((bf16[16,4,3584]{2,1,0:T(4,128)(2,1)}), bf16[16,4,3584]{2,1,0:T(4,128)(2,1)S(1)}, u32[]{:S(2)}, u32[]{:S(2)}) async-start(bf16[16,4,3584]{2,1,0:T(4,128)(2,1)} %bitcast.17), calls=%async_computation.1 | async-start | bytes 917504 | tf_op jit(solution)/shard_map/all_to_all | solution.py:45
  55.8 8.6 %collective-permute-start = (bf16[2,3712]{1,0:T(2,128)(2,1)S(1)}, bf16[2,3712]{1,0:T(2,128)(2,1)S(1)}, u32[]{:S(2)}, u32[]{:S(2)}) collective-permute-start(bf16[2,3712]{1,0:T(2,128)(2,1)S(1)} %concatenate.34), channel_id=1, source_target_pairs={{0,1},{1,0},{2,3},{3,2},{4,5},{5,4},{6,7},{7,6},{8,9},{9,8},{10,11... | collective-permute-start | bytes 44552 | tf_op jit(solution)/shard_map/ppermute | solution.py:37
  64.2 23.5 %copy-start = (bf16[1,7168,256]{2,1,0:T(8,128)(2,1)S(1)}, bf16[1,7168,256]{2,1,0:T(8,128)(2,1)}, u32[]{:S(2)}) copy-start(bf16[1,7168,256]{2,1,0:T(8,128)(2,1)} %param.21) | copy-start | bytes 11010052
  77.6 7.1 %collective-permute-start.15 = (bf16[32,3712]{1,0:T(8,128)(2,1)S(1)}, bf16[32,3712]{1,0:T(8,128)(2,1)S(1)}, u32[]{:S(2)}, u32[]{:S(2)}) collective-permute-start(bf16[32,3712]{1,0:T(8,128)(2,1)S(1)} %bitcast.36), channel_id=1, source_target_pairs={{0,3},{3,4},{4,7},{7,0},{9,10},{10,13},{13,14},{14,9},{16,19},{19,... | collective-permute-start | bytes 712712 | tf_op jit(solution)/shard_map/ppermute | solution.py:41
  78.4 6.3 %collective-permute-start.14 = (bf16[32,3712]{1,0:T(8,128)(2,1)S(1)}, bf16[32,3712]{1,0:T(8,128)(2,1)S(1)}, u32[]{:S(2)}, u32[]{:S(2)}) collective-permute-start(bf16[32,3712]{1,0:T(8,128)(2,1)S(1)} %bitcast.34), channel_id=1, source_target_pairs={{0,7},{3,0},{4,3},{7,4},{9,14},{10,9},{13,10},{14,13},{16,23},{19,... | collective-permute-start | bytes 712712 | tf_op jit(solution)/shard_map/ppermute | solution.py:41
  80.6 10.1 %collective-permute-start.13 = (bf16[32,3712]{1,0:T(8,128)(2,1)S(1)}, bf16[32,3712]{1,0:T(8,128)(2,1)S(1)}, u32[]{:S(2)}, u32[]{:S(2)}) collective-permute-start(bf16[32,3712]{1,0:T(8,128)(2,1)S(1)} %bitcast.37), channel_id=1, source_target_pairs={{0,7},{3,0},{4,3},{7,4},{9,14},{10,9},{13,10},{14,13},{16,23},{19,... | collective-permute-start | bytes 712712 | tf_op jit(solution)/shard_map/ppermute | solution.py:41
  80.9 9.7 %collective-permute-start.16 = (bf16[32,3712]{1,0:T(8,128)(2,1)S(1)}, bf16[32,3712]{1,0:T(8,128)(2,1)S(1)}, u32[]{:S(2)}, u32[]{:S(2)}) collective-permute-start(bf16[32,3712]{1,0:T(8,128)(2,1)S(1)} %bitcast.35), channel_id=1, source_target_pairs={{0,3},{3,4},{4,7},{7,0},{9,10},{10,13},{13,14},{14,9},{16,19},{19,... | collective-permute-start | bytes 712712 | tf_op jit(solution)/shard_map/ppermute | solution.py:41
  84.7 8.1 %collective-permute-start.18 = (bf16[32,3712]{1,0:T(8,128)(2,1)S(1)}, bf16[32,3712]{1,0:T(8,128)(2,1)S(1)}, u32[]{:S(2)}, u32[]{:S(2)}) collective-permute-start(bf16[32,3712]{1,0:T(8,128)(2,1)S(1)} %collective-permute-done.15.refs_3_), channel_id=1, source_target_pairs={{0,3},{3,4},{4,7},{7,0},{9,10},{10,13},{13,14},{14,9},{16,19},{19,... | collective-permute-start | bytes 712712 | tf_op jit(solution)/shard_map/ppermute | solution.py:41
  84.7 8.1 %collective-permute-start.19 = (bf16[32,3712]{1,0:T(8,128)(2,1)S(1)}, bf16[32,3712]{1,0:T(8,128)(2,1)S(1)}, u32[]{:S(2)}, u32[]{:S(2)}) collective-permute-start(bf16[32,3712]{1,0:T(8,128)(2,1)S(1)} %collective-permute-done.14.refs_2_), channel_id=1, source_target_pairs={{0,7},{3,0},{4,3},{7,4},{9,14},{10,9},{13,10},{14,13},{16,23},{19,... | collective-permute-start | bytes 712712 | tf_op jit(solution)/shard_map/ppermute | solution.py:41
  94.3 3.7 %collective-permute-start.20 = (bf16[256,1152]{1,0:T(8,128)(2,1)S(1)}, bf16[256,1152]{1,0:T(8,128)(2,1)S(1)}, u32[]{:S(2)}, u32[]{:S(2)}) collective-permute-start(bf16[256,1152]{1,0:T(8,128)(2,1)S(1)} %get-tuple-element.57), channel_id=1, source_target_pairs={{0,1},{1,0},{2,3},{3,2},{4,5},{5,4},{6,7},{7,6},{8,9},{9,8},{10,11... | collective-permute-start | bytes 1769480 | tf_op jit(solution)/shard_map/ppermute | solution.py:37
  99.8 5.8 %collective-permute-start.25 = (bf16[32,3584]{1,0:T(8,128)(2,1)S(1)}, bf16[32,3584]{1,0:T(8,128)(2,1)S(1)}, u32[]{:S(2)}, u32[]{:S(2)}) collective-permute-start(bf16[32,3584]{1,0:T(8,128)(2,1)S(1)} %get-tuple-element.64), channel_id=1, source_target_pairs={{0,7},{3,0},{4,3},{7,4},{9,14},{10,9},{13,10},{14,13},{16,23},{19,... | collective-permute-start | bytes 688136 | tf_op jit(solution)/shard_map/ppermute | solution.py:41
  102.1 7.0 %collective-permute-start.21 = (bf16[32,3584]{1,0:T(8,128)(2,1)S(1)}, bf16[32,3584]{1,0:T(8,128)(2,1)S(1)}, u32[]{:S(2)}, u32[]{:S(2)}) collective-permute-start(bf16[32,3584]{1,0:T(8,128)(2,1)S(1)} %get-tuple-element.60), channel_id=1, source_target_pairs={{0,3},{3,4},{4,7},{7,0},{9,10},{10,13},{13,14},{14,9},{16,19},{19,... | collective-permute-start | bytes 688136 | tf_op jit(solution)/shard_map/ppermute | solution.py:41
  102.1 9.1 %collective-permute-start.23 = (bf16[32,3584]{1,0:T(8,128)(2,1)S(1)}, bf16[32,3584]{1,0:T(8,128)(2,1)S(1)}, u32[]{:S(2)}, u32[]{:S(2)}) collective-permute-start(bf16[32,3584]{1,0:T(8,128)(2,1)S(1)} %get-tuple-element.61), channel_id=1, source_target_pairs={{0,3},{3,4},{4,7},{7,0},{9,10},{10,13},{13,14},{14,9},{16,19},{19,... | collective-permute-start | bytes 688136 | tf_op jit(solution)/shard_map/ppermute | solution.py:41
  102.1 9.1 %collective-permute-start.24 = (bf16[32,3584]{1,0:T(8,128)(2,1)S(1)}, bf16[32,3584]{1,0:T(8,128)(2,1)S(1)}, u32[]{:S(2)}, u32[]{:S(2)}) collective-permute-start(bf16[32,3584]{1,0:T(8,128)(2,1)S(1)} %get-tuple-element.62), channel_id=1, source_target_pairs={{0,7},{3,0},{4,3},{7,4},{9,14},{10,9},{13,10},{14,13},{16,23},{19,... | collective-permute-start | bytes 688136 | tf_op jit(solution)/shard_map/ppermute | solution.py:41
  105.6 6.2 %collective-permute-start.26 = (bf16[32,3584]{1,0:T(8,128)(2,1)S(1)}, bf16[32,3584]{1,0:T(8,128)(2,1)S(1)}, u32[]{:S(2)}, u32[]{:S(2)}) collective-permute-start(bf16[32,3584]{1,0:T(8,128)(2,1)S(1)} %add_convert_fusion.2), channel_id=1, source_target_pairs={{0,7},{3,0},{4,3},{7,4},{9,14},{10,9},{13,10},{14,13},{16,23},{19,... | collective-permute-start | bytes 688136 | tf_op jit(solution)/shard_map/ppermute | solution.py:41
  109.1 6.7 %collective-permute-start.22 = (bf16[32,3584]{1,0:T(8,128)(2,1)S(1)}, bf16[32,3584]{1,0:T(8,128)(2,1)S(1)}, u32[]{:S(2)}, u32[]{:S(2)}) collective-permute-start(bf16[32,3584]{1,0:T(8,128)(2,1)S(1)} %add_convert_fusion.3), channel_id=1, source_target_pairs={{0,3},{3,4},{4,7},{7,0},{9,10},{10,13},{13,14},{14,9},{16,19},{19,... | collective-permute-start | bytes 688136 | tf_op jit(solution)/shard_map/ppermute | solution.py:41
  128.2 2.4 %collective-permute-start.27 = (bf16[2,3584]{1,0:T(2,128)(2,1)S(1)}, bf16[2,3584]{1,0:T(2,128)(2,1)S(1)}, u32[]{:S(2)}, u32[]{:S(2)}) collective-permute-start(bf16[2,3584]{1,0:T(2,128)(2,1)S(1)} %get-tuple-element.72), channel_id=1, source_target_pairs={{0,1},{1,0},{2,3},{3,2},{4,5},{5,4},{6,7},{7,6},{8,9},{9,8},{10,11... | collective-permute-start | bytes 43016 | tf_op jit(solution)/shard_map/ppermute | solution.py:37
  (6 other events, 98.1 us)

commit v5 on v4

--- a/solution.py
+++ b/solution.py
@@ -287,7 +287,7 @@
         ref[:, columns] = full[lo:hi].astype(BF16)
 
 
-def project_kernel(mine, theirs, w, *refs):
+def project_kernel(mine, theirs, w, rows, back, *refs):
     outs, val = refs[:-1], refs[-1]
     _, _, me_t, me_p = coordinates()
     i = iota((128, 1), 0)
@@ -475,10 +475,11 @@
         ]
     )
     res, names = rows[:, :half].astype(F32), rows[:, half:]
+    back = (1.0 / own(gain, 0)).reshape(1, half)
 
     pieces = call(
         project_kernel,
-        (mine, swap(mine), w_out),
+        (mine, swap(mine), w_out, rows, back),
         product_outs(half),
         "project",
         1 << 29,
@@ -500,7 +501,6 @@
         42,
     )
     near, far = gather_rows(jnp.concatenate([scaled, names], axis=1))
-    back = (1.0 / own(gain, 0)).reshape(1, half)
     p0, sent, q0, w0 = gate_up((), near, back, w_gu)
     p1, sent, q1, w1 = gate_up((sent,), far, back, w_gu)
     w_down = load(

time: 132 us -> 132 us (level)
  Pallas kernels: 21.6 us -> 23.3 us
  waiting for transfers between devices: 34.2 us -> 32.7 us
  other arithmetic: 1.79 us -> 3.16 us
    ppermute x21, waiting for transfers between devices: 23.6 us -> 22.1 us  [ahead(): lax.ppermute(a, AXES, [(r[i], r[(i + step) % 4]) for r in RINGS for i in...]
  transfers between devices with their start and end apart: 30 -> 30, of which waited for: 19 -> 18; matrix products, arithmetic and copies ran while one was open for 2% -> 3% of each run, Pallas kernels for 9% -> 10%
where the time goes in v5:
time: 132 us
  starting transfers between devices  45.9 us (35%)
  waiting for transfers between devices  32.7 us (25%)
  blocking collectives  24.2 us (18%)
  Pallas kernels  23.3 us (18%)
  other arithmetic  3.16 us (2%)
  local copies, waits for them, and re-layouts  2.33 us (2%)
    ppermute x21, starting transfers between devices, ahead(): lax.ppermute(a, AXES, [(r[i], r[(i + step) % 4]) for r in RINGS for i in...  27 us
    all_to_all x2, blocking collectives, plane(): return lax.all_to_all(a, AXES, 0, 0, axis_index_groups=PLANES, tiled=True)  24.2 us
    ppermute x21, waiting for transfers between devices, ahead(): lax.ppermute(a, AXES, [(r[i], r[(i + step) % 4]) for r in RINGS for i in...  22.1 us
    all_to_all x2, starting transfers between devices, plane(): return lax.all_to_all(a, AXES, 0, 0, axis_index_groups=PLANES, tiled=True)  11.3 us
    all_to_all x2, waiting for transfers between devices, plane(): return lax.all_to_all(a, AXES, 0, 0, axis_index_groups=PLANES, tiled=True)  9.22 us
    ppermute x7, starting transfers between devices, swap(): return lax.ppermute(a, AXES, SIBLING)  7.66 us
    pallas_call x5, Pallas kernels, call(): pl.pallas_call(kernel, in_specs=[VMEM] * len(args), out_specs=[VMEM] * le...  6.47 us
    pallas_call x1, Pallas kernels, attend(): pl.pallas_call(attend_kernel, in_specs=[pl.BlockSpec(memory_space=pltpu.S...  6.45 us
  transfers between devices with their start and end apart: 30, of which 18 were waited for; matrix products, arithmetic and copies ran while one was open for 3% of the time, Pallas kernels for 10%

profile of v5, /device:TPU:1, one launch (start us, length us, event | category | flops | bytes accessed | tf_op | source)
XLA Modules:
  0.0 132.0 jit_solution(9225296435280169050)
XLA Ops:
  0.0 6.4 %attend.1 = (bf16[16,16,512]{2,1,0:T(8,128)(2,1)}, bf16[128,3584]{1,0:T(8,128)(2,1)}) custom-call(s32[2]{0:T(128)} %lens.1, bf16[2,576,128]{2,1,0:T(8,128)(2,1)} %bitcast.33, bf16[2,576,2048]{2,1,0:T(8,128)(2,1)} %bitcast.27, bf16[128,7168]{1,0:T(8,128)(2,1)} %refs_0_.1), custom_call_target="tpu_custom_call" | custom-call | tf_op jit(solution)/shard_map/attend/pallas_call | solution.py:142
  6.5 7.7 %all-to-all-start = ((bf16[16,16,512]{2,1,0:T(8,128)(2,1)}), bf16[16,16,512]{2,1,0:T(8,128)(2,1)S(1)}, u32[]{:S(2)}, u32[]{:S(2)}) async-start(bf16[16,16,512]{2,1,0:T(8,128)(2,1)} %get-tuple-element.35), calls=%async_computation | async-start | bytes 524288 | tf_op jit(solution)/shard_map/all_to_all | solution.py:45
  14.2 1.8 %collective-permute-start.4 = (bf16[512,128]{1,0:T(8,128)(2,1)S(1)}, bf16[512,128]{1,0:T(8,128)(2,1)S(1)}, u32[]{:S(2)}, u32[]{:S(2)}) collective-permute-start(bf16[512,128]{1,0:T(8,128)(2,1)S(1)} %bitcast.23), channel_id=1, source_target_pairs={{0,1},{1,0},{2,3},{3,2},{4,5},{5,4},{6,7},{7,6},{8,9},{9,8},{10,11... | collective-permute-start | bytes 393224 | tf_op jit(solution)/shard_map/ppermute | solution.py:37
  16.7 4.5 %pack.1 = (bf16[10752,256]{1,0:T(8,128)(2,1)}, f32[8,128]{1,0:T(8,128)S(1)}) custom-call(bf16[7168,256]{1,0:T(8,128)(2,1)} %bitcast.18, bf16[7168,256]{1,0:T(8,128)(2,1)} %bitcast.25, bf16[256,7168]{1,0:T(8,128)(2,1)} %bitcast.20, bf16[128,3584]{1,0:T(8,128)(2,1)} %get-tuple-element.36.after), custom_call_target="tpu_custom_call" | custom-call | bytes 12582912 | tf_op jit(solution)/shard_map/pack/pallas_call | solution.py:233
  22.7 5.3 %collective-permute-start.1 = (bf16[64,512]{1,0:T(8,128)(2,1)}, bf16[64,512]{1,0:T(8,128)(2,1)S(1)}, u32[]{:S(2)}, u32[]{:S(2)}) collective-permute-start(bf16[64,512]{1,0:T(8,128)(2,1)} %get-tuple-element.39), channel_id=1, source_target_pairs={{0,7},{3,0},{4,3},{7,4},{9,14},{10,9},{13,10},{14,13},{16,23},{19,... | collective-permute-start | bytes 196616 | tf_op jit(solution)/shard_map/ppermute | solution.py:41
  28.9 1.4 %broadcast_divide_fusion = (f32[3584]{0:T(1024)S(1)}, f32[3584]{0:T(1024)}) fusion(f32[7168]{0:T(1024)} %param.18, s32[]{:T(128)S(6)} %select_n.17), kind=kLoop, calls=%fused_computation.21 | loop fusion | flops 3584 | bytes 43012 | tf_op jit(solution)/shard_map/div | solution.py:478
  30.4 2.3 %collective-permute-done.2.p2 = bf16[64,512]{1,0:T(8,128)(2,1)S(1)} collective-permute-done((bf16[64,512]{1,0:T(8,128)(2,1)S(1)}, bf16[64,512]{1,0:T(8,128)(2,1)S(1)}, u32[]{:S(2)}, u32[]{:S(2)}) %collective-permute-start.2) | collective-permute-done | bytes 65568 | tf_op jit(solution)/shard_map/ppermute | solution.py:41
  33.9 1.4 %collective-permute-start.5 = (bf16[128,256]{1,0:T(8,128)(2,1)S(1)}, bf16[128,256]{1,0:T(8,128)(2,1)S(1)}, u32[]{:S(2)}, u32[]{:S(2)}) collective-permute-start(bf16[128,256]{1,0:T(8,128)(2,1)S(1)} %values.1.mine), channel_id=1, source_target_pairs={{0,1},{1,0},{2,3},{3,2},{4,5},{5,4},{6,7},{7,6},{8,9},{9,8},{10,11... | collective-permute-start | bytes 196616 | tf_op jit(solution)/shard_map/ppermute | solution.py:37
  38.8 1.7 %collective-permute-start.10 = (bf16[32,3584]{1,0:T(8,128)(2,1)S(1)}, bf16[32,3584]{1,0:T(8,128)(2,1)S(1)}, u32[]{:S(2)}, u32[]{:S(2)}) collective-permute-start(bf16[32,3584]{1,0:T(8,128)(2,1)S(1)} %get-tuple-element.46), channel_id=1, source_target_pairs={{0,7},{3,0},{4,3},{7,4},{9,14},{10,9},{13,10},{14,13},{16,23},{19,... | collective-permute-start | bytes 688136 | tf_op jit(solution)/shard_map/ppermute | solution.py:41
  40.6 2.2 %collective-permute-done.11 = bf16[32,3584]{1,0:T(8,128)(2,1)S(1)} collective-permute-done((bf16[32,3584]{1,0:T(8,128)(2,1)S(1)}, bf16[32,3584]{1,0:T(8,128)(2,1)S(1)}, u32[]{:S(2)}, u32[]{:S(2)}) %collective-permute-start.11) | collective-permute-done | bytes 229408 | tf_op jit(solution)/shard_map/ppermute | solution.py:41
  45.3 1.9 %collective-permute-done.9 = bf16[32,3584]{1,0:T(8,128)(2,1)S(1)} collective-permute-done((bf16[32,3584]{1,0:T(8,128)(2,1)S(1)}, bf16[32,3584]{1,0:T(8,128)(2,1)S(1)}, u32[]{:S(2)}, u32[]{:S(2)}) %collective-permute-start.9) | collective-permute-done | bytes 229408 | tf_op jit(solution)/shard_map/ppermute | solution.py:41
  47.2 1.6 %collective-permute-done.12 = bf16[32,3584]{1,0:T(8,128)(2,1)S(1)} collective-permute-done((bf16[32,3584]{1,0:T(8,128)(2,1)S(1)}, bf16[32,3584]{1,0:T(8,128)(2,1)S(1)}, u32[]{:S(2)}, u32[]{:S(2)}) %collective-permute-start.12) | collective-permute-done | bytes 229408 | tf_op jit(solution)/shard_map/ppermute | solution.py:41
  48.7 2.6 %collective-permute-done.8 = bf16[32,3584]{1,0:T(8,128)(2,1)S(1)} collective-permute-done((bf16[32,3584]{1,0:T(8,128)(2,1)S(1)}, bf16[32,3584]{1,0:T(8,128)(2,1)S(1)}, u32[]{:S(2)}, u32[]{:S(2)}) %collective-permute-start.8) | collective-permute-done | bytes 229408 | tf_op jit(solution)/shard_map/ppermute | solution.py:41
  52.6 3.6 %all-to-all-start.1 = ((bf16[16,4,3584]{2,1,0:T(4,128)(2,1)}), bf16[16,4,3584]{2,1,0:T(4,128)(2,1)S(1)}, u32[]{:S(2)}, u32[]{:S(2)}) async-start(bf16[16,4,3584]{2,1,0:T(4,128)(2,1)} %bitcast.17), calls=%async_computation.1 | async-start | bytes 917504 | tf_op jit(solution)/shard_map/all_to_all | solution.py:45
  56.2 8.6 %all-to-all-done.1 = bf16[16,4,3584]{2,1,0:T(4,128)(2,1)S(1)} async-done(((bf16[16,4,3584]{2,1,0:T(4,128)(2,1)}), bf16[16,4,3584]{2,1,0:T(4,128)(2,1)S(1)}, u32[]{:S(2)}, u32[]{:S(2)}) %all-to-all-start.1) | async-done | bytes 458784 | tf_op jit(solution)/shard_map/all_to_all | solution.py:45
  65.1 12.6 %all_to_all.20 = bf16[16,4,3712]{2,1,0:T(4,128)(2,1)S(1)} all-to-all(bf16[16,4,3712]{2,1,0:T(4,128)(2,1)S(1)} %broadcast_in_dim.8), channel_id=1, replica_groups={{0,9,16,25,32,41,48,57,64,73,80,89,96,105,112,121},{3,10,19,26,35,42,51..., dimensions={0} | all-to-all | bytes 950272 | tf_op jit(solution)/shard_map/all_to_all | solution.py:45
  78.9 2.2 %collective-permute-start.14 = (bf16[32,3712]{1,0:T(8,128)(2,1)S(1)}, bf16[32,3712]{1,0:T(8,128)(2,1)S(1)}, u32[]{:S(2)}, u32[]{:S(2)}) collective-permute-start(bf16[32,3712]{1,0:T(8,128)(2,1)S(1)} %bitcast.34), channel_id=1, source_target_pairs={{0,7},{3,0},{4,3},{7,4},{9,14},{10,9},{13,10},{14,13},{16,23},{19,... | collective-permute-start | bytes 712712 | tf_op jit(solution)/shard_map/ppermute | solution.py:41
  82.9 2.3 %collective-permute-done.15.refs_3_ = bf16[32,3712]{1,0:T(8,128)(2,1)S(1)} collective-permute-done((bf16[32,3712]{1,0:T(8,128)(2,1)S(1)}, bf16[32,3712]{1,0:T(8,128)(2,1)S(1)}, u32[]{:S(2)}, u32[]{:S(2)}) %collective-permute-start.15) | collective-permute-done | bytes 237600 | tf_op jit(solution)/shard_map/ppermute | solution.py:41
  85.3 3.0 %collective-permute-start.19 = (bf16[32,3712]{1,0:T(8,128)(2,1)S(1)}, bf16[32,3712]{1,0:T(8,128)(2,1)S(1)}, u32[]{:S(2)}, u32[]{:S(2)}) collective-permute-start(bf16[32,3712]{1,0:T(8,128)(2,1)S(1)} %collective-permute-done.14.refs_2_), channel_id=1, source_target_pairs={{0,7},{3,0},{4,3},{7,4},{9,14},{10,9},{13,10},{14,13},{16,23},{19,... | collective-permute-start | bytes 712712 | tf_op jit(solution)/shard_map/ppermute | solution.py:41
  88.3 2.9 %load_gate_up.1.refs_6_.refs_4_ = bf16[3584,1024]{1,0:T(8,128)(2,1)S(1)} custom-call(bf16[7168,256]{1,0:T(8,128)(2,1)S(1)} %bitcast.19, bf16[7168,256]{1,0:T(8,128)(2,1)} %bitcast.26, bf16[10752,256]{1,0:T(8,128)(2,1)} %collective-permute-done.17.refs_2_.refs_1_), custom_call_target="tpu_custom_call" | custom-call | bytes 14680064 | tf_op jit(solution)/shard_map/load_gate_up/pallas_call | solution.py:189
  91.2 2.1 %gate_up.2 = (f32[192,1024]{1,0:T(8,128)S(1)}, bf16[192,1152]{1,0:T(8,128)(2,1)S(1)}, f32[192,1]{1,0:T(8,128)S(1)}, f32[192,1]{1,0:T(8,128)S(1)}) custom-call(bf16[64,3712]{1,0:T(8,128)(2,1)S(1)} %bitcast.22, bf16[32,3712]{1,0:T(8,128)(2,1)S(1)} %collective-permute-done.13.refs_1_, bf16[32,3712]{1,0:T(8,128)(2,1)S(1)} %collective-permute-done.14.refs_2_, ...), custom_call_target="tpu_custom_call" | custom-call | flops 1610612736 | bytes 1048576 | tf_op jit(solution)/shard_map/gate_up/pallas_call | solution.py:249
  93.3 1.5 %gate_up.3 = (f32[64,1024]{1,0:T(8,128)S(1)}, bf16[256,1152]{1,0:T(8,128)(2,1)S(1)}, f32[64,1]{1,0:T(8,128)S(1)}, f32[64,1]{1,0:T(8,128)S(1)}) custom-call(bf16[192,1152]{1,0:T(8,128)(2,1)S(1)} %get-tuple-element.53.refs_0_, bf16[32,3712]{1,0:T(8,128)(2,1)S(1)} %collective-permute-done.18.refs_1_, bf16[32,3712]{1,0:T(8,128)(2,1)S(1)} %collective-permute-done.19.refs_2_, ...), custom_call_target="tpu_custom_call" | custom-call | flops 536870912 | bytes 1048576 | tf_op jit(solution)/shard_map/gate_up/pallas_call | solution.py:249
  94.8 1.9 %collective-permute-start.20 = (bf16[256,1152]{1,0:T(8,128)(2,1)S(1)}, bf16[256,1152]{1,0:T(8,128)(2,1)S(1)}, u32[]{:S(2)}, u32[]{:S(2)}) collective-permute-start(bf16[256,1152]{1,0:T(8,128)(2,1)S(1)} %get-tuple-element.57), channel_id=1, source_target_pairs={{0,1},{1,0},{2,3},{3,2},{4,5},{5,4},{6,7},{7,6},{8,9},{9,8},{10,11... | collective-permute-start | bytes 1769480 | tf_op jit(solution)/shard_map/ppermute | solution.py:37
  96.7 1.8 %load_down.1.w = bf16[512,3584]{1,0:T(8,128)(2,1)S(1)} custom-call(bf16[256,7168]{1,0:T(8,128)(2,1)S(1)} %bitcast.21, bf16[10752,256]{1,0:T(8,128)(2,1)} %collective-permute-done.17.refs_2_.refs_1_), custom_call_target="tpu_custom_call" | custom-call | bytes 7340032 | tf_op jit(solution)/shard_map/load_down/pallas_call | solution.py:189
  98.5 1.9 %down.1 = (bf16[64,3584]{1,0:T(8,128)(2,1)S(1)}, bf16[32,3584]{1,0:T(8,128)(2,1)S(1)}, bf16[32,3584]{1,0:T(8,128)(2,1)S(1)}, bf16[32,3584]{1,0:T(8,128)(2,1)S(1)...) custom-call(f32[192,1024]{1,0:T(8,128)S(1)} %get-tuple-element.50.p0, ...), custom_call_target="tpu_custom_call" | custom-call | flops 1073741824 | bytes 1048576 | tf_op jit(solution)/shard_map/down/pallas_call | solution.py:249
  100.4 2.3 %collective-permute-start.25 = (bf16[32,3584]{1,0:T(8,128)(2,1)S(1)}, bf16[32,3584]{1,0:T(8,128)(2,1)S(1)}, u32[]{:S(2)}, u32[]{:S(2)}) collective-permute-start(bf16[32,3584]{1,0:T(8,128)(2,1)S(1)} %get-tuple-element.64), channel_id=1, source_target_pairs={{0,7},{3,0},{4,3},{7,4},{9,14},{10,9},{13,10},{14,13},{16,23},{19,... | collective-permute-start | bytes 688136 | tf_op jit(solution)/shard_map/ppermute | solution.py:41
  102.7 3.0 %collective-permute-start.24 = (bf16[32,3584]{1,0:T(8,128)(2,1)S(1)}, bf16[32,3584]{1,0:T(8,128)(2,1)S(1)}, u32[]{:S(2)}, u32[]{:S(2)}) collective-permute-start(bf16[32,3584]{1,0:T(8,128)(2,1)S(1)} %get-tuple-element.62), channel_id=1, source_target_pairs={{0,7},{3,0},{4,3},{7,4},{9,14},{10,9},{13,10},{14,13},{16,23},{19,... | collective-permute-start | bytes 688136 | tf_op jit(solution)/shard_map/ppermute | solution.py:41
  106.3 3.3 %collective-permute-start.26 = (bf16[32,3584]{1,0:T(8,128)(2,1)S(1)}, bf16[32,3584]{1,0:T(8,128)(2,1)S(1)}, u32[]{:S(2)}, u32[]{:S(2)}) collective-permute-start(bf16[32,3584]{1,0:T(8,128)(2,1)S(1)} %add_convert_fusion.2), channel_id=1, source_target_pairs={{0,7},{3,0},{4,3},{7,4},{9,14},{10,9},{13,10},{14,13},{16,23},{19,... | collective-permute-start | bytes 688136 | tf_op jit(solution)/shard_map/ppermute | solution.py:41
  109.8 2.0 %collective-permute-done.23 = bf16[32,3584]{1,0:T(8,128)(2,1)S(1)} collective-permute-done((bf16[32,3584]{1,0:T(8,128)(2,1)S(1)}, bf16[32,3584]{1,0:T(8,128)(2,1)S(1)}, u32[]{:S(2)}, u32[]{:S(2)}) %collective-permute-start.23) | collective-permute-done | bytes 229408 | tf_op jit(solution)/shard_map/ppermute | solution.py:41
  112.5 4.0 %collective-permute-done.22 = bf16[32,3584]{1,0:T(8,128)(2,1)S(1)} collective-permute-done((bf16[32,3584]{1,0:T(8,128)(2,1)S(1)}, bf16[32,3584]{1,0:T(8,128)(2,1)S(1)}, u32[]{:S(2)}, u32[]{:S(2)}) %collective-permute-start.22) | collective-permute-done | bytes 229408 | tf_op jit(solution)/shard_map/ppermute | solution.py:41
  117.0 11.6 %all_to_all.21 = bf16[16,4,3584]{2,1,0:T(4,128)(2,1)S(1)} all-to-all(bf16[16,4,3584]{2,1,0:T(4,128)(2,1)S(1)} %bitcast.32), channel_id=1, replica_groups={{0,9,16,25,32,41,48,57,64,73,80,89,96,105,112,121},{3,10,19,26,35,42,51..., dimensions={0} | all-to-all | bytes 917504 | tf_op jit(solution)/shard_map/all_to_all | solution.py:45
  128.9 1.6 %collective-permute-start.27 = (bf16[2,3584]{1,0:T(2,128)(2,1)S(1)}, bf16[2,3584]{1,0:T(2,128)(2,1)S(1)}, u32[]{:S(2)}, u32[]{:S(2)}) collective-permute-start(bf16[2,3584]{1,0:T(2,128)(2,1)S(1)} %get-tuple-element.72), channel_id=1, source_target_pairs={{0,1},{1,0},{2,3},{3,2},{4,5},{5,4},{6,7},{7,6},{8,9},{9,8},{10,11... | collective-permute-start | bytes 43016 | tf_op jit(solution)/shard_map/ppermute | solution.py:37
  (87 shorter events, 18.8 us)
Async XLA Ops:
  6.5 15.4 %all-to-all-start = ((bf16[16,16,512]{2,1,0:T(8,128)(2,1)}), bf16[16,16,512]{2,1,0:T(8,128)(2,1)S(1)}, u32[]{:S(2)}, u32[]{:S(2)}) async-start(bf16[16,16,512]{2,1,0:T(8,128)(2,1)} %get-tuple-element.35), calls=%async_computation | async-start | bytes 524288 | tf_op jit(solution)/shard_map/all_to_all | solution.py:45
  14.2 13.8 %collective-permute-start.4 = (bf16[512,128]{1,0:T(8,128)(2,1)S(1)}, bf16[512,128]{1,0:T(8,128)(2,1)S(1)}, u32[]{:S(2)}, u32[]{:S(2)}) collective-permute-start(bf16[512,128]{1,0:T(8,128)(2,1)S(1)} %bitcast.23), channel_id=1, source_target_pairs={{0,1},{1,0},{2,3},{3,2},{4,5},{5,4},{6,7},{7,6},{8,9},{9,8},{10,11... | collective-permute-start | bytes 393224 | tf_op jit(solution)/shard_map/ppermute | solution.py:37
  16.0 19.4 %collective-permute-start.6 = (bf16[128,3584]{1,0:T(8,128)(2,1)}, bf16[128,3584]{1,0:T(8,128)(2,1)S(1)}, u32[]{:S(2)}, u32[]{:S(2)}) collective-permute-start(bf16[128,3584]{1,0:T(8,128)(2,1)} %get-tuple-element.36.after), channel_id=1, source_target_pairs={{0,1},{1,0},{2,3},{3,2},{4,5},{5,4},{6,7},{7,6},{8,9},{9,8},{10,11... | collective-permute-start | bytes 2752520 | tf_op jit(solution)/shard_map/ppermute | solution.py:37
  16.3 19.0 %collective-permute-start = (bf16[2,3712]{1,0:T(2,128)(2,1)S(1)}, bf16[2,3712]{1,0:T(2,128)(2,1)S(1)}, u32[]{:S(2)}, u32[]{:S(2)}) collective-permute-start(bf16[2,3712]{1,0:T(2,128)(2,1)S(1)} %concatenate.34), channel_id=1, source_target_pairs={{0,1},{1,0},{2,3},{3,2},{4,5},{5,4},{6,7},{7,6},{8,9},{9,8},{10,11... | collective-permute-start | bytes 44552 | tf_op jit(solution)/shard_map/ppermute | solution.py:37
  22.7 7.7 %collective-permute-start.1 = (bf16[64,512]{1,0:T(8,128)(2,1)}, bf16[64,512]{1,0:T(8,128)(2,1)S(1)}, u32[]{:S(2)}, u32[]{:S(2)}) collective-permute-start(bf16[64,512]{1,0:T(8,128)(2,1)} %get-tuple-element.39), channel_id=1, source_target_pairs={{0,7},{3,0},{4,3},{7,4},{9,14},{10,9},{13,10},{14,13},{16,23},{19,... | collective-permute-start | bytes 196616 | tf_op jit(solution)/shard_map/ppermute | solution.py:41
  28.0 4.7 %collective-permute-start.2 = (bf16[64,512]{1,0:T(8,128)(2,1)S(1)}, bf16[64,512]{1,0:T(8,128)(2,1)S(1)}, u32[]{:S(2)}, u32[]{:S(2)}) collective-permute-start(bf16[64,512]{1,0:T(8,128)(2,1)S(1)} %get-tuple-element.40), channel_id=1, source_target_pairs={{0,4},{3,7},{4,0},{7,3},{9,13},{10,14},{13,9},{14,10},{16,20},{19,... | collective-permute-start | bytes 196616 | tf_op jit(solution)/shard_map/ppermute | solution.py:41
  28.1 5.6 %collective-permute-start.3 = (bf16[64,512]{1,0:T(8,128)(2,1)S(1)}, bf16[64,512]{1,0:T(8,128)(2,1)S(1)}, u32[]{:S(2)}, u32[]{:S(2)}) collective-permute-start(bf16[64,512]{1,0:T(8,128)(2,1)S(1)} %get-tuple-element.41), channel_id=1, source_target_pairs={{0,3},{3,4},{4,7},{7,0},{9,10},{10,13},{13,14},{14,9},{16,19},{19,... | collective-permute-start | bytes 196616 | tf_op jit(solution)/shard_map/ppermute | solution.py:41
  33.9 2.3 %collective-permute-start.5 = (bf16[128,256]{1,0:T(8,128)(2,1)S(1)}, bf16[128,256]{1,0:T(8,128)(2,1)S(1)}, u32[]{:S(2)}, u32[]{:S(2)}) collective-permute-start(bf16[128,256]{1,0:T(8,128)(2,1)S(1)} %values.1.mine), channel_id=1, source_target_pairs={{0,1},{1,0},{2,3},{3,2},{4,5},{5,4},{6,7},{7,6},{8,9},{9,8},{10,11... | collective-permute-start | bytes 196616 | tf_op jit(solution)/shard_map/ppermute | solution.py:37
  35.7 29.2 %copy-start.4 = (f32[3584]{0:T(1024)S(1)}, f32[3584]{0:T(1024)}, u32[]{:S(2)}) copy-start(f32[3584]{0:T(1024)} %get-tuple-element.66) | copy-start | bytes 43012
  37.0 5.8 %collective-permute-start.11 = (bf16[32,3584]{1,0:T(8,128)(2,1)S(1)}, bf16[32,3584]{1,0:T(8,128)(2,1)S(1)}, u32[]{:S(2)}, u32[]{:S(2)}) collective-permute-start(bf16[32,3584]{1,0:T(8,128)(2,1)S(1)} %get-tuple-element.48), channel_id=1, source_target_pairs={{0,7},{3,0},{4,3},{7,4},{9,14},{10,9},{13,10},{14,13},{16,23},{19,... | collective-permute-start | bytes 688136 | tf_op jit(solution)/shard_map/ppermute | solution.py:41
  37.1 51.2 %collective-permute-start.17 = (bf16[10752,256]{1,0:T(8,128)(2,1)}, bf16[10752,256]{1,0:T(8,128)(2,1)}, u32[]{:S(2)}, u32[]{:S(2)}) collective-permute-start(bf16[10752,256]{1,0:T(8,128)(2,1)} %get-tuple-element.49), channel_id=1, source_target_pairs={{0,1},{1,0},{2,3},{3,2},{4,5},{5,4},{6,7},{7,6},{8,9},{9,8},{10,11... | collective-permute-start | bytes 16515080 | tf_op jit(solution)/shard_map/ppermute | solution.py:37
  37.5 7.0 %collective-permute-start.7 = (bf16[32,3584]{1,0:T(8,128)(2,1)S(1)}, bf16[32,3584]{1,0:T(8,128)(2,1)S(1)}, u32[]{:S(2)}, u32[]{:S(2)}) collective-permute-start(bf16[32,3584]{1,0:T(8,128)(2,1)S(1)} %get-tuple-element.44), channel_id=1, source_target_pairs={{0,3},{3,4},{4,7},{7,0},{9,10},{10,13},{13,14},{14,9},{16,19},{19,... | collective-permute-start | bytes 688136 | tf_op jit(solution)/shard_map/ppermute | solution.py:41
  38.8 6.4 %collective-permute-start.10 = (bf16[32,3584]{1,0:T(8,128)(2,1)S(1)}, bf16[32,3584]{1,0:T(8,128)(2,1)S(1)}, u32[]{:S(2)}, u32[]{:S(2)}) collective-permute-start(bf16[32,3584]{1,0:T(8,128)(2,1)S(1)} %get-tuple-element.46), channel_id=1, source_target_pairs={{0,7},{3,0},{4,3},{7,4},{9,14},{10,9},{13,10},{14,13},{16,23},{19,... | collective-permute-start | bytes 688136 | tf_op jit(solution)/shard_map/ppermute | solution.py:41
  40.5 6.7 %collective-permute-start.9 = (bf16[32,3584]{1,0:T(8,128)(2,1)S(1)}, bf16[32,3584]{1,0:T(8,128)(2,1)S(1)}, u32[]{:S(2)}, u32[]{:S(2)}) collective-permute-start(bf16[32,3584]{1,0:T(8,128)(2,1)S(1)} %get-tuple-element.45), channel_id=1, source_target_pairs={{0,3},{3,4},{4,7},{7,0},{9,10},{10,13},{13,14},{14,9},{16,19},{19,... | collective-permute-start | bytes 688136 | tf_op jit(solution)/shard_map/ppermute | solution.py:41
  42.9 5.8 %collective-permute-start.12 = (bf16[32,3584]{1,0:T(8,128)(2,1)S(1)}, bf16[32,3584]{1,0:T(8,128)(2,1)S(1)}, u32[]{:S(2)}, u32[]{:S(2)}) collective-permute-start(bf16[32,3584]{1,0:T(8,128)(2,1)S(1)} %add_convert_fusion.4), channel_id=1, source_target_pairs={{0,7},{3,0},{4,3},{7,4},{9,14},{10,9},{13,10},{14,13},{16,23},{19,... | collective-permute-start | bytes 688136 | tf_op jit(solution)/shard_map/ppermute | solution.py:41
  44.6 6.7 %collective-permute-start.8 = (bf16[32,3584]{1,0:T(8,128)(2,1)S(1)}, bf16[32,3584]{1,0:T(8,128)(2,1)S(1)}, u32[]{:S(2)}, u32[]{:S(2)}) collective-permute-start(bf16[32,3584]{1,0:T(8,128)(2,1)S(1)} %add_convert_fusion.5), channel_id=1, source_target_pairs={{0,3},{3,4},{4,7},{7,0},{9,10},{10,13},{13,14},{14,9},{16,19},{19,... | collective-permute-start | bytes 688136 | tf_op jit(solution)/shard_map/ppermute | solution.py:41
  52.6 12.2 %all-to-all-start.1 = ((bf16[16,4,3584]{2,1,0:T(4,128)(2,1)}), bf16[16,4,3584]{2,1,0:T(4,128)(2,1)S(1)}, u32[]{:S(2)}, u32[]{:S(2)}) async-start(bf16[16,4,3584]{2,1,0:T(4,128)(2,1)} %bitcast.17), calls=%async_computation.1 | async-start | bytes 917504 | tf_op jit(solution)/shard_map/all_to_all | solution.py:45
  64.7 23.5 %copy-start = (bf16[1,7168,256]{2,1,0:T(8,128)(2,1)S(1)}, bf16[1,7168,256]{2,1,0:T(8,128)(2,1)}, u32[]{:S(2)}) copy-start(bf16[1,7168,256]{2,1,0:T(8,128)(2,1)} %param.21) | copy-start | bytes 11010052
  78.1 7.1 %collective-permute-start.15 = (bf16[32,3712]{1,0:T(8,128)(2,1)S(1)}, bf16[32,3712]{1,0:T(8,128)(2,1)S(1)}, u32[]{:S(2)}, u32[]{:S(2)}) collective-permute-start(bf16[32,3712]{1,0:T(8,128)(2,1)S(1)} %bitcast.36), channel_id=1, source_target_pairs={{0,3},{3,4},{4,7},{7,0},{9,10},{10,13},{13,14},{14,9},{16,19},{19,... | collective-permute-start | bytes 712712 | tf_op jit(solution)/shard_map/ppermute | solution.py:41
  78.9 6.3 %collective-permute-start.14 = (bf16[32,3712]{1,0:T(8,128)(2,1)S(1)}, bf16[32,3712]{1,0:T(8,128)(2,1)S(1)}, u32[]{:S(2)}, u32[]{:S(2)}) collective-permute-start(bf16[32,3712]{1,0:T(8,128)(2,1)S(1)} %bitcast.34), channel_id=1, source_target_pairs={{0,7},{3,0},{4,3},{7,4},{9,14},{10,9},{13,10},{14,13},{16,23},{19,... | collective-permute-start | bytes 712712 | tf_op jit(solution)/shard_map/ppermute | solution.py:41
  81.2 10.0 %collective-permute-start.13 = (bf16[32,3712]{1,0:T(8,128)(2,1)S(1)}, bf16[32,3712]{1,0:T(8,128)(2,1)S(1)}, u32[]{:S(2)}, u32[]{:S(2)}) collective-permute-start(bf16[32,3712]{1,0:T(8,128)(2,1)S(1)} %bitcast.37), channel_id=1, source_target_pairs={{0,7},{3,0},{4,3},{7,4},{9,14},{10,9},{13,10},{14,13},{16,23},{19,... | collective-permute-start | bytes 712712 | tf_op jit(solution)/shard_map/ppermute | solution.py:41
  81.5 9.7 %collective-permute-start.16 = (bf16[32,3712]{1,0:T(8,128)(2,1)S(1)}, bf16[32,3712]{1,0:T(8,128)(2,1)S(1)}, u32[]{:S(2)}, u32[]{:S(2)}) collective-permute-start(bf16[32,3712]{1,0:T(8,128)(2,1)S(1)} %bitcast.35), channel_id=1, source_target_pairs={{0,3},{3,4},{4,7},{7,0},{9,10},{10,13},{13,14},{14,9},{16,19},{19,... | collective-permute-start | bytes 712712 | tf_op jit(solution)/shard_map/ppermute | solution.py:41
  85.2 8.1 %collective-permute-start.18 = (bf16[32,3712]{1,0:T(8,128)(2,1)S(1)}, bf16[32,3712]{1,0:T(8,128)(2,1)S(1)}, u32[]{:S(2)}, u32[]{:S(2)}) collective-permute-start(bf16[32,3712]{1,0:T(8,128)(2,1)S(1)} %collective-permute-done.15.refs_3_), channel_id=1, source_target_pairs={{0,3},{3,4},{4,7},{7,0},{9,10},{10,13},{13,14},{14,9},{16,19},{19,... | collective-permute-start | bytes 712712 | tf_op jit(solution)/shard_map/ppermute | solution.py:41
  85.3 8.1 %collective-permute-start.19 = (bf16[32,3712]{1,0:T(8,128)(2,1)S(1)}, bf16[32,3712]{1,0:T(8,128)(2,1)S(1)}, u32[]{:S(2)}, u32[]{:S(2)}) collective-permute-start(bf16[32,3712]{1,0:T(8,128)(2,1)S(1)} %collective-permute-done.14.refs_2_), channel_id=1, source_target_pairs={{0,7},{3,0},{4,3},{7,4},{9,14},{10,9},{13,10},{14,13},{16,23},{19,... | collective-permute-start | bytes 712712 | tf_op jit(solution)/shard_map/ppermute | solution.py:41
  94.8 3.7 %collective-permute-start.20 = (bf16[256,1152]{1,0:T(8,128)(2,1)S(1)}, bf16[256,1152]{1,0:T(8,128)(2,1)S(1)}, u32[]{:S(2)}, u32[]{:S(2)}) collective-permute-start(bf16[256,1152]{1,0:T(8,128)(2,1)S(1)} %get-tuple-element.57), channel_id=1, source_target_pairs={{0,1},{1,0},{2,3},{3,2},{4,5},{5,4},{6,7},{7,6},{8,9},{9,8},{10,11... | collective-permute-start | bytes 1769480 | tf_op jit(solution)/shard_map/ppermute | solution.py:37
  100.4 5.8 %collective-permute-start.25 = (bf16[32,3584]{1,0:T(8,128)(2,1)S(1)}, bf16[32,3584]{1,0:T(8,128)(2,1)S(1)}, u32[]{:S(2)}, u32[]{:S(2)}) collective-permute-start(bf16[32,3584]{1,0:T(8,128)(2,1)S(1)} %get-tuple-element.64), channel_id=1, source_target_pairs={{0,7},{3,0},{4,3},{7,4},{9,14},{10,9},{13,10},{14,13},{16,23},{19,... | collective-permute-start | bytes 688136 | tf_op jit(solution)/shard_map/ppermute | solution.py:41
  102.7 7.0 %collective-permute-start.21 = (bf16[32,3584]{1,0:T(8,128)(2,1)S(1)}, bf16[32,3584]{1,0:T(8,128)(2,1)S(1)}, u32[]{:S(2)}, u32[]{:S(2)}) collective-permute-start(bf16[32,3584]{1,0:T(8,128)(2,1)S(1)} %get-tuple-element.60), channel_id=1, source_target_pairs={{0,3},{3,4},{4,7},{7,0},{9,10},{10,13},{13,14},{14,9},{16,19},{19,... | collective-permute-start | bytes 688136 | tf_op jit(solution)/shard_map/ppermute | solution.py:41
  102.7 9.1 %collective-permute-start.23 = (bf16[32,3584]{1,0:T(8,128)(2,1)S(1)}, bf16[32,3584]{1,0:T(8,128)(2,1)S(1)}, u32[]{:S(2)}, u32[]{:S(2)}) collective-permute-start(bf16[32,3584]{1,0:T(8,128)(2,1)S(1)} %get-tuple-element.61), channel_id=1, source_target_pairs={{0,3},{3,4},{4,7},{7,0},{9,10},{10,13},{13,14},{14,9},{16,19},{19,... | collective-permute-start | bytes 688136 | tf_op jit(solution)/shard_map/ppermute | solution.py:41
  102.7 9.1 %collective-permute-start.24 = (bf16[32,3584]{1,0:T(8,128)(2,1)S(1)}, bf16[32,3584]{1,0:T(8,128)(2,1)S(1)}, u32[]{:S(2)}, u32[]{:S(2)}) collective-permute-start(bf16[32,3584]{1,0:T(8,128)(2,1)S(1)} %get-tuple-element.62), channel_id=1, source_target_pairs={{0,7},{3,0},{4,3},{7,4},{9,14},{10,9},{13,10},{14,13},{16,23},{19,... | collective-permute-start | bytes 688136 | tf_op jit(solution)/shard_map/ppermute | solution.py:41
  106.3 6.2 %collective-permute-start.26 = (bf16[32,3584]{1,0:T(8,128)(2,1)S(1)}, bf16[32,3584]{1,0:T(8,128)(2,1)S(1)}, u32[]{:S(2)}, u32[]{:S(2)}) collective-permute-start(bf16[32,3584]{1,0:T(8,128)(2,1)S(1)} %add_convert_fusion.2), channel_id=1, source_target_pairs={{0,7},{3,0},{4,3},{7,4},{9,14},{10,9},{13,10},{14,13},{16,23},{19,... | collective-permute-start | bytes 688136 | tf_op jit(solution)/shard_map/ppermute | solution.py:41
  109.7 6.7 %collective-permute-start.22 = (bf16[32,3584]{1,0:T(8,128)(2,1)S(1)}, bf16[32,3584]{1,0:T(8,128)(2,1)S(1)}, u32[]{:S(2)}, u32[]{:S(2)}) collective-permute-start(bf16[32,3584]{1,0:T(8,128)(2,1)S(1)} %add_convert_fusion.3), channel_id=1, source_target_pairs={{0,3},{3,4},{4,7},{7,0},{9,10},{10,13},{13,14},{14,9},{16,19},{19,... | collective-permute-start | bytes 688136 | tf_op jit(solution)/shard_map/ppermute | solution.py:41
  128.9 2.4 %collective-permute-start.27 = (bf16[2,3584]{1,0:T(2,128)(2,1)S(1)}, bf16[2,3584]{1,0:T(2,128)(2,1)S(1)}, u32[]{:S(2)}, u32[]{:S(2)}) collective-permute-start(bf16[2,3584]{1,0:T(2,128)(2,1)S(1)} %get-tuple-element.72), channel_id=1, source_target_pairs={{0,1},{1,0},{2,3},{3,2},{4,5},{5,4},{6,7},{7,6},{8,9},{9,8},{10,11... | collective-permute-start | bytes 43016 | tf_op jit(solution)/shard_map/ppermute | solution.py:37
  (6 other events, 84.5 us)

commit v6 on v4

--- a/solution.py
+++ b/solution.py
@@ -167,17 +167,16 @@
     *arrays, out, sems = refs
     core = coordinates()[0]
     copies = []
-    for n, (which, part, rows, columns) in enumerate(places):
-        array = arrays[which]
-        if part == 0:
-            start = pl.multiple_of(core * out.shape[0], 128)
-            array = array.at[pl.ds(start, out.shape[0]), :]
-        elif part == 1:
-            start = pl.multiple_of(core * out.shape[1], 128)
-            array = array.at[:, pl.ds(start, out.shape[1])]
+    for n, (which, part, at, size) in enumerate(places):
+        axis, start = part
+        if axis is not None:
+            start = pl.multiple_of(core * out.shape[axis] + start, 128)
+        if axis == 1:
+            array = arrays[which].at[:, pl.ds(start, size[1])]
         else:
-            array = array.at[part, :]
-        copies.append(pltpu.make_async_copy(array, out.at[rows, columns], sems.at[n]))
+            array = arrays[which].at[pl.ds(start, size[0]), :]
+        spot = out.at[pl.ds(at[0], size[0]), pl.ds(at[1], size[1])]
+        copies.append(pltpu.make_async_copy(array, spot, sems.at[n]))
     for copy in copies:
         copy.start()
     for copy in copies:
@@ -446,10 +445,13 @@
     )(plane(sent), mark)
     blocks = exchange(blocks)
     out_other = swap(out_other)
-    every = slice(None)
+    quarter = half // 4
     w_out = load(
         (w_out, out_other),
-        ((0, 1, slice(0, VHEAD), every), (1, every, slice(VHEAD, 2 * VHEAD), every)),
+        (
+            *((0, (1, n), (0, n), (VHEAD, quarter)) for n in range(0, half, quarter)),
+            (1, (None, 0), (VHEAD, 0), (VHEAD, half)),
+        ),
         (2 * VHEAD, half),
         "load_out",
         8,
@@ -489,11 +491,15 @@
     scaled = (mixed * own(gain, 0)).astype(BF16)
     w_gu = load(
         (w_gate[0], w_up[0], packed),
-        (
-            (0, 0, every, slice(0, 256)),
-            (1, 0, every, slice(256, 512)),
-            (2, slice(0, half), every, slice(512, 768)),
-            (2, slice(half, 2 * half), every, slice(768, 1024)),
+        tuple(
+            place
+            for n in range(0, half, quarter)
+            for place in (
+                (0, (0, n), (n, 0), (quarter, 256)),
+                (1, (0, n), (n, 256), (quarter, 256)),
+                (2, (None, n), (n, 512), (quarter, 256)),
+                (2, (None, half + n), (n, 768), (quarter, 256)),
+            )
         ),
         (half, 1024),
         "load_gate_up",
@@ -506,11 +512,8 @@
     w_down = load(
         (w_down[0], packed),
         (
-            (0, 1, slice(0, 256), every),
-            *(
-                (1, slice(2 * half + n, 2 * half + n + 256), slice(256, 512), slice(n, n + 256))
-                for n in range(0, half, 256)
-            ),
+            *((0, (1, n), (0, n), (256, quarter)) for n in range(0, half, quarter)),
+            *((1, (None, 2 * half + n), (256, n), (256, 256)) for n in range(0, half, 256)),
         ),
         (512, half),
         "load_down",

time: 132 us -> 132 us (level)
  no operation moved by 1% of the time
where the time goes in v6:
time: 132 us; the launch traced here: 131 us
  starting transfers between devices  45.7 us (35%)
  waiting for transfers between devices  34.3 us (26%)
  blocking collectives  24.3 us (18%)
  Pallas kernels  22.7 us (17%)
  local copies, waits for them, and re-layouts  2.35 us (2%)
  other arithmetic  1.79 us (1%)
    ppermute x21, starting transfers between devices, ahead(): lax.ppermute(a, AXES, [(r[i], r[(i + step) % 4]) for r in RINGS for i in...  26.9 us
    all_to_all x2, blocking collectives, plane(): return lax.all_to_all(a, AXES, 0, 0, axis_index_groups=PLANES, tiled=True)  24.3 us
    ppermute x21, waiting for transfers between devices, ahead(): lax.ppermute(a, AXES, [(r[i], r[(i + step) % 4]) for r in RINGS for i in...  23.6 us
    all_to_all x2, starting transfers between devices, plane(): return lax.all_to_all(a, AXES, 0, 0, axis_index_groups=PLANES, tiled=True)  10.2 us
    all_to_all x2, waiting for transfers between devices, plane(): return lax.all_to_all(a, AXES, 0, 0, axis_index_groups=PLANES, tiled=True)  9.45 us
    ppermute x7, starting transfers between devices, swap(): return lax.ppermute(a, AXES, SIBLING)  8.57 us
    pallas_call x1, Pallas kernels, attend(): pl.pallas_call(attend_kernel, in_specs=[pl.BlockSpec(memory_space=pltpu.S...  6.45 us
    pallas_call x5, Pallas kernels, call(): pl.pallas_call(kernel, in_specs=[VMEM] * len(args), out_specs=[VMEM] * le...  6.42 us
  transfers between devices with their start and end apart: 30, of which 19 were waited for; matrix products, arithmetic and copies ran while one was open for 2% of the time, Pallas kernels for 9%

profile of v6, /device:TPU:1, one launch (start us, length us, event | category | flops | bytes accessed | tf_op | source)
XLA Modules:
  0.0 131.5 jit_solution(14952503986566965665)
XLA Ops:
  0.0 6.4 %attend.1 = (bf16[16,16,512]{2,1,0:T(8,128)(2,1)}, bf16[128,3584]{1,0:T(8,128)(2,1)}) custom-call(s32[2]{0:T(128)} %lens.1, bf16[2,576,128]{2,1,0:T(8,128)(2,1)} %bitcast.33, bf16[2,576,2048]{2,1,0:T(8,128)(2,1)} %bitcast.27, bf16[128,7168]{1,0:T(8,128)(2,1)} %refs_0_.1), custom_call_target="tpu_custom_call" | custom-call | tf_op jit(solution)/shard_map/attend/pallas_call | solution.py:142
  6.5 1.5 %collective-permute-start.6 = (bf16[128,3584]{1,0:T(8,128)(2,1)}, bf16[128,3584]{1,0:T(8,128)(2,1)S(1)}, u32[]{:S(2)}, u32[]{:S(2)}) collective-permute-start(bf16[128,3584]{1,0:T(8,128)(2,1)} %get-tuple-element.36.after), channel_id=1, source_target_pairs={{0,1},{1,0},{2,3},{3,2},{4,5},{5,4},{6,7},{7,6},{8,9},{9,8},{10,11... | collective-permute-start | bytes 2752520 | tf_op jit(solution)/shard_map/ppermute | solution.py:37
  8.0 6.7 %all-to-all-start = ((bf16[16,16,512]{2,1,0:T(8,128)(2,1)}), bf16[16,16,512]{2,1,0:T(8,128)(2,1)S(1)}, u32[]{:S(2)}, u32[]{:S(2)}) async-start(bf16[16,16,512]{2,1,0:T(8,128)(2,1)} %get-tuple-element.35), calls=%async_computation | async-start | bytes 524288 | tf_op jit(solution)/shard_map/all_to_all | solution.py:45
  14.6 1.5 %collective-permute-start.4 = (bf16[512,128]{1,0:T(8,128)(2,1)S(1)}, bf16[512,128]{1,0:T(8,128)(2,1)S(1)}, u32[]{:S(2)}, u32[]{:S(2)}) collective-permute-start(bf16[512,128]{1,0:T(8,128)(2,1)S(1)} %bitcast.23), channel_id=1, source_target_pairs={{0,1},{1,0},{2,3},{3,2},{4,5},{5,4},{6,7},{7,6},{8,9},{9,8},{10,11... | collective-permute-start | bytes 393224 | tf_op jit(solution)/shard_map/ppermute | solution.py:37
  16.1 4.5 %pack.1 = (bf16[10752,256]{1,0:T(8,128)(2,1)}, f32[8,128]{1,0:T(8,128)S(1)}) custom-call(bf16[7168,256]{1,0:T(8,128)(2,1)} %bitcast.18, bf16[7168,256]{1,0:T(8,128)(2,1)} %bitcast.25, bf16[256,7168]{1,0:T(8,128)(2,1)} %bitcast.20, bf16[128,3584]{1,0:T(8,128)(2,1)} %get-tuple-element.36.after), custom_call_target="tpu_custom_call" | custom-call | bytes 12582912 | tf_op jit(solution)/shard_map/pack/pallas_call | solution.py:232
  20.6 1.7 %all-to-all-done.got = bf16[16,16,512]{2,1,0:T(8,128)(2,1)S(1)} async-done(((bf16[16,16,512]{2,1,0:T(8,128)(2,1)}), bf16[16,16,512]{2,1,0:T(8,128)(2,1)S(1)}, u32[]{:S(2)}, u32[]{:S(2)}) %all-to-all-start) | async-done | bytes 262176 | tf_op jit(solution)/shard_map/all_to_all | solution.py:45
  22.6 5.2 %collective-permute-start.1 = (bf16[64,512]{1,0:T(8,128)(2,1)S(1)}, bf16[64,512]{1,0:T(8,128)(2,1)S(1)}, u32[]{:S(2)}, u32[]{:S(2)}) collective-permute-start(bf16[64,512]{1,0:T(8,128)(2,1)S(1)} %get-tuple-element.39), channel_id=1, source_target_pairs={{0,7},{3,0},{4,3},{7,4},{9,14},{10,9},{13,10},{14,13},{16,23},{19,... | collective-permute-start | bytes 196616 | tf_op jit(solution)/shard_map/ppermute | solution.py:41
  29.1 3.3 %collective-permute-done.2.p2 = bf16[64,512]{1,0:T(8,128)(2,1)S(1)} collective-permute-done((bf16[64,512]{1,0:T(8,128)(2,1)S(1)}, bf16[64,512]{1,0:T(8,128)(2,1)S(1)}, u32[]{:S(2)}, u32[]{:S(2)}) %collective-permute-start.2) | collective-permute-done | bytes 65568 | tf_op jit(solution)/shard_map/ppermute | solution.py:41
  38.3 1.7 %collective-permute-start.10 = (bf16[32,3584]{1,0:T(8,128)(2,1)S(1)}, bf16[32,3584]{1,0:T(8,128)(2,1)S(1)}, u32[]{:S(2)}, u32[]{:S(2)}) collective-permute-start(bf16[32,3584]{1,0:T(8,128)(2,1)S(1)} %get-tuple-element.46), channel_id=1, source_target_pairs={{0,7},{3,0},{4,3},{7,4},{9,14},{10,9},{13,10},{14,13},{16,23},{19,... | collective-permute-start | bytes 688136 | tf_op jit(solution)/shard_map/ppermute | solution.py:41
  40.1 2.2 %collective-permute-done.11 = bf16[32,3584]{1,0:T(8,128)(2,1)S(1)} collective-permute-done((bf16[32,3584]{1,0:T(8,128)(2,1)S(1)}, bf16[32,3584]{1,0:T(8,128)(2,1)S(1)}, u32[]{:S(2)}, u32[]{:S(2)}) %collective-permute-start.11) | collective-permute-done | bytes 229408 | tf_op jit(solution)/shard_map/ppermute | solution.py:41
  44.8 1.9 %collective-permute-done.9 = bf16[32,3584]{1,0:T(8,128)(2,1)S(1)} collective-permute-done((bf16[32,3584]{1,0:T(8,128)(2,1)S(1)}, bf16[32,3584]{1,0:T(8,128)(2,1)S(1)}, u32[]{:S(2)}, u32[]{:S(2)}) %collective-permute-start.9) | collective-permute-done | bytes 229408 | tf_op jit(solution)/shard_map/ppermute | solution.py:41
  46.6 1.5 %collective-permute-done.12 = bf16[32,3584]{1,0:T(8,128)(2,1)S(1)} collective-permute-done((bf16[32,3584]{1,0:T(8,128)(2,1)S(1)}, bf16[32,3584]{1,0:T(8,128)(2,1)S(1)}, u32[]{:S(2)}, u32[]{:S(2)}) %collective-permute-start.12) | collective-permute-done | bytes 229408 | tf_op jit(solution)/shard_map/ppermute | solution.py:41
  48.2 2.6 %collective-permute-done.8 = bf16[32,3584]{1,0:T(8,128)(2,1)S(1)} collective-permute-done((bf16[32,3584]{1,0:T(8,128)(2,1)S(1)}, bf16[32,3584]{1,0:T(8,128)(2,1)S(1)}, u32[]{:S(2)}, u32[]{:S(2)}) %collective-permute-start.8) | collective-permute-done | bytes 229408 | tf_op jit(solution)/shard_map/ppermute | solution.py:41
  52.0 3.6 %all-to-all-start.1 = ((bf16[16,4,3584]{2,1,0:T(4,128)(2,1)}), bf16[16,4,3584]{2,1,0:T(4,128)(2,1)S(1)}, u32[]{:S(2)}, u32[]{:S(2)}) async-start(bf16[16,4,3584]{2,1,0:T(4,128)(2,1)} %bitcast.17), calls=%async_computation.1 | async-start | bytes 917504 | tf_op jit(solution)/shard_map/all_to_all | solution.py:45
  56.5 7.7 %all-to-all-done.1 = bf16[16,4,3584]{2,1,0:T(4,128)(2,1)S(1)} async-done(((bf16[16,4,3584]{2,1,0:T(4,128)(2,1)}), bf16[16,4,3584]{2,1,0:T(4,128)(2,1)S(1)}, u32[]{:S(2)}, u32[]{:S(2)}) %all-to-all-start.1) | async-done | bytes 458784 | tf_op jit(solution)/shard_map/all_to_all | solution.py:45
  64.6 12.6 %all_to_all.20 = bf16[16,4,3712]{2,1,0:T(4,128)(2,1)S(1)} all-to-all(bf16[16,4,3712]{2,1,0:T(4,128)(2,1)S(1)} %broadcast_in_dim.8), channel_id=1, replica_groups={{0,9,16,25,32,41,48,57,64,73,80,89,96,105,112,121},{3,10,19,26,35,42,51..., dimensions={0} | all-to-all | bytes 950272 | tf_op jit(solution)/shard_map/all_to_all | solution.py:45
  78.4 2.2 %collective-permute-start.14 = (bf16[32,3712]{1,0:T(8,128)(2,1)S(1)}, bf16[32,3712]{1,0:T(8,128)(2,1)S(1)}, u32[]{:S(2)}, u32[]{:S(2)}) collective-permute-start(bf16[32,3712]{1,0:T(8,128)(2,1)S(1)} %bitcast.34), channel_id=1, source_target_pairs={{0,7},{3,0},{4,3},{7,4},{9,14},{10,9},{13,10},{14,13},{16,23},{19,... | collective-permute-start | bytes 712712 | tf_op jit(solution)/shard_map/ppermute | solution.py:41
  82.4 2.3 %collective-permute-done.15.refs_3_ = bf16[32,3712]{1,0:T(8,128)(2,1)S(1)} collective-permute-done((bf16[32,3712]{1,0:T(8,128)(2,1)S(1)}, bf16[32,3712]{1,0:T(8,128)(2,1)S(1)}, u32[]{:S(2)}, u32[]{:S(2)}) %collective-permute-start.15) | collective-permute-done | bytes 237600 | tf_op jit(solution)/shard_map/ppermute | solution.py:41
  84.7 3.0 %collective-permute-start.19 = (bf16[32,3712]{1,0:T(8,128)(2,1)S(1)}, bf16[32,3712]{1,0:T(8,128)(2,1)S(1)}, u32[]{:S(2)}, u32[]{:S(2)}) collective-permute-start(bf16[32,3712]{1,0:T(8,128)(2,1)S(1)} %collective-permute-done.14.refs_2_), channel_id=1, source_target_pairs={{0,7},{3,0},{4,3},{7,4},{9,14},{10,9},{13,10},{14,13},{16,23},{19,... | collective-permute-start | bytes 712712 | tf_op jit(solution)/shard_map/ppermute | solution.py:41
  87.8 2.8 %load_gate_up.1.refs_6_.refs_4_ = bf16[3584,1024]{1,0:T(8,128)(2,1)S(1)} custom-call(bf16[7168,256]{1,0:T(8,128)(2,1)S(1)} %bitcast.19, bf16[7168,256]{1,0:T(8,128)(2,1)} %bitcast.26, bf16[10752,256]{1,0:T(8,128)(2,1)} %collective-permute-done.17.refs_2_.refs_1_), custom_call_target="tpu_custom_call" | custom-call | bytes 14680064 | tf_op jit(solution)/shard_map/load_gate_up/pallas_call | solution.py:188
  90.6 2.1 %gate_up.2 = (f32[192,1024]{1,0:T(8,128)S(1)}, bf16[192,1152]{1,0:T(8,128)(2,1)S(1)}, f32[192,1]{1,0:T(8,128)S(1)}, f32[192,1]{1,0:T(8,128)S(1)}) custom-call(bf16[64,3712]{1,0:T(8,128)(2,1)S(1)} %bitcast.22, bf16[32,3712]{1,0:T(8,128)(2,1)S(1)} %collective-permute-done.13.refs_1_, bf16[32,3712]{1,0:T(8,128)(2,1)S(1)} %collective-permute-done.14.refs_2_, ...), custom_call_target="tpu_custom_call" | custom-call | flops 1610612736 | bytes 1048576 | tf_op jit(solution)/shard_map/gate_up/pallas_call | solution.py:248
  92.7 1.5 %gate_up.3 = (f32[64,1024]{1,0:T(8,128)S(1)}, bf16[256,1152]{1,0:T(8,128)(2,1)S(1)}, f32[64,1]{1,0:T(8,128)S(1)}, f32[64,1]{1,0:T(8,128)S(1)}) custom-call(bf16[192,1152]{1,0:T(8,128)(2,1)S(1)} %get-tuple-element.53.refs_0_, bf16[32,3712]{1,0:T(8,128)(2,1)S(1)} %collective-permute-done.18.refs_1_, bf16[32,3712]{1,0:T(8,128)(2,1)S(1)} %collective-permute-done.19.refs_2_, ...), custom_call_target="tpu_custom_call" | custom-call | flops 536870912 | bytes 1048576 | tf_op jit(solution)/shard_map/gate_up/pallas_call | solution.py:248
  94.2 1.9 %collective-permute-start.20 = (bf16[256,1152]{1,0:T(8,128)(2,1)S(1)}, bf16[256,1152]{1,0:T(8,128)(2,1)S(1)}, u32[]{:S(2)}, u32[]{:S(2)}) collective-permute-start(bf16[256,1152]{1,0:T(8,128)(2,1)S(1)} %get-tuple-element.57), channel_id=1, source_target_pairs={{0,1},{1,0},{2,3},{3,2},{4,5},{5,4},{6,7},{7,6},{8,9},{9,8},{10,11... | collective-permute-start | bytes 1769480 | tf_op jit(solution)/shard_map/ppermute | solution.py:37
  96.1 1.9 %load_down.1.w = bf16[512,3584]{1,0:T(8,128)(2,1)S(1)} custom-call(bf16[256,7168]{1,0:T(8,128)(2,1)S(1)} %bitcast.21, bf16[10752,256]{1,0:T(8,128)(2,1)} %collective-permute-done.17.refs_2_.refs_1_), custom_call_target="tpu_custom_call" | custom-call | bytes 7340032 | tf_op jit(solution)/shard_map/load_down/pallas_call | solution.py:188
  98.0 1.8 %down.1 = (bf16[64,3584]{1,0:T(8,128)(2,1)S(1)}, bf16[32,3584]{1,0:T(8,128)(2,1)S(1)}, bf16[32,3584]{1,0:T(8,128)(2,1)S(1)}, bf16[32,3584]{1,0:T(8,128)(2,1)S(1)...) custom-call(f32[192,1024]{1,0:T(8,128)S(1)} %get-tuple-element.50.p0, ...), custom_call_target="tpu_custom_call" | custom-call | flops 1073741824 | bytes 1048576 | tf_op jit(solution)/shard_map/down/pallas_call | solution.py:248
  99.8 2.3 %collective-permute-start.25 = (bf16[32,3584]{1,0:T(8,128)(2,1)S(1)}, bf16[32,3584]{1,0:T(8,128)(2,1)S(1)}, u32[]{:S(2)}, u32[]{:S(2)}) collective-permute-start(bf16[32,3584]{1,0:T(8,128)(2,1)S(1)} %get-tuple-element.64), channel_id=1, source_target_pairs={{0,7},{3,0},{4,3},{7,4},{9,14},{10,9},{13,10},{14,13},{16,23},{19,... | collective-permute-start | bytes 688136 | tf_op jit(solution)/shard_map/ppermute | solution.py:41
  102.2 3.0 %collective-permute-start.24 = (bf16[32,3584]{1,0:T(8,128)(2,1)S(1)}, bf16[32,3584]{1,0:T(8,128)(2,1)S(1)}, u32[]{:S(2)}, u32[]{:S(2)}) collective-permute-start(bf16[32,3584]{1,0:T(8,128)(2,1)S(1)} %get-tuple-element.62), channel_id=1, source_target_pairs={{0,7},{3,0},{4,3},{7,4},{9,14},{10,9},{13,10},{14,13},{16,23},{19,... | collective-permute-start | bytes 688136 | tf_op jit(solution)/shard_map/ppermute | solution.py:41
  105.7 3.3 %collective-permute-start.26 = (bf16[32,3584]{1,0:T(8,128)(2,1)S(1)}, bf16[32,3584]{1,0:T(8,128)(2,1)S(1)}, u32[]{:S(2)}, u32[]{:S(2)}) collective-permute-start(bf16[32,3584]{1,0:T(8,128)(2,1)S(1)} %add_convert_fusion.2), channel_id=1, source_target_pairs={{0,7},{3,0},{4,3},{7,4},{9,14},{10,9},{13,10},{14,13},{16,23},{19,... | collective-permute-start | bytes 688136 | tf_op jit(solution)/shard_map/ppermute | solution.py:41
  109.3 2.0 %collective-permute-done.23 = bf16[32,3584]{1,0:T(8,128)(2,1)S(1)} collective-permute-done((bf16[32,3584]{1,0:T(8,128)(2,1)S(1)}, bf16[32,3584]{1,0:T(8,128)(2,1)S(1)}, u32[]{:S(2)}, u32[]{:S(2)}) %collective-permute-start.23) | collective-permute-done | bytes 229408 | tf_op jit(solution)/shard_map/ppermute | solution.py:41
  111.9 4.0 %collective-permute-done.22 = bf16[32,3584]{1,0:T(8,128)(2,1)S(1)} collective-permute-done((bf16[32,3584]{1,0:T(8,128)(2,1)S(1)}, bf16[32,3584]{1,0:T(8,128)(2,1)S(1)}, u32[]{:S(2)}, u32[]{:S(2)}) %collective-permute-start.22) | collective-permute-done | bytes 229408 | tf_op jit(solution)/shard_map/ppermute | solution.py:41
  116.4 11.7 %all_to_all.21 = bf16[16,4,3584]{2,1,0:T(4,128)(2,1)S(1)} all-to-all(bf16[16,4,3584]{2,1,0:T(4,128)(2,1)S(1)} %bitcast.32), channel_id=1, replica_groups={{0,9,16,25,32,41,48,57,64,73,80,89,96,105,112,121},{3,10,19,26,35,42,51..., dimensions={0} | all-to-all | bytes 917504 | tf_op jit(solution)/shard_map/all_to_all | solution.py:45
  128.4 1.6 %collective-permute-start.27 = (bf16[2,3584]{1,0:T(2,128)(2,1)S(1)}, bf16[2,3584]{1,0:T(2,128)(2,1)S(1)}, u32[]{:S(2)}, u32[]{:S(2)}) collective-permute-start(bf16[2,3584]{1,0:T(2,128)(2,1)S(1)} %get-tuple-element.72), channel_id=1, source_target_pairs={{0,1},{1,0},{2,3},{3,2},{4,5},{5,4},{6,7},{7,6},{8,9},{9,8},{10,11... | collective-permute-start | bytes 43016 | tf_op jit(solution)/shard_map/ppermute | solution.py:37
  (85 shorter events, 19.2 us)
Async XLA Ops:
  6.5 28.3 %collective-permute-start.6 = (bf16[128,3584]{1,0:T(8,128)(2,1)}, bf16[128,3584]{1,0:T(8,128)(2,1)S(1)}, u32[]{:S(2)}, u32[]{:S(2)}) collective-permute-start(bf16[128,3584]{1,0:T(8,128)(2,1)} %get-tuple-element.36.after), channel_id=1, source_target_pairs={{0,1},{1,0},{2,3},{3,2},{4,5},{5,4},{6,7},{7,6},{8,9},{9,8},{10,11... | collective-permute-start | bytes 2752520 | tf_op jit(solution)/shard_map/ppermute | solution.py:37
  8.0 14.4 %all-to-all-start = ((bf16[16,16,512]{2,1,0:T(8,128)(2,1)}), bf16[16,16,512]{2,1,0:T(8,128)(2,1)S(1)}, u32[]{:S(2)}, u32[]{:S(2)}) async-start(bf16[16,16,512]{2,1,0:T(8,128)(2,1)} %get-tuple-element.35), calls=%async_computation | async-start | bytes 524288 | tf_op jit(solution)/shard_map/all_to_all | solution.py:45
  14.6 14.1 %collective-permute-start.4 = (bf16[512,128]{1,0:T(8,128)(2,1)S(1)}, bf16[512,128]{1,0:T(8,128)(2,1)S(1)}, u32[]{:S(2)}, u32[]{:S(2)}) collective-permute-start(bf16[512,128]{1,0:T(8,128)(2,1)S(1)} %bitcast.23), channel_id=1, source_target_pairs={{0,1},{1,0},{2,3},{3,2},{4,5},{5,4},{6,7},{7,6},{8,9},{9,8},{10,11... | collective-permute-start | bytes 393224 | tf_op jit(solution)/shard_map/ppermute | solution.py:37
  22.6 6.5 %collective-permute-start.1 = (bf16[64,512]{1,0:T(8,128)(2,1)S(1)}, bf16[64,512]{1,0:T(8,128)(2,1)S(1)}, u32[]{:S(2)}, u32[]{:S(2)}) collective-permute-start(bf16[64,512]{1,0:T(8,128)(2,1)S(1)} %get-tuple-element.39), channel_id=1, source_target_pairs={{0,7},{3,0},{4,3},{7,4},{9,14},{10,9},{13,10},{14,13},{16,23},{19,... | collective-permute-start | bytes 196616 | tf_op jit(solution)/shard_map/ppermute | solution.py:41
  27.7 4.7 %collective-permute-start.2 = (bf16[64,512]{1,0:T(8,128)(2,1)S(1)}, bf16[64,512]{1,0:T(8,128)(2,1)S(1)}, u32[]{:S(2)}, u32[]{:S(2)}) collective-permute-start(bf16[64,512]{1,0:T(8,128)(2,1)S(1)} %get-tuple-element.40), channel_id=1, source_target_pairs={{0,4},{3,7},{4,0},{7,3},{9,13},{10,14},{13,9},{14,10},{16,20},{19,... | collective-permute-start | bytes 196616 | tf_op jit(solution)/shard_map/ppermute | solution.py:41
  27.8 5.6 %collective-permute-start.3 = (bf16[64,512]{1,0:T(8,128)(2,1)S(1)}, bf16[64,512]{1,0:T(8,128)(2,1)S(1)}, u32[]{:S(2)}, u32[]{:S(2)}) collective-permute-start(bf16[64,512]{1,0:T(8,128)(2,1)S(1)} %get-tuple-element.41), channel_id=1, source_target_pairs={{0,3},{3,4},{4,7},{7,0},{9,10},{10,13},{13,14},{14,9},{16,19},{19,... | collective-permute-start | bytes 196616 | tf_op jit(solution)/shard_map/ppermute | solution.py:41
  33.6 2.1 %collective-permute-start.5 = (bf16[128,256]{1,0:T(8,128)(2,1)S(1)}, bf16[128,256]{1,0:T(8,128)(2,1)S(1)}, u32[]{:S(2)}, u32[]{:S(2)}) collective-permute-start(bf16[128,256]{1,0:T(8,128)(2,1)S(1)} %values.1.mine), channel_id=1, source_target_pairs={{0,1},{1,0},{2,3},{3,2},{4,5},{5,4},{6,7},{7,6},{8,9},{9,8},{10,11... | collective-permute-start | bytes 196616 | tf_op jit(solution)/shard_map/ppermute | solution.py:37
  35.2 21.2 %copy-start.5 = (f32[7168]{0:T(1024)S(1)}, f32[7168]{0:T(1024)}, u32[]{:S(2)}) copy-start(f32[7168]{0:T(1024)} %param.18) | copy-start | bytes 86020
  36.5 5.8 %collective-permute-start.11 = (bf16[32,3584]{1,0:T(8,128)(2,1)S(1)}, bf16[32,3584]{1,0:T(8,128)(2,1)S(1)}, u32[]{:S(2)}, u32[]{:S(2)}) collective-permute-start(bf16[32,3584]{1,0:T(8,128)(2,1)S(1)} %get-tuple-element.48), channel_id=1, source_target_pairs={{0,7},{3,0},{4,3},{7,4},{9,14},{10,9},{13,10},{14,13},{16,23},{19,... | collective-permute-start | bytes 688136 | tf_op jit(solution)/shard_map/ppermute | solution.py:41
  36.6 51.2 %collective-permute-start.17 = (bf16[10752,256]{1,0:T(8,128)(2,1)}, bf16[10752,256]{1,0:T(8,128)(2,1)}, u32[]{:S(2)}, u32[]{:S(2)}) collective-permute-start(bf16[10752,256]{1,0:T(8,128)(2,1)} %get-tuple-element.49), channel_id=1, source_target_pairs={{0,1},{1,0},{2,3},{3,2},{4,5},{5,4},{6,7},{7,6},{8,9},{9,8},{10,11... | collective-permute-start | bytes 16515080 | tf_op jit(solution)/shard_map/ppermute | solution.py:37
  37.0 7.0 %collective-permute-start.7 = (bf16[32,3584]{1,0:T(8,128)(2,1)S(1)}, bf16[32,3584]{1,0:T(8,128)(2,1)S(1)}, u32[]{:S(2)}, u32[]{:S(2)}) collective-permute-start(bf16[32,3584]{1,0:T(8,128)(2,1)S(1)} %get-tuple-element.44), channel_id=1, source_target_pairs={{0,3},{3,4},{4,7},{7,0},{9,10},{10,13},{13,14},{14,9},{16,19},{19,... | collective-permute-start | bytes 688136 | tf_op jit(solution)/shard_map/ppermute | solution.py:41
  38.3 6.4 %collective-permute-start.10 = (bf16[32,3584]{1,0:T(8,128)(2,1)S(1)}, bf16[32,3584]{1,0:T(8,128)(2,1)S(1)}, u32[]{:S(2)}, u32[]{:S(2)}) collective-permute-start(bf16[32,3584]{1,0:T(8,128)(2,1)S(1)} %get-tuple-element.46), channel_id=1, source_target_pairs={{0,7},{3,0},{4,3},{7,4},{9,14},{10,9},{13,10},{14,13},{16,23},{19,... | collective-permute-start | bytes 688136 | tf_op jit(solution)/shard_map/ppermute | solution.py:41
  40.0 6.7 %collective-permute-start.9 = (bf16[32,3584]{1,0:T(8,128)(2,1)S(1)}, bf16[32,3584]{1,0:T(8,128)(2,1)S(1)}, u32[]{:S(2)}, u32[]{:S(2)}) collective-permute-start(bf16[32,3584]{1,0:T(8,128)(2,1)S(1)} %get-tuple-element.45), channel_id=1, source_target_pairs={{0,3},{3,4},{4,7},{7,0},{9,10},{10,13},{13,14},{14,9},{16,19},{19,... | collective-permute-start | bytes 688136 | tf_op jit(solution)/shard_map/ppermute | solution.py:41
  42.4 5.8 %collective-permute-start.12 = (bf16[32,3584]{1,0:T(8,128)(2,1)S(1)}, bf16[32,3584]{1,0:T(8,128)(2,1)S(1)}, u32[]{:S(2)}, u32[]{:S(2)}) collective-permute-start(bf16[32,3584]{1,0:T(8,128)(2,1)S(1)} %add_convert_fusion.4), channel_id=1, source_target_pairs={{0,7},{3,0},{4,3},{7,4},{9,14},{10,9},{13,10},{14,13},{16,23},{19,... | collective-permute-start | bytes 688136 | tf_op jit(solution)/shard_map/ppermute | solution.py:41
  44.0 6.7 %collective-permute-start.8 = (bf16[32,3584]{1,0:T(8,128)(2,1)S(1)}, bf16[32,3584]{1,0:T(8,128)(2,1)S(1)}, u32[]{:S(2)}, u32[]{:S(2)}) collective-permute-start(bf16[32,3584]{1,0:T(8,128)(2,1)S(1)} %add_convert_fusion.5), channel_id=1, source_target_pairs={{0,3},{3,4},{4,7},{7,0},{9,10},{10,13},{13,14},{14,9},{16,19},{19,... | collective-permute-start | bytes 688136 | tf_op jit(solution)/shard_map/ppermute | solution.py:41
  52.0 12.2 %all-to-all-start.1 = ((bf16[16,4,3584]{2,1,0:T(4,128)(2,1)}), bf16[16,4,3584]{2,1,0:T(4,128)(2,1)S(1)}, u32[]{:S(2)}, u32[]{:S(2)}) async-start(bf16[16,4,3584]{2,1,0:T(4,128)(2,1)} %bitcast.17), calls=%async_computation.1 | async-start | bytes 917504 | tf_op jit(solution)/shard_map/all_to_all | solution.py:45
  55.8 8.6 %collective-permute-start = (bf16[2,3712]{1,0:T(2,128)(2,1)S(1)}, bf16[2,3712]{1,0:T(2,128)(2,1)S(1)}, u32[]{:S(2)}, u32[]{:S(2)}) collective-permute-start(bf16[2,3712]{1,0:T(2,128)(2,1)S(1)} %concatenate.34), channel_id=1, source_target_pairs={{0,1},{1,0},{2,3},{3,2},{4,5},{5,4},{6,7},{7,6},{8,9},{9,8},{10,11... | collective-permute-start | bytes 44552 | tf_op jit(solution)/shard_map/ppermute | solution.py:37
  64.2 23.6 %copy-start = (bf16[1,7168,256]{2,1,0:T(8,128)(2,1)S(1)}, bf16[1,7168,256]{2,1,0:T(8,128)(2,1)}, u32[]{:S(2)}) copy-start(bf16[1,7168,256]{2,1,0:T(8,128)(2,1)} %param.21) | copy-start | bytes 11010052
  77.6 7.1 %collective-permute-start.15 = (bf16[32,3712]{1,0:T(8,128)(2,1)S(1)}, bf16[32,3712]{1,0:T(8,128)(2,1)S(1)}, u32[]{:S(2)}, u32[]{:S(2)}) collective-permute-start(bf16[32,3712]{1,0:T(8,128)(2,1)S(1)} %bitcast.36), channel_id=1, source_target_pairs={{0,3},{3,4},{4,7},{7,0},{9,10},{10,13},{13,14},{14,9},{16,19},{19,... | collective-permute-start | bytes 712712 | tf_op jit(solution)/shard_map/ppermute | solution.py:41
  78.4 6.3 %collective-permute-start.14 = (bf16[32,3712]{1,0:T(8,128)(2,1)S(1)}, bf16[32,3712]{1,0:T(8,128)(2,1)S(1)}, u32[]{:S(2)}, u32[]{:S(2)}) collective-permute-start(bf16[32,3712]{1,0:T(8,128)(2,1)S(1)} %bitcast.34), channel_id=1, source_target_pairs={{0,7},{3,0},{4,3},{7,4},{9,14},{10,9},{13,10},{14,13},{16,23},{19,... | collective-permute-start | bytes 712712 | tf_op jit(solution)/shard_map/ppermute | solution.py:41
  80.6 10.0 %collective-permute-start.13 = (bf16[32,3712]{1,0:T(8,128)(2,1)S(1)}, bf16[32,3712]{1,0:T(8,128)(2,1)S(1)}, u32[]{:S(2)}, u32[]{:S(2)}) collective-permute-start(bf16[32,3712]{1,0:T(8,128)(2,1)S(1)} %bitcast.37), channel_id=1, source_target_pairs={{0,7},{3,0},{4,3},{7,4},{9,14},{10,9},{13,10},{14,13},{16,23},{19,... | collective-permute-start | bytes 712712 | tf_op jit(solution)/shard_map/ppermute | solution.py:41
  81.0 9.6 %collective-permute-start.16 = (bf16[32,3712]{1,0:T(8,128)(2,1)S(1)}, bf16[32,3712]{1,0:T(8,128)(2,1)S(1)}, u32[]{:S(2)}, u32[]{:S(2)}) collective-permute-start(bf16[32,3712]{1,0:T(8,128)(2,1)S(1)} %bitcast.35), channel_id=1, source_target_pairs={{0,3},{3,4},{4,7},{7,0},{9,10},{10,13},{13,14},{14,9},{16,19},{19,... | collective-permute-start | bytes 712712 | tf_op jit(solution)/shard_map/ppermute | solution.py:41
  84.7 8.0 %collective-permute-start.18 = (bf16[32,3712]{1,0:T(8,128)(2,1)S(1)}, bf16[32,3712]{1,0:T(8,128)(2,1)S(1)}, u32[]{:S(2)}, u32[]{:S(2)}) collective-permute-start(bf16[32,3712]{1,0:T(8,128)(2,1)S(1)} %collective-permute-done.15.refs_3_), channel_id=1, source_target_pairs={{0,3},{3,4},{4,7},{7,0},{9,10},{10,13},{13,14},{14,9},{16,19},{19,... | collective-permute-start | bytes 712712 | tf_op jit(solution)/shard_map/ppermute | solution.py:41
  84.7 8.0 %collective-permute-start.19 = (bf16[32,3712]{1,0:T(8,128)(2,1)S(1)}, bf16[32,3712]{1,0:T(8,128)(2,1)S(1)}, u32[]{:S(2)}, u32[]{:S(2)}) collective-permute-start(bf16[32,3712]{1,0:T(8,128)(2,1)S(1)} %collective-permute-done.14.refs_2_), channel_id=1, source_target_pairs={{0,7},{3,0},{4,3},{7,4},{9,14},{10,9},{13,10},{14,13},{16,23},{19,... | collective-permute-start | bytes 712712 | tf_op jit(solution)/shard_map/ppermute | solution.py:41
  94.2 3.7 %collective-permute-start.20 = (bf16[256,1152]{1,0:T(8,128)(2,1)S(1)}, bf16[256,1152]{1,0:T(8,128)(2,1)S(1)}, u32[]{:S(2)}, u32[]{:S(2)}) collective-permute-start(bf16[256,1152]{1,0:T(8,128)(2,1)S(1)} %get-tuple-element.57), channel_id=1, source_target_pairs={{0,1},{1,0},{2,3},{3,2},{4,5},{5,4},{6,7},{7,6},{8,9},{9,8},{10,11... | collective-permute-start | bytes 1769480 | tf_op jit(solution)/shard_map/ppermute | solution.py:37
  99.8 5.8 %collective-permute-start.25 = (bf16[32,3584]{1,0:T(8,128)(2,1)S(1)}, bf16[32,3584]{1,0:T(8,128)(2,1)S(1)}, u32[]{:S(2)}, u32[]{:S(2)}) collective-permute-start(bf16[32,3584]{1,0:T(8,128)(2,1)S(1)} %get-tuple-element.64), channel_id=1, source_target_pairs={{0,7},{3,0},{4,3},{7,4},{9,14},{10,9},{13,10},{14,13},{16,23},{19,... | collective-permute-start | bytes 688136 | tf_op jit(solution)/shard_map/ppermute | solution.py:41
  102.2 7.0 %collective-permute-start.21 = (bf16[32,3584]{1,0:T(8,128)(2,1)S(1)}, bf16[32,3584]{1,0:T(8,128)(2,1)S(1)}, u32[]{:S(2)}, u32[]{:S(2)}) collective-permute-start(bf16[32,3584]{1,0:T(8,128)(2,1)S(1)} %get-tuple-element.60), channel_id=1, source_target_pairs={{0,3},{3,4},{4,7},{7,0},{9,10},{10,13},{13,14},{14,9},{16,19},{19,... | collective-permute-start | bytes 688136 | tf_op jit(solution)/shard_map/ppermute | solution.py:41
  102.2 9.1 %collective-permute-start.23 = (bf16[32,3584]{1,0:T(8,128)(2,1)S(1)}, bf16[32,3584]{1,0:T(8,128)(2,1)S(1)}, u32[]{:S(2)}, u32[]{:S(2)}) collective-permute-start(bf16[32,3584]{1,0:T(8,128)(2,1)S(1)} %get-tuple-element.61), channel_id=1, source_target_pairs={{0,3},{3,4},{4,7},{7,0},{9,10},{10,13},{13,14},{14,9},{16,19},{19,... | collective-permute-start | bytes 688136 | tf_op jit(solution)/shard_map/ppermute | solution.py:41
  102.2 9.1 %collective-permute-start.24 = (bf16[32,3584]{1,0:T(8,128)(2,1)S(1)}, bf16[32,3584]{1,0:T(8,128)(2,1)S(1)}, u32[]{:S(2)}, u32[]{:S(2)}) collective-permute-start(bf16[32,3584]{1,0:T(8,128)(2,1)S(1)} %get-tuple-element.62), channel_id=1, source_target_pairs={{0,7},{3,0},{4,3},{7,4},{9,14},{10,9},{13,10},{14,13},{16,23},{19,... | collective-permute-start | bytes 688136 | tf_op jit(solution)/shard_map/ppermute | solution.py:41
  105.7 6.2 %collective-permute-start.26 = (bf16[32,3584]{1,0:T(8,128)(2,1)S(1)}, bf16[32,3584]{1,0:T(8,128)(2,1)S(1)}, u32[]{:S(2)}, u32[]{:S(2)}) collective-permute-start(bf16[32,3584]{1,0:T(8,128)(2,1)S(1)} %add_convert_fusion.2), channel_id=1, source_target_pairs={{0,7},{3,0},{4,3},{7,4},{9,14},{10,9},{13,10},{14,13},{16,23},{19,... | collective-permute-start | bytes 688136 | tf_op jit(solution)/shard_map/ppermute | solution.py:41
  109.2 6.7 %collective-permute-start.22 = (bf16[32,3584]{1,0:T(8,128)(2,1)S(1)}, bf16[32,3584]{1,0:T(8,128)(2,1)S(1)}, u32[]{:S(2)}, u32[]{:S(2)}) collective-permute-start(bf16[32,3584]{1,0:T(8,128)(2,1)S(1)} %add_convert_fusion.3), channel_id=1, source_target_pairs={{0,3},{3,4},{4,7},{7,0},{9,10},{10,13},{13,14},{14,9},{16,19},{19,... | collective-permute-start | bytes 688136 | tf_op jit(solution)/shard_map/ppermute | solution.py:41
  128.4 2.4 %collective-permute-start.27 = (bf16[2,3584]{1,0:T(2,128)(2,1)S(1)}, bf16[2,3584]{1,0:T(2,128)(2,1)S(1)}, u32[]{:S(2)}, u32[]{:S(2)}) collective-permute-start(bf16[2,3584]{1,0:T(2,128)(2,1)S(1)} %get-tuple-element.72), channel_id=1, source_target_pairs={{0,1},{1,0},{2,3},{3,2},{4,5},{5,4},{6,7},{7,6},{8,9},{9,8},{10,11... | collective-permute-start | bytes 43016 | tf_op jit(solution)/shard_map/ppermute | solution.py:37
  (6 other events, 98.1 us)

commit v7 on v4

--- a/solution.py
+++ b/solution.py
@@ -312,7 +312,7 @@
 
 
 def gate_up_kernel(*refs):
-    *refs, back, w, part, sent, squares, weight = refs
+    *refs, back, w, packed, part, sent, squares, weight = refs
     count = part.shape[0]
     first = sent.shape[0] - count
     pieces = refs
@@ -327,11 +327,14 @@
     for q in range(4):
         columns = slice(q * quarter, (q + 1) * quarter)
         a = jnp.concatenate([p[:, columns] for p in pieces], axis=0)
-        share = jnp.dot(a, w[columns, :], preferred_element_type=F32)
-        if q == 0:
-            part[...] = share
-        else:
-            part[...] += share
+        up = slice(half + q * quarter, half + (q + 1) * quarter)
+        for at, block in ((0, w[columns, :]), (512, packed[columns, :]), (768, packed[up, :])):
+            share = jnp.dot(a, block, preferred_element_type=F32)
+            spot = slice(at, at + block.shape[1])
+            if q == 0:
+                part[:, spot] = share
+            else:
+                part[:, spot] += share
         plain = a.astype(F32) * back[:, columns]
         sq += jnp.sum(plain * plain, axis=1, keepdims=True)
     squares[...] = sq
@@ -350,12 +353,12 @@
     weight[...] = jnp.sum(jnp.where(hit, high + low, 0.0), axis=1, keepdims=True)
 
 
-def gate_up(before, pieces, back, w):
+def gate_up(before, pieces, back, w, packed):
     count = sum(p.shape[0] for p in pieces)
     rows = count + sum(b.shape[0] for b in before)
     return call(
         gate_up_kernel,
-        (*before, *pieces, back, w),
+        (*before, *pieces, back, w, packed),
         [((count, 1024), F32), ((rows, 1152), BF16), ((count, 1), F32), ((count, 1), F32)],
         "gate_up",
         count << 23,
@@ -488,21 +491,19 @@
 
     scaled = (mixed * own(gain, 0)).astype(BF16)
     w_gu = load(
-        (w_gate[0], w_up[0], packed),
+        (w_gate[0], w_up[0]),
         (
             (0, 0, every, slice(0, 256)),
             (1, 0, every, slice(256, 512)),
-            (2, slice(0, half), every, slice(512, 768)),
-            (2, slice(half, 2 * half), every, slice(768, 1024)),
         ),
-        (half, 1024),
+        (half, 512),
         "load_gate_up",
         42,
     )
     near, far = gather_rows(jnp.concatenate([scaled, names], axis=1))
     back = (1.0 / own(gain, 0)).reshape(1, half)
-    p0, sent, q0, w0 = gate_up((), near, back, w_gu)
-    p1, sent, q1, w1 = gate_up((sent,), far, back, w_gu)
+    p0, sent, q0, w0 = gate_up((), near, back, w_gu, packed)
+    p1, sent, q1, w1 = gate_up((sent,), far, back, w_gu, packed)
     w_down = load(
         (w_down[0], packed),
         (

time: 132 us -> 136 us (1.030)
  Pallas kernels: 21.6 us -> 24.1 us
  local copies, waits for them, and re-layouts: 2.35 us -> 4.4 us
    pallas_call x5, Pallas kernels: 6.42 us -> 11.5 us  [call(): pl.pallas_call(kernel, in_specs=[VMEM] * len(args), out_specs=[VMEM] * le...]
    pallas_call x3, Pallas kernels: 5 us -> 2.4 us  [load(): pl.pallas_call(functools.partial(load_kernel, places), in_specs=[HBM] * l...]
    unnamed x16 -> x18, local copies, waits for them, and re-layouts: 0.04 us -> 2.08 us
where the time goes in v7:
time: 136 us; the launch traced here: 135 us
  starting transfers between devices  46.5 us (34%)
  waiting for transfers between devices  34 us (25%)
  Pallas kernels  24.1 us (18%)
  blocking collectives  24.1 us (18%)
  local copies, waits for them, and re-layouts  4.4 us (3%)
  other arithmetic  1.79 us (1%)
    ppermute x21, starting transfers between devices, ahead(): lax.ppermute(a, AXES, [(r[i], r[(i + step) % 4]) for r in RINGS for i in...  27 us
    all_to_all x2, blocking collectives, plane(): return lax.all_to_all(a, AXES, 0, 0, axis_index_groups=PLANES, tiled=True)  24.1 us
    ppermute x21, waiting for transfers between devices, ahead(): lax.ppermute(a, AXES, [(r[i], r[(i + step) % 4]) for r in RINGS for i in...  23.6 us
    pallas_call x5, Pallas kernels, call(): pl.pallas_call(kernel, in_specs=[VMEM] * len(args), out_specs=[VMEM] * le...  11.5 us
    all_to_all x2, starting transfers between devices, plane(): return lax.all_to_all(a, AXES, 0, 0, axis_index_groups=PLANES, tiled=True)  11 us
    all_to_all x2, waiting for transfers between devices, plane(): return lax.all_to_all(a, AXES, 0, 0, axis_index_groups=PLANES, tiled=True)  9.03 us
    ppermute x7, starting transfers between devices, swap(): return lax.ppermute(a, AXES, SIBLING)  8.49 us
    pallas_call x1, Pallas kernels, attend(): pl.pallas_call(attend_kernel, in_specs=[pl.BlockSpec(memory_space=pltpu.S...  5.47 us
  transfers between devices with their start and end apart: 30, of which 19 were waited for; matrix products, arithmetic and copies ran while one was open for 2% of the time, Pallas kernels for 9%

profile of v7, /device:TPU:1, one launch (start us, length us, event | category | flops | bytes accessed | tf_op | source)
XLA Modules:
  0.0 135.2 jit_solution(15974453459621482354)
XLA Ops:
  0.0 5.5 %attend.1 = (bf16[16,16,512]{2,1,0:T(8,128)(2,1)}, bf16[128,3584]{1,0:T(8,128)(2,1)}) custom-call(s32[2]{0:T(128)} %lens.1, bf16[2,576,128]{2,1,0:T(8,128)(2,1)} %bitcast.33, bf16[2,576,2048]{2,1,0:T(8,128)(2,1)} %bitcast.27, bf16[128,7168]{1,0:T(8,128)(2,1)} %refs_0_.1), custom_call_target="tpu_custom_call" | custom-call | tf_op jit(solution)/shard_map/attend/pallas_call | solution.py:142
  5.5 1.5 %collective-permute-start.6 = (bf16[128,3584]{1,0:T(8,128)(2,1)}, bf16[128,3584]{1,0:T(8,128)(2,1)S(1)}, u32[]{:S(2)}, u32[]{:S(2)}) collective-permute-start(bf16[128,3584]{1,0:T(8,128)(2,1)} %get-tuple-element.36.after), channel_id=1, source_target_pairs={{0,1},{1,0},{2,3},{3,2},{4,5},{5,4},{6,7},{7,6},{8,9},{9,8},{10,11... | collective-permute-start | bytes 2752520 | tf_op jit(solution)/shard_map/ppermute | solution.py:37
  7.0 7.4 %all-to-all-start = ((bf16[16,16,512]{2,1,0:T(8,128)(2,1)}), bf16[16,16,512]{2,1,0:T(8,128)(2,1)S(1)}, u32[]{:S(2)}, u32[]{:S(2)}) async-start(bf16[16,16,512]{2,1,0:T(8,128)(2,1)} %get-tuple-element.35), calls=%async_computation | async-start | bytes 524288 | tf_op jit(solution)/shard_map/all_to_all | solution.py:45
  14.5 1.8 %collective-permute-start.4 = (bf16[512,128]{1,0:T(8,128)(2,1)S(1)}, bf16[512,128]{1,0:T(8,128)(2,1)S(1)}, u32[]{:S(2)}, u32[]{:S(2)}) collective-permute-start(bf16[512,128]{1,0:T(8,128)(2,1)S(1)} %bitcast.25), channel_id=1, source_target_pairs={{0,1},{1,0},{2,3},{3,2},{4,5},{5,4},{6,7},{7,6},{8,9},{9,8},{10,11... | collective-permute-start | bytes 393224 | tf_op jit(solution)/shard_map/ppermute | solution.py:37
  16.3 4.5 %pack.1 = (bf16[10752,256]{1,0:T(8,128)(2,1)}, f32[8,128]{1,0:T(8,128)S(1)}) custom-call(bf16[7168,256]{1,0:T(8,128)(2,1)} %bitcast.20, bf16[7168,256]{1,0:T(8,128)(2,1)} %bitcast.22, bf16[256,7168]{1,0:T(8,128)(2,1)} %bitcast.18, bf16[128,3584]{1,0:T(8,128)(2,1)} %get-tuple-element.36.after), custom_call_target="tpu_custom_call" | custom-call | bytes 12582912 | tf_op jit(solution)/shard_map/pack/pallas_call | solution.py:233
  22.3 5.2 %collective-permute-start.1 = (bf16[64,512]{1,0:T(8,128)(2,1)S(1)}, bf16[64,512]{1,0:T(8,128)(2,1)S(1)}, u32[]{:S(2)}, u32[]{:S(2)}) collective-permute-start(bf16[64,512]{1,0:T(8,128)(2,1)S(1)} %get-tuple-element.39), channel_id=1, source_target_pairs={{0,7},{3,0},{4,3},{7,4},{9,14},{10,9},{13,10},{14,13},{16,23},{19,... | collective-permute-start | bytes 196616 | tf_op jit(solution)/shard_map/ppermute | solution.py:41
  28.9 3.3 %collective-permute-done.2.p2 = bf16[64,512]{1,0:T(8,128)(2,1)S(1)} collective-permute-done((bf16[64,512]{1,0:T(8,128)(2,1)S(1)}, bf16[64,512]{1,0:T(8,128)(2,1)S(1)}, u32[]{:S(2)}, u32[]{:S(2)}) %collective-permute-start.2) | collective-permute-done | bytes 65568 | tf_op jit(solution)/shard_map/ppermute | solution.py:41
  33.4 1.4 %collective-permute-start.5 = (bf16[128,256]{1,0:T(8,128)(2,1)S(1)}, bf16[128,256]{1,0:T(8,128)(2,1)S(1)}, u32[]{:S(2)}, u32[]{:S(2)}) collective-permute-start(bf16[128,256]{1,0:T(8,128)(2,1)S(1)} %values.1.mine), channel_id=1, source_target_pairs={{0,1},{1,0},{2,3},{3,2},{4,5},{5,4},{6,7},{7,6},{8,9},{9,8},{10,11... | collective-permute-start | bytes 196616 | tf_op jit(solution)/shard_map/ppermute | solution.py:37
  38.4 1.7 %collective-permute-start.10 = (bf16[32,3584]{1,0:T(8,128)(2,1)S(1)}, bf16[32,3584]{1,0:T(8,128)(2,1)S(1)}, u32[]{:S(2)}, u32[]{:S(2)}) collective-permute-start(bf16[32,3584]{1,0:T(8,128)(2,1)S(1)} %get-tuple-element.46), channel_id=1, source_target_pairs={{0,7},{3,0},{4,3},{7,4},{9,14},{10,9},{13,10},{14,13},{16,23},{19,... | collective-permute-start | bytes 688136 | tf_op jit(solution)/shard_map/ppermute | solution.py:41
  40.1 2.2 %collective-permute-done.11 = bf16[32,3584]{1,0:T(8,128)(2,1)S(1)} collective-permute-done((bf16[32,3584]{1,0:T(8,128)(2,1)S(1)}, bf16[32,3584]{1,0:T(8,128)(2,1)S(1)}, u32[]{:S(2)}, u32[]{:S(2)}) %collective-permute-start.11) | collective-permute-done | bytes 229408 | tf_op jit(solution)/shard_map/ppermute | solution.py:41
  44.8 1.9 %collective-permute-done.9 = bf16[32,3584]{1,0:T(8,128)(2,1)S(1)} collective-permute-done((bf16[32,3584]{1,0:T(8,128)(2,1)S(1)}, bf16[32,3584]{1,0:T(8,128)(2,1)S(1)}, u32[]{:S(2)}, u32[]{:S(2)}) %collective-permute-start.9) | collective-permute-done | bytes 229408 | tf_op jit(solution)/shard_map/ppermute | solution.py:41
  46.7 1.5 %collective-permute-done.12 = bf16[32,3584]{1,0:T(8,128)(2,1)S(1)} collective-permute-done((bf16[32,3584]{1,0:T(8,128)(2,1)S(1)}, bf16[32,3584]{1,0:T(8,128)(2,1)S(1)}, u32[]{:S(2)}, u32[]{:S(2)}) %collective-permute-start.12) | collective-permute-done | bytes 229408 | tf_op jit(solution)/shard_map/ppermute | solution.py:41
  48.2 2.6 %collective-permute-done.8 = bf16[32,3584]{1,0:T(8,128)(2,1)S(1)} collective-permute-done((bf16[32,3584]{1,0:T(8,128)(2,1)S(1)}, bf16[32,3584]{1,0:T(8,128)(2,1)S(1)}, u32[]{:S(2)}, u32[]{:S(2)}) %collective-permute-start.8) | collective-permute-done | bytes 229408 | tf_op jit(solution)/shard_map/ppermute | solution.py:41
  52.1 3.6 %all-to-all-start.1 = ((bf16[16,4,3584]{2,1,0:T(4,128)(2,1)}), bf16[16,4,3584]{2,1,0:T(4,128)(2,1)S(1)}, u32[]{:S(2)}, u32[]{:S(2)}) async-start(bf16[16,4,3584]{2,1,0:T(4,128)(2,1)} %bitcast.17), calls=%async_computation.1 | async-start | bytes 917504 | tf_op jit(solution)/shard_map/all_to_all | solution.py:45
  56.5 7.7 %all-to-all-done.1 = bf16[16,4,3584]{2,1,0:T(4,128)(2,1)S(1)} async-done(((bf16[16,4,3584]{2,1,0:T(4,128)(2,1)}), bf16[16,4,3584]{2,1,0:T(4,128)(2,1)S(1)}, u32[]{:S(2)}, u32[]{:S(2)}) %all-to-all-start.1) | async-done | bytes 458784 | tf_op jit(solution)/shard_map/all_to_all | solution.py:45
  64.7 12.6 %all_to_all.20 = bf16[16,4,3712]{2,1,0:T(4,128)(2,1)S(1)} all-to-all(bf16[16,4,3712]{2,1,0:T(4,128)(2,1)S(1)} %broadcast_in_dim.8), channel_id=1, replica_groups={{0,9,16,25,32,41,48,57,64,73,80,89,96,105,112,121},{3,10,19,26,35,42,51..., dimensions={0} | all-to-all | bytes 950272 | tf_op jit(solution)/shard_map/all_to_all | solution.py:45
  78.5 2.2 %collective-permute-start.14 = (bf16[32,3712]{1,0:T(8,128)(2,1)S(1)}, bf16[32,3712]{1,0:T(8,128)(2,1)S(1)}, u32[]{:S(2)}, u32[]{:S(2)}) collective-permute-start(bf16[32,3712]{1,0:T(8,128)(2,1)S(1)} %bitcast.34), channel_id=1, source_target_pairs={{0,7},{3,0},{4,3},{7,4},{9,14},{10,9},{13,10},{14,13},{16,23},{19,... | collective-permute-start | bytes 712712 | tf_op jit(solution)/shard_map/ppermute | solution.py:41
  81.0 1.4 %collective-permute-start.16 = (bf16[32,3712]{1,0:T(8,128)(2,1)S(1)}, bf16[32,3712]{1,0:T(8,128)(2,1)S(1)}, u32[]{:S(2)}, u32[]{:S(2)}) collective-permute-start(bf16[32,3712]{1,0:T(8,128)(2,1)S(1)} %bitcast.35), channel_id=1, source_target_pairs={{0,3},{3,4},{4,7},{7,0},{9,10},{10,13},{13,14},{14,9},{16,19},{19,... | collective-permute-start | bytes 712712 | tf_op jit(solution)/shard_map/ppermute | solution.py:41
  82.4 2.3 %collective-permute-done.15.refs_3_ = bf16[32,3712]{1,0:T(8,128)(2,1)S(1)} collective-permute-done((bf16[32,3712]{1,0:T(8,128)(2,1)S(1)}, bf16[32,3712]{1,0:T(8,128)(2,1)S(1)}, u32[]{:S(2)}, u32[]{:S(2)}) %collective-permute-start.15) | collective-permute-done | bytes 237600 | tf_op jit(solution)/shard_map/ppermute | solution.py:41
  84.8 3.0 %collective-permute-start.19 = (bf16[32,3712]{1,0:T(8,128)(2,1)S(1)}, bf16[32,3712]{1,0:T(8,128)(2,1)S(1)}, u32[]{:S(2)}, u32[]{:S(2)}) collective-permute-start(bf16[32,3712]{1,0:T(8,128)(2,1)S(1)} %collective-permute-done.14.refs_2_), channel_id=1, source_target_pairs={{0,7},{3,0},{4,3},{7,4},{9,14},{10,9},{13,10},{14,13},{16,23},{19,... | collective-permute-start | bytes 712712 | tf_op jit(solution)/shard_map/ppermute | solution.py:41
  87.7 2.0 %copy-done.2 = bf16[1,7168,256]{2,1,0:T(8,128)(2,1)S(1)} copy-done((bf16[1,7168,256]{2,1,0:T(8,128)(2,1)S(1)}, bf16[1,7168,256]{2,1,0:T(8,128)(2,1)}, u32[]{:S(2)}) %copy-start.2) | copy-done | bytes 3670040
  90.2 4.5 %gate_up.2 = (f32[192,1024]{1,0:T(8,128)S(1)}, bf16[192,1152]{1,0:T(8,128)(2,1)S(1)}, f32[192,1]{1,0:T(8,128)S(1)}, f32[192,1]{1,0:T(8,128)S(1)}) custom-call(bf16[64,3712]{1,0:T(8,128)(2,1)S(1)} %bitcast.24, bf16[32,3712]{1,0:T(8,128)(2,1)S(1)} %collective-permute-done.13.refs_1_, bf16[32,3712]{1,0:T(8,128)(2,1)S(1)} %collective-permute-done.14.refs_2_, ...), custom_call_target="tpu_custom_call" | custom-call | flops 1610612736 | bytes 1048576 | tf_op jit(solution)/shard_map/gate_up/pallas_call | solution.py:249
  94.7 4.2 %gate_up.3 = (f32[64,1024]{1,0:T(8,128)S(1)}, bf16[256,1152]{1,0:T(8,128)(2,1)S(1)}, f32[64,1]{1,0:T(8,128)S(1)}, f32[64,1]{1,0:T(8,128)S(1)}) custom-call(bf16[192,1152]{1,0:T(8,128)(2,1)S(1)} %get-tuple-element.53.refs_0_, bf16[32,3712]{1,0:T(8,128)(2,1)S(1)} %collective-permute-done.18.refs_1_, bf16[32,3712]{1,0:T(8,128)(2,1)S(1)} %collective-permute-done.19.refs_2_, ...), custom_call_target="tpu_custom_call" | custom-call | flops 536870912 | bytes 1048576 | tf_op jit(solution)/shard_map/gate_up/pallas_call | solution.py:249
  98.9 1.9 %collective-permute-start.20 = (bf16[256,1152]{1,0:T(8,128)(2,1)S(1)}, bf16[256,1152]{1,0:T(8,128)(2,1)S(1)}, u32[]{:S(2)}, u32[]{:S(2)}) collective-permute-start(bf16[256,1152]{1,0:T(8,128)(2,1)S(1)} %get-tuple-element.57), channel_id=1, source_target_pairs={{0,1},{1,0},{2,3},{3,2},{4,5},{5,4},{6,7},{7,6},{8,9},{9,8},{10,11... | collective-permute-start | bytes 1769480 | tf_op jit(solution)/shard_map/ppermute | solution.py:37
  100.8 1.8 %load_down.1.w = bf16[512,3584]{1,0:T(8,128)(2,1)S(1)} custom-call(bf16[256,7168]{1,0:T(8,128)(2,1)S(1)} %bitcast.19, bf16[10752,256]{1,0:T(8,128)(2,1)} %collective-permute-done.17.refs_7_.refs_5_.refs_1_), custom_call_target="tpu_custom_call" | custom-call | bytes 7340032 | tf_op jit(solution)/shard_map/load_down/pallas_call | solution.py:189
  102.6 1.8 %down.1 = (bf16[64,3584]{1,0:T(8,128)(2,1)S(1)}, bf16[32,3584]{1,0:T(8,128)(2,1)S(1)}, bf16[32,3584]{1,0:T(8,128)(2,1)S(1)}, bf16[32,3584]{1,0:T(8,128)(2,1)S(1)...) custom-call(f32[192,1024]{1,0:T(8,128)S(1)} %get-tuple-element.50.p0, ...), custom_call_target="tpu_custom_call" | custom-call | flops 1073741824 | bytes 1048576 | tf_op jit(solution)/shard_map/down/pallas_call | solution.py:249
  104.4 2.3 %collective-permute-start.25 = (bf16[32,3584]{1,0:T(8,128)(2,1)S(1)}, bf16[32,3584]{1,0:T(8,128)(2,1)S(1)}, u32[]{:S(2)}, u32[]{:S(2)}) collective-permute-start(bf16[32,3584]{1,0:T(8,128)(2,1)S(1)} %get-tuple-element.64), channel_id=1, source_target_pairs={{0,7},{3,0},{4,3},{7,4},{9,14},{10,9},{13,10},{14,13},{16,23},{19,... | collective-permute-start | bytes 688136 | tf_op jit(solution)/shard_map/ppermute | solution.py:41
  106.8 3.0 %collective-permute-start.24 = (bf16[32,3584]{1,0:T(8,128)(2,1)S(1)}, bf16[32,3584]{1,0:T(8,128)(2,1)S(1)}, u32[]{:S(2)}, u32[]{:S(2)}) collective-permute-start(bf16[32,3584]{1,0:T(8,128)(2,1)S(1)} %get-tuple-element.62), channel_id=1, source_target_pairs={{0,7},{3,0},{4,3},{7,4},{9,14},{10,9},{13,10},{14,13},{16,23},{19,... | collective-permute-start | bytes 688136 | tf_op jit(solution)/shard_map/ppermute | solution.py:41
  110.3 3.3 %collective-permute-start.26 = (bf16[32,3584]{1,0:T(8,128)(2,1)S(1)}, bf16[32,3584]{1,0:T(8,128)(2,1)S(1)}, u32[]{:S(2)}, u32[]{:S(2)}) collective-permute-start(bf16[32,3584]{1,0:T(8,128)(2,1)S(1)} %add_convert_fusion.2), channel_id=1, source_target_pairs={{0,7},{3,0},{4,3},{7,4},{9,14},{10,9},{13,10},{14,13},{16,23},{19,... | collective-permute-start | bytes 688136 | tf_op jit(solution)/shard_map/ppermute | solution.py:41
  113.9 2.3 %collective-permute-done.23 = bf16[32,3584]{1,0:T(8,128)(2,1)S(1)} collective-permute-done((bf16[32,3584]{1,0:T(8,128)(2,1)S(1)}, bf16[32,3584]{1,0:T(8,128)(2,1)S(1)}, u32[]{:S(2)}, u32[]{:S(2)}) %collective-permute-start.23) | collective-permute-done | bytes 229408 | tf_op jit(solution)/shard_map/ppermute | solution.py:41
  116.5 4.0 %collective-permute-done.22 = bf16[32,3584]{1,0:T(8,128)(2,1)S(1)} collective-permute-done((bf16[32,3584]{1,0:T(8,128)(2,1)S(1)}, bf16[32,3584]{1,0:T(8,128)(2,1)S(1)}, u32[]{:S(2)}, u32[]{:S(2)}) %collective-permute-start.22) | collective-permute-done | bytes 229408 | tf_op jit(solution)/shard_map/ppermute | solution.py:41
  121.0 11.5 %all_to_all.21 = bf16[16,4,3584]{2,1,0:T(4,128)(2,1)S(1)} all-to-all(bf16[16,4,3584]{2,1,0:T(4,128)(2,1)S(1)} %bitcast.32), channel_id=1, replica_groups={{0,9,16,25,32,41,48,57,64,73,80,89,96,105,112,121},{3,10,19,26,35,42,51..., dimensions={0} | all-to-all | bytes 917504 | tf_op jit(solution)/shard_map/all_to_all | solution.py:45
  (87 shorter events, 18.9 us)
Async XLA Ops:
  5.5 29.3 %collective-permute-start.6 = (bf16[128,3584]{1,0:T(8,128)(2,1)}, bf16[128,3584]{1,0:T(8,128)(2,1)S(1)}, u32[]{:S(2)}, u32[]{:S(2)}) collective-permute-start(bf16[128,3584]{1,0:T(8,128)(2,1)} %get-tuple-element.36.after), channel_id=1, source_target_pairs={{0,1},{1,0},{2,3},{3,2},{4,5},{5,4},{6,7},{7,6},{8,9},{9,8},{10,11... | collective-permute-start | bytes 2752520 | tf_op jit(solution)/shard_map/ppermute | solution.py:37
  7.0 15.1 %all-to-all-start = ((bf16[16,16,512]{2,1,0:T(8,128)(2,1)}), bf16[16,16,512]{2,1,0:T(8,128)(2,1)S(1)}, u32[]{:S(2)}, u32[]{:S(2)}) async-start(bf16[16,16,512]{2,1,0:T(8,128)(2,1)} %get-tuple-element.35), calls=%async_computation | async-start | bytes 524288 | tf_op jit(solution)/shard_map/all_to_all | solution.py:45
  14.5 14.1 %collective-permute-start.4 = (bf16[512,128]{1,0:T(8,128)(2,1)S(1)}, bf16[512,128]{1,0:T(8,128)(2,1)S(1)}, u32[]{:S(2)}, u32[]{:S(2)}) collective-permute-start(bf16[512,128]{1,0:T(8,128)(2,1)S(1)} %bitcast.25), channel_id=1, source_target_pairs={{0,1},{1,0},{2,3},{3,2},{4,5},{5,4},{6,7},{7,6},{8,9},{9,8},{10,11... | collective-permute-start | bytes 393224 | tf_op jit(solution)/shard_map/ppermute | solution.py:37
  22.3 6.6 %collective-permute-start.1 = (bf16[64,512]{1,0:T(8,128)(2,1)S(1)}, bf16[64,512]{1,0:T(8,128)(2,1)S(1)}, u32[]{:S(2)}, u32[]{:S(2)}) collective-permute-start(bf16[64,512]{1,0:T(8,128)(2,1)S(1)} %get-tuple-element.39), channel_id=1, source_target_pairs={{0,7},{3,0},{4,3},{7,4},{9,14},{10,9},{13,10},{14,13},{16,23},{19,... | collective-permute-start | bytes 196616 | tf_op jit(solution)/shard_map/ppermute | solution.py:41
  27.6 4.7 %collective-permute-start.2 = (bf16[64,512]{1,0:T(8,128)(2,1)S(1)}, bf16[64,512]{1,0:T(8,128)(2,1)S(1)}, u32[]{:S(2)}, u32[]{:S(2)}) collective-permute-start(bf16[64,512]{1,0:T(8,128)(2,1)S(1)} %get-tuple-element.40), channel_id=1, source_target_pairs={{0,4},{3,7},{4,0},{7,3},{9,13},{10,14},{13,9},{14,10},{16,20},{19,... | collective-permute-start | bytes 196616 | tf_op jit(solution)/shard_map/ppermute | solution.py:41
  27.6 5.6 %collective-permute-start.3 = (bf16[64,512]{1,0:T(8,128)(2,1)S(1)}, bf16[64,512]{1,0:T(8,128)(2,1)S(1)}, u32[]{:S(2)}, u32[]{:S(2)}) collective-permute-start(bf16[64,512]{1,0:T(8,128)(2,1)S(1)} %get-tuple-element.41), channel_id=1, source_target_pairs={{0,3},{3,4},{4,7},{7,0},{9,10},{10,13},{13,14},{14,9},{16,19},{19,... | collective-permute-start | bytes 196616 | tf_op jit(solution)/shard_map/ppermute | solution.py:41
  33.4 2.3 %collective-permute-start.5 = (bf16[128,256]{1,0:T(8,128)(2,1)S(1)}, bf16[128,256]{1,0:T(8,128)(2,1)S(1)}, u32[]{:S(2)}, u32[]{:S(2)}) collective-permute-start(bf16[128,256]{1,0:T(8,128)(2,1)S(1)} %values.1.mine), channel_id=1, source_target_pairs={{0,1},{1,0},{2,3},{3,2},{4,5},{5,4},{6,7},{7,6},{8,9},{9,8},{10,11... | collective-permute-start | bytes 196616 | tf_op jit(solution)/shard_map/ppermute | solution.py:37
  35.2 21.3 %copy-start.6 = (f32[7168]{0:T(1024)S(1)}, f32[7168]{0:T(1024)}, u32[]{:S(2)}) copy-start(f32[7168]{0:T(1024)} %param.18) | copy-start | bytes 86020
  36.5 5.8 %collective-permute-start.11 = (bf16[32,3584]{1,0:T(8,128)(2,1)S(1)}, bf16[32,3584]{1,0:T(8,128)(2,1)S(1)}, u32[]{:S(2)}, u32[]{:S(2)}) collective-permute-start(bf16[32,3584]{1,0:T(8,128)(2,1)S(1)} %get-tuple-element.48), channel_id=1, source_target_pairs={{0,7},{3,0},{4,3},{7,4},{9,14},{10,9},{13,10},{14,13},{16,23},{19,... | collective-permute-start | bytes 688136 | tf_op jit(solution)/shard_map/ppermute | solution.py:41
  36.6 53.6 %collective-permute-start.17 = (bf16[10752,256]{1,0:T(8,128)(2,1)}, bf16[10752,256]{1,0:T(8,128)(2,1)}, u32[]{:S(2)}, u32[]{:S(2)}) collective-permute-start(bf16[10752,256]{1,0:T(8,128)(2,1)} %get-tuple-element.49), channel_id=1, source_target_pairs={{0,1},{1,0},{2,3},{3,2},{4,5},{5,4},{6,7},{7,6},{8,9},{9,8},{10,11... | collective-permute-start | bytes 16515080 | tf_op jit(solution)/shard_map/ppermute | solution.py:37
  37.1 7.0 %collective-permute-start.7 = (bf16[32,3584]{1,0:T(8,128)(2,1)S(1)}, bf16[32,3584]{1,0:T(8,128)(2,1)S(1)}, u32[]{:S(2)}, u32[]{:S(2)}) collective-permute-start(bf16[32,3584]{1,0:T(8,128)(2,1)S(1)} %get-tuple-element.44), channel_id=1, source_target_pairs={{0,3},{3,4},{4,7},{7,0},{9,10},{10,13},{13,14},{14,9},{16,19},{19,... | collective-permute-start | bytes 688136 | tf_op jit(solution)/shard_map/ppermute | solution.py:41
  38.4 6.4 %collective-permute-start.10 = (bf16[32,3584]{1,0:T(8,128)(2,1)S(1)}, bf16[32,3584]{1,0:T(8,128)(2,1)S(1)}, u32[]{:S(2)}, u32[]{:S(2)}) collective-permute-start(bf16[32,3584]{1,0:T(8,128)(2,1)S(1)} %get-tuple-element.46), channel_id=1, source_target_pairs={{0,7},{3,0},{4,3},{7,4},{9,14},{10,9},{13,10},{14,13},{16,23},{19,... | collective-permute-start | bytes 688136 | tf_op jit(solution)/shard_map/ppermute | solution.py:41
  40.0 6.7 %collective-permute-start.9 = (bf16[32,3584]{1,0:T(8,128)(2,1)S(1)}, bf16[32,3584]{1,0:T(8,128)(2,1)S(1)}, u32[]{:S(2)}, u32[]{:S(2)}) collective-permute-start(bf16[32,3584]{1,0:T(8,128)(2,1)S(1)} %get-tuple-element.45), channel_id=1, source_target_pairs={{0,3},{3,4},{4,7},{7,0},{9,10},{10,13},{13,14},{14,9},{16,19},{19,... | collective-permute-start | bytes 688136 | tf_op jit(solution)/shard_map/ppermute | solution.py:41
  42.4 5.8 %collective-permute-start.12 = (bf16[32,3584]{1,0:T(8,128)(2,1)S(1)}, bf16[32,3584]{1,0:T(8,128)(2,1)S(1)}, u32[]{:S(2)}, u32[]{:S(2)}) collective-permute-start(bf16[32,3584]{1,0:T(8,128)(2,1)S(1)} %add_convert_fusion.4), channel_id=1, source_target_pairs={{0,7},{3,0},{4,3},{7,4},{9,14},{10,9},{13,10},{14,13},{16,23},{19,... | collective-permute-start | bytes 688136 | tf_op jit(solution)/shard_map/ppermute | solution.py:41
  44.1 6.7 %collective-permute-start.8 = (bf16[32,3584]{1,0:T(8,128)(2,1)S(1)}, bf16[32,3584]{1,0:T(8,128)(2,1)S(1)}, u32[]{:S(2)}, u32[]{:S(2)}) collective-permute-start(bf16[32,3584]{1,0:T(8,128)(2,1)S(1)} %add_convert_fusion.5), channel_id=1, source_target_pairs={{0,3},{3,4},{4,7},{7,0},{9,10},{10,13},{13,14},{14,9},{16,19},{19,... | collective-permute-start | bytes 688136 | tf_op jit(solution)/shard_map/ppermute | solution.py:41
  52.1 12.2 %all-to-all-start.1 = ((bf16[16,4,3584]{2,1,0:T(4,128)(2,1)}), bf16[16,4,3584]{2,1,0:T(4,128)(2,1)S(1)}, u32[]{:S(2)}, u32[]{:S(2)}) async-start(bf16[16,4,3584]{2,1,0:T(4,128)(2,1)} %bitcast.17), calls=%async_computation.1 | async-start | bytes 917504 | tf_op jit(solution)/shard_map/all_to_all | solution.py:45
  55.9 8.6 %collective-permute-start = (bf16[2,3712]{1,0:T(2,128)(2,1)S(1)}, bf16[2,3712]{1,0:T(2,128)(2,1)S(1)}, u32[]{:S(2)}, u32[]{:S(2)}) collective-permute-start(bf16[2,3712]{1,0:T(2,128)(2,1)S(1)} %concatenate.34), channel_id=1, source_target_pairs={{0,1},{1,0},{2,3},{3,2},{4,5},{5,4},{6,7},{7,6},{8,9},{9,8},{10,11... | collective-permute-start | bytes 44552 | tf_op jit(solution)/shard_map/ppermute | solution.py:37
  64.3 23.5 %copy-start.1 = (bf16[1,7168,256]{2,1,0:T(8,128)(2,1)S(1)}, bf16[1,7168,256]{2,1,0:T(8,128)(2,1)}, u32[]{:S(2)}) copy-start(bf16[1,7168,256]{2,1,0:T(8,128)(2,1)} %param.21) | copy-start | bytes 11010052
  77.7 7.1 %collective-permute-start.15 = (bf16[32,3712]{1,0:T(8,128)(2,1)S(1)}, bf16[32,3712]{1,0:T(8,128)(2,1)S(1)}, u32[]{:S(2)}, u32[]{:S(2)}) collective-permute-start(bf16[32,3712]{1,0:T(8,128)(2,1)S(1)} %bitcast.36), channel_id=1, source_target_pairs={{0,3},{3,4},{4,7},{7,0},{9,10},{10,13},{13,14},{14,9},{16,19},{19,... | collective-permute-start | bytes 712712 | tf_op jit(solution)/shard_map/ppermute | solution.py:41
  78.5 6.3 %collective-permute-start.14 = (bf16[32,3712]{1,0:T(8,128)(2,1)S(1)}, bf16[32,3712]{1,0:T(8,128)(2,1)S(1)}, u32[]{:S(2)}, u32[]{:S(2)}) collective-permute-start(bf16[32,3712]{1,0:T(8,128)(2,1)S(1)} %bitcast.34), channel_id=1, source_target_pairs={{0,7},{3,0},{4,3},{7,4},{9,14},{10,9},{13,10},{14,13},{16,23},{19,... | collective-permute-start | bytes 712712 | tf_op jit(solution)/shard_map/ppermute | solution.py:41
  80.7 9.5 %collective-permute-start.13 = (bf16[32,3712]{1,0:T(8,128)(2,1)S(1)}, bf16[32,3712]{1,0:T(8,128)(2,1)S(1)}, u32[]{:S(2)}, u32[]{:S(2)}) collective-permute-start(bf16[32,3712]{1,0:T(8,128)(2,1)S(1)} %bitcast.37), channel_id=1, source_target_pairs={{0,7},{3,0},{4,3},{7,4},{9,14},{10,9},{13,10},{14,13},{16,23},{19,... | collective-permute-start | bytes 712712 | tf_op jit(solution)/shard_map/ppermute | solution.py:41
  81.0 9.1 %collective-permute-start.16 = (bf16[32,3712]{1,0:T(8,128)(2,1)S(1)}, bf16[32,3712]{1,0:T(8,128)(2,1)S(1)}, u32[]{:S(2)}, u32[]{:S(2)}) collective-permute-start(bf16[32,3712]{1,0:T(8,128)(2,1)S(1)} %bitcast.35), channel_id=1, source_target_pairs={{0,3},{3,4},{4,7},{7,0},{9,10},{10,13},{13,14},{14,9},{16,19},{19,... | collective-permute-start | bytes 712712 | tf_op jit(solution)/shard_map/ppermute | solution.py:41
  84.8 9.9 %collective-permute-start.18 = (bf16[32,3712]{1,0:T(8,128)(2,1)S(1)}, bf16[32,3712]{1,0:T(8,128)(2,1)S(1)}, u32[]{:S(2)}, u32[]{:S(2)}) collective-permute-start(bf16[32,3712]{1,0:T(8,128)(2,1)S(1)} %collective-permute-done.15.refs_3_), channel_id=1, source_target_pairs={{0,3},{3,4},{4,7},{7,0},{9,10},{10,13},{13,14},{14,9},{16,19},{19,... | collective-permute-start | bytes 712712 | tf_op jit(solution)/shard_map/ppermute | solution.py:41
  84.8 9.9 %collective-permute-start.19 = (bf16[32,3712]{1,0:T(8,128)(2,1)S(1)}, bf16[32,3712]{1,0:T(8,128)(2,1)S(1)}, u32[]{:S(2)}, u32[]{:S(2)}) collective-permute-start(bf16[32,3712]{1,0:T(8,128)(2,1)S(1)} %collective-permute-done.14.refs_2_), channel_id=1, source_target_pairs={{0,7},{3,0},{4,3},{7,4},{9,14},{10,9},{13,10},{14,13},{16,23},{19,... | collective-permute-start | bytes 712712 | tf_op jit(solution)/shard_map/ppermute | solution.py:41
  98.9 3.7 %collective-permute-start.20 = (bf16[256,1152]{1,0:T(8,128)(2,1)S(1)}, bf16[256,1152]{1,0:T(8,128)(2,1)S(1)}, u32[]{:S(2)}, u32[]{:S(2)}) collective-permute-start(bf16[256,1152]{1,0:T(8,128)(2,1)S(1)} %get-tuple-element.57), channel_id=1, source_target_pairs={{0,1},{1,0},{2,3},{3,2},{4,5},{5,4},{6,7},{7,6},{8,9},{9,8},{10,11... | collective-permute-start | bytes 1769480 | tf_op jit(solution)/shard_map/ppermute | solution.py:37
  104.4 5.8 %collective-permute-start.25 = (bf16[32,3584]{1,0:T(8,128)(2,1)S(1)}, bf16[32,3584]{1,0:T(8,128)(2,1)S(1)}, u32[]{:S(2)}, u32[]{:S(2)}) collective-permute-start(bf16[32,3584]{1,0:T(8,128)(2,1)S(1)} %get-tuple-element.64), channel_id=1, source_target_pairs={{0,7},{3,0},{4,3},{7,4},{9,14},{10,9},{13,10},{14,13},{16,23},{19,... | collective-permute-start | bytes 688136 | tf_op jit(solution)/shard_map/ppermute | solution.py:41
  106.8 7.0 %collective-permute-start.21 = (bf16[32,3584]{1,0:T(8,128)(2,1)S(1)}, bf16[32,3584]{1,0:T(8,128)(2,1)S(1)}, u32[]{:S(2)}, u32[]{:S(2)}) collective-permute-start(bf16[32,3584]{1,0:T(8,128)(2,1)S(1)} %get-tuple-element.60), channel_id=1, source_target_pairs={{0,3},{3,4},{4,7},{7,0},{9,10},{10,13},{13,14},{14,9},{16,19},{19,... | collective-permute-start | bytes 688136 | tf_op jit(solution)/shard_map/ppermute | solution.py:41
  106.8 9.4 %collective-permute-start.23 = (bf16[32,3584]{1,0:T(8,128)(2,1)S(1)}, bf16[32,3584]{1,0:T(8,128)(2,1)S(1)}, u32[]{:S(2)}, u32[]{:S(2)}) collective-permute-start(bf16[32,3584]{1,0:T(8,128)(2,1)S(1)} %get-tuple-element.61), channel_id=1, source_target_pairs={{0,3},{3,4},{4,7},{7,0},{9,10},{10,13},{13,14},{14,9},{16,19},{19,... | collective-permute-start | bytes 688136 | tf_op jit(solution)/shard_map/ppermute | solution.py:41
  106.8 9.4 %collective-permute-start.24 = (bf16[32,3584]{1,0:T(8,128)(2,1)S(1)}, bf16[32,3584]{1,0:T(8,128)(2,1)S(1)}, u32[]{:S(2)}, u32[]{:S(2)}) collective-permute-start(bf16[32,3584]{1,0:T(8,128)(2,1)S(1)} %get-tuple-element.62), channel_id=1, source_target_pairs={{0,7},{3,0},{4,3},{7,4},{9,14},{10,9},{13,10},{14,13},{16,23},{19,... | collective-permute-start | bytes 688136 | tf_op jit(solution)/shard_map/ppermute | solution.py:41
  110.3 6.2 %collective-permute-start.26 = (bf16[32,3584]{1,0:T(8,128)(2,1)S(1)}, bf16[32,3584]{1,0:T(8,128)(2,1)S(1)}, u32[]{:S(2)}, u32[]{:S(2)}) collective-permute-start(bf16[32,3584]{1,0:T(8,128)(2,1)S(1)} %add_convert_fusion.2), channel_id=1, source_target_pairs={{0,7},{3,0},{4,3},{7,4},{9,14},{10,9},{13,10},{14,13},{16,23},{19,... | collective-permute-start | bytes 688136 | tf_op jit(solution)/shard_map/ppermute | solution.py:41
  113.8 6.7 %collective-permute-start.22 = (bf16[32,3584]{1,0:T(8,128)(2,1)S(1)}, bf16[32,3584]{1,0:T(8,128)(2,1)S(1)}, u32[]{:S(2)}, u32[]{:S(2)}) collective-permute-start(bf16[32,3584]{1,0:T(8,128)(2,1)S(1)} %add_convert_fusion.3), channel_id=1, source_target_pairs={{0,3},{3,4},{4,7},{7,0},{9,10},{10,13},{13,14},{14,9},{16,19},{19,... | collective-permute-start | bytes 688136 | tf_op jit(solution)/shard_map/ppermute | solution.py:41
  132.8 1.8 %collective-permute-start.27 = (bf16[2,3584]{1,0:T(2,128)(2,1)S(1)}, bf16[2,3584]{1,0:T(2,128)(2,1)S(1)}, u32[]{:S(2)}, u32[]{:S(2)}) collective-permute-start(bf16[2,3584]{1,0:T(2,128)(2,1)S(1)} %get-tuple-element.72), channel_id=1, source_target_pairs={{0,1},{1,0},{2,3},{3,2},{4,5},{5,4},{6,7},{7,6},{8,9},{9,8},{10,11... | collective-permute-start | bytes 43016 | tf_op jit(solution)/shard_map/ppermute | solution.py:37
  (7 other events, 102.8 us)
